TPU v7x, 256 devices: a whole 4x4x8 slice. The times are simulated.
256 devices in a mesh: group: 16 (over y_hi, z), vocab: 16 (over y_lo, x, core).
Axes of the slice: x: 4, y: 4 (y_hi: 2, y_lo: 2; y = y_hi * 2 + y_lo), z: 8, core: 2. Of those that a mesh axis runs over, the one named last changes fastest.
Arguments:
- teacher_codes: bfloat16 [4096, 8192], P('vocab', 'group'), may hold values from -8 to 8
- block_scales: float32 [64, 4096], P('group', 'vocab'), may hold values from 0.3 to 3
- teacher_head: bfloat16 [8192, 16384], P('group', 'vocab'), may hold values from -0.25 to 0.25
- student_hidden: bfloat16 [4096, 2048], P('group', 'vocab'), may hold values from -12 to 12
- student_head: bfloat16 [2048, 16384], P(None, 'vocab'), may hold values from -0.5 to 0.5
- token_ids: int32 [4096], P('group'), may hold values from 0 to 16383
- loss_mask: int32 [4096], P('group'), may hold values from 0 to 1, as said below
Outputs:
- grad_hidden: bfloat16 [4096, 2048], P('group', 'vocab')
- token_loss: float32 [4096], P('group')
Inputs may be any that keep to these rules, and one draw needn't show every extreme that they name: `loss_mask`: most tokens are live with a chance that rises from about 0.3 at the first token to about 0.9 at the last.
All inputs are finite; a program needn't handle non-finite values.
Results may differ from a plain program's by a relative error of at most 0.006.
Values may be sent and summed in bfloat16 or wider, within the bound.
No kernel may reach another device: no remote copies, remote signals or barrier semaphores. Data moves between devices by JAX's collectives and lax.ppermute only.
A program may use at most 128 MiB of HBM per device.

v0:
```python
import jax
import jax.numpy as jnp
from jax import lax
from jax.sharding import PartitionSpec as P

BLOCK = 128


CROSS_WEIGHT = 0.5


def dequantize(codes, scales):
    rows, cols = codes.shape
    blocks = (
        codes.astype(jnp.float32).reshape(rows, cols // BLOCK, BLOCK)
        * jnp.transpose(scales)[:, :, None]
    )
    return blocks.reshape(rows, cols).astype(jnp.bfloat16)


def body(
    teacher_codes, block_scales, teacher_head, student_hidden, student_head, token_ids, loss_mask
):
    local_rows = dequantize(teacher_codes, block_scales)
    teacher_rows = lax.all_gather(local_rows, "vocab", axis=0, tiled=True)
    own_rows = student_hidden.shape[0]
    shard_width = teacher_head.shape[1]
    teacher_logits = lax.psum_scatter(
        jnp.dot(teacher_rows, teacher_head, preferred_element_type=jnp.float32),
        "group",
        scatter_dimension=0,
        tiled=True,
    )
    student_logits = jnp.dot(
        lax.all_gather(student_hidden, "vocab", axis=1, tiled=True),
        student_head,
        preferred_element_type=jnp.float32,
    )
    columns = lax.axis_index("vocab") * shard_width + lax.broadcasted_iota(
        jnp.int32, (own_rows, shard_width), 1
    )
    chosen = token_ids[:, None] == columns
    target_part = jnp.sum(jnp.where(chosen, student_logits, 0.0), axis=1)
    top_teacher, top_student = lax.pmax(
        (jnp.max(teacher_logits, axis=1), jnp.max(student_logits, axis=1)), "vocab"
    )
    teacher_exp = jnp.exp(teacher_logits - top_teacher[:, None])
    student_exp = jnp.exp(student_logits - top_student[:, None])
    sum_teacher, sum_student, weighted, target = lax.psum(
        (
            jnp.sum(teacher_exp, axis=1),
            jnp.sum(student_exp, axis=1),
            jnp.sum(teacher_exp * (teacher_logits - student_logits), axis=1),
            target_part,
        ),
        "vocab",
    )
    divergence = (
        weighted / sum_teacher
        - top_teacher
        - jnp.log(sum_teacher)
        + top_student
        + jnp.log(sum_student)
    )
    cross_rows = top_student + jnp.log(sum_student) - target
    live_mask = loss_mask.astype(jnp.float32)
    token_loss = live_mask * (divergence + CROSS_WEIGHT * cross_rows)
    teacher_prob = teacher_exp / sum_teacher[:, None]
    student_prob = student_exp / sum_student[:, None]
    logit_grad = (
        live_mask[:, None]
        * (
            (1.0 + CROSS_WEIGHT) * student_prob
            - teacher_prob
            - CROSS_WEIGHT * chosen.astype(jnp.float32)
        )
    ).astype(jnp.bfloat16)
    hidden_terms = lax.dot_general(
        logit_grad, student_head, (((1,), (1,)), ((), ())), preferred_element_type=jnp.float32
    )
    grad_hidden = lax.psum_scatter(hidden_terms, "vocab", scatter_dimension=1, tiled=True).astype(
        jnp.bfloat16
    )
    return (grad_hidden, token_loss)


def solution(mesh):
    placed = (
        P("vocab", "group"),
        P("group", "vocab"),
        P("group", "vocab"),
        P("group", "vocab"),
        P(None, "vocab"),
        P("group"),
        P("group"),
    )
    return jax.shard_map(
        body,
        mesh=mesh,
        in_specs=placed,
        out_specs=(P("group", "vocab"), P("group")),
        check_vma=False,
    )
```

profile of v0, /device:TPU:1, one launch (start us, length us, event | category | flops | bytes accessed | tf_op | source)
XLA Modules:
  0.0 514.0 jit_solution(1379251801910061421)
XLA Ops:
  7.2 0.0 copy-start
  7.2 0.0 all-gather.5.cloned.1.call-start
  7.2 0.9 copy.9
  8.1 0.3 mul.49
  8.5 1.7 fusion.8
  10.2 0.0 all-gather.5.cloned.1.call-update
  10.2 0.0 all-gather.3.cloned.1.call-start
  10.3 0.7 all-gather.3.cloned.1.call-update
  11.0 0.0 reduce-scatter.3.cloned.1.call-start
  11.0 43.4 %all-gather.5.cloned.1.call-done = bf16[4096,512]{1,0:T(8,128)(2,1)} async-done(((bf16[256,512]{1,0:T(8,128)(2,1)}), bf16[4096,512]{1,0:T(8,128)(2,1)}) %all-gather.5.cloned.1.call-update) | async-done | bytes 4194320 | tf_op jit(solution)/shard_map/all_gather | solution.py:25
  54.4 0.0 copy-done
  54.4 10.3 %fusion.23 = f32[4096,1024]{1,0:T(8,128)} fusion(bf16[4096,512]{1,0:T(8,128)(2,1)} %all-gather.5.cloned.1.call-done, bf16[512,1024]{1,0:T(8,128)(2,1)S(1)} %copy-done), kind=kOutput, calls=%fused_computation.30 | convolution fusion | flops 4294967296 | bytes 22020096 | tf_op jit(solution)/shard_map/dot_general | solution.py:29
  64.8 0.0 copy-start.1
  64.8 0.0 reduce-scatter.3.cloned.1.call-update
  64.8 0.0 reduce-scatter.5.cloned.1.call-start
  64.9 0.6 copy-done.1
  65.5 0.0 copy-start.2
  65.5 27.4 %all-gather.3.cloned.1.call-done = bf16[256,2048]{1,0:T(8,128)(2,1)} async-done(((bf16[256,128]{1,0:T(8,128)(2,1)}), bf16[256,2048]{1,0:T(8,128)(2,1)}) %all-gather.3.cloned.1.call-update) | async-done | bytes 1048592 | tf_op jit(solution)/shard_map/all_gather | solution.py:35
  92.9 3.8 fusion.22
  96.7 285.6 %reduce-scatter.3.cloned.1.call-done = f32[256,1024]{1,0:T(8,128)} async-done(((f32[4096,1024]{1,0:T(8,128)}), f32[256,1024]{1,0:T(8,128)}) %reduce-scatter.3.cloned.1.call-update) | async-done | bytes 1048592 | tf_op jit(solution)/shard_map/reduce_scatter | solution.py:28
  382.3 1.4 reduce_max.19
  383.7 27.7 %all-reduce.1 = (f32[256]{0:T(256)S(1)}, f32[256]{0:T(256)S(1)}) all-reduce(f32[256]{0:T(256)S(1)} %reduce_max.19, f32[256]{0:T(256)S(1)} %get-tuple-element.12), channel_id=1, replica_groups=mesh['group'=16,'vocab'=16] {'vocab'}, use_global_device_ids=true, to_apply=%region_6.7 | all-reduce | flops 512 | bytes 4096 | tf_op jit(solution)/shard_map/pmax | solution.py:44
  411.4 0.0 copy-done.2
  411.4 2.0 multiply_reduce_fusion
  413.4 28.7 %all-reduce = (f32[256]{0:T(256)S(1)}, f32[256]{0:T(256)S(1)}, f32[256]{0:T(256)S(1)}, f32[256]{0:T(256)S(1)}) all-reduce(f32[256]{0:T(256)S(1)} %get-tuple-element.3, f32[256]{0:T(256)S(1)} %get-tuple-element.5, f32[256]{0:T(256)S(1)} %get-tuple-element.4, f32[256]{0:T(256)S(1)} %get-tuple-element.2), channel_id=1, replica_groups=mesh['group'=16,'vocab'=16] {'vocab'}, use_global_device_ids=true, to_apply=%region_8.9 | all-reduce | flops 1024 | bytes 8192 | tf_op jit(solution)/shard_map/psum | solution.py:49
  442.1 5.6 %fusion.6 = f32[256,2048]{1,0:T(8,128)} fusion(bf16[2048,1024]{1,0:T(8,128)(2,1)} %param.11, f32[256,1024]{1,0:T(8,128)} %reduce-scatter.3.cloned.1.call-done, f32[256,1024]{1,0:T(8,128)S(1)} %get-tuple-element.13, s32[1024]{0:T(1024)S(1)} %iota_add_fusion, f32[256]{0:T(256)S(1)} %get-tuple-element.6, f32[256]{0:T(256)S(1)} %get-tuple-element.10, ...), kind=kOutput, calls=%fused_computation.11 | convolution fusion | flops 1076625408 | bytes 8398848 | tf_op jit(solution)/shard_map/dot_general | solution.py:78
  447.7 0.0 reduce-scatter.5.cloned.1.call-update
  447.7 0.6 add_multiply_fusion
  448.3 57.6 %reduce-scatter.5.cloned.1.call-done = f32[256,128]{1,0:T(8,128)} async-done(((f32[256,2048]{1,0:T(8,128)}), f32[256,128]{1,0:T(8,128)}) %reduce-scatter.5.cloned.1.call-update) | async-done | bytes 131088 | tf_op jit(solution)/shard_map/reduce_scatter | solution.py:81
  505.9 1.5 convert_element_type.20
  (2 shorter events, 0.0 us)
Async XLA Ops:
  7.2 47.3 %copy-start = (bf16[512,1024]{1,0:T(8,128)(2,1)S(1)}, bf16[512,1024]{1,0:T(8,128)(2,1)}, u32[]{:S(2)}) copy-start(bf16[512,1024]{1,0:T(8,128)(2,1)} %param.9) | copy-start | bytes 3145732
  7.2 47.3 %all-gather.5.cloned.1.call-start = ((), (), s32[]{:S(2)}) async-start(), calls=%async_computation.3 | async-start | bytes 4456448 | tf_op jit(solution)/shard_map/all_gather | solution.py:25
  10.2 82.6 %all-gather.3.cloned.1.call-start = ((), (), s32[]{:S(2)}) async-start(), calls=%async_computation.2 | async-start | bytes 1114112 | tf_op jit(solution)/shard_map/all_gather | solution.py:35
  11.0 371.4 %reduce-scatter.3.cloned.1.call-start = ((), (), s32[]{:S(2)}) async-start(), calls=%async_computation.4 | async-start | bytes 17825792 | tf_op jit(solution)/shard_map/reduce_scatter | solution.py:28
  64.8 0.7 copy-start.1
  64.8 441.1 %reduce-scatter.5.cloned.1.call-start = ((), (), s32[]{:S(2)}) async-start(), calls=%async_computation.5 | async-start | bytes 2228224 | tf_op jit(solution)/shard_map/reduce_scatter | solution.py:81
  65.5 346.0 %copy-start.2 = (s32[256]{0:T(256)S(1)}, s32[256]{0:T(256)}, u32[]{:S(2)}) copy-start(s32[256]{0:T(256)} %param.12) | copy-start | bytes 3076
Sparse Core Ops, SparseCore 0:
  10.3 44.0 all-gather.4
  56.2 36.5 all-gather.2
  97.0 285.3 reduce-scatter.2
  447.9 57.9 reduce-scatter.4
where the time goes:
time: 516 us; the launch traced here: 514 us
  waiting for transfers between devices  415 us (80%)
  blocking collectives  56.4 us (11%)
  matrix products  19.8 us (4%)
  between operations  13.8 us (3%)
  other arithmetic  7.19 us (1%)
    reduce_scatter x1, waiting for transfers between devices, body(): lax.psum_scatter(jnp.dot(teacher_rows, teacher_head, preferred_element_ty...  286 us
    reduce_scatter x1, waiting for transfers between devices, body(): lax.psum_scatter(hidden_terms, 'vocab', scatter_dimension=1, tiled=True)  57.6 us
    all_gather x1, waiting for transfers between devices, body(): teacher_rows = lax.all_gather(local_rows, 'vocab', axis=0, tiled=True)  43.4 us
    psum x1, blocking collectives, body(): lax.psum((jnp.sum(teacher_exp, axis=1), jnp.sum(student_exp, axis=1), jnp...  28.7 us
    pmax x1, blocking collectives, body(): lax.pmax((jnp.max(teacher_logits, axis=1), jnp.max(student_logits, axis=1...  27.7 us
    all_gather x1, waiting for transfers between devices, body(): lax.all_gather(student_hidden, 'vocab', axis=1, tiled=True)  27.4 us
    dot_general x1, matrix products, body(): jnp.dot(teacher_rows, teacher_head, preferred_element_type=jnp.float32)  10.3 us
  transfers between devices with their start and end apart: 4, of which 4 were waited for; matrix products, arithmetic and copies ran while one was open for 3% of the time, Pallas kernels for 0%

commit v1 on v0

v1 whole, which is shorter than its diff:
```python
import jax
import jax.numpy as jnp
from jax import lax
from jax.experimental import pallas as pl
from jax.experimental.pallas import tpu as pltpu
from jax.sharding import Mesh
from jax.sharding import PartitionSpec as P

BLOCK = 128
CROSS_WEIGHT = 0.5
GROUP = ("yh", "z")
VOCAB = ("yl", "x", "c")
NZ = 8
CHUNKS = 4


def dequantize(codes, scales):
    rows, cols = codes.shape
    blocks = (
        codes.astype(jnp.float32).reshape(rows, cols // BLOCK, BLOCK)
        * jnp.transpose(scales)[:, :, None]
    )
    return blocks.reshape(rows, cols).astype(jnp.bfloat16)


def shift(x, s):
    return lax.ppermute(x, "z", [(i, (i + s) % NZ) for i in range(NZ)])


def after(x, gate):
    return lax.optimization_barrier((x, gate))[0]


def swap_rows_features():
    pairs = []
    for z in range(NZ):
        for x in range(4):
            for c in range(2):
                pairs.append(((z * 4 + x) * 2 + c, ((2 * x + c) * 4 + z // 2) * 2 + z % 2))
    return pairs


def chunk_kernel(where, rows, *refs):
    heads, (away, keep) = refs[:NZ], refs[NZ:]
    for side, out in ((0, away), (1, keep)):
        total = None
        for s in range(NZ):
            part = jnp.dot(rows[where[side, s]], heads[s][...], preferred_element_type=jnp.float32)
            total = part if total is None else total + part
        out[...] = total


def chunk_logits(where, rows, heads):
    tokens, width = rows.shape[1], heads[0].shape[1]
    out = jax.ShapeDtypeStruct((tokens, width), jnp.float32)
    vmem = pl.BlockSpec(memory_space=pltpu.VMEM)
    return pl.pallas_call(
        chunk_kernel,
        out_shape=(out, out),
        in_specs=[pl.BlockSpec(memory_space=pltpu.SMEM)] + [vmem] * (1 + NZ),
        out_specs=(vmem, vmem),
        compiler_params=pltpu.CompilerParams(vmem_limit_bytes=24 * 2**20),
        cost_estimate=pl.CostEstimate(
            flops=4 * tokens * width * NZ * rows.shape[2],
            bytes_accessed=rows.size * 2 + NZ * heads[0].size * 2 + 8 * tokens * width,
            transcendentals=0,
        ),
    )(where, rows, *heads)


def ring_chunks(head):
    width = head.shape[1] // CHUNKS
    results, gate = [], None
    for k in range(CHUNKS):
        own = head[:, k * width : (k + 1) * width]
        plus, minus = [own], [own]
        next_gate = None
        for s in range(1, 5):
            if s == 2 and gate is not None:
                plus[-1] = after(plus[-1], gate[0])
                minus[-1] = after(minus[-1], gate[1])
            if s < 4 or k % 2 == 0:
                plus.append(shift(plus[-1], 1))
            if s < 4 or k % 2 == 1:
                minus.append(shift(minus[-1], -1))
            if s == 2:
                next_gate = (plus[-1], minus[-1])
        gate = next_gate
        last = plus[4] if k % 2 == 0 else minus[4]
        results.append([own, plus[1], minus[1], plus[2], minus[2], plus[3], minus[3], last])
    return results


ORDER = (0, -1, 1, -2, 2, -3, 3, 4)


def body(
    teacher_codes, block_scales, teacher_head, student_hidden, student_head, token_ids, loss_mask
):
    yh, z = lax.axis_index("yh"), lax.axis_index("z")
    local_rows = dequantize(teacher_codes, block_scales)
    moved = lax.ppermute(local_rows, ("z", "x", "c"), swap_rows_features())
    rows = lax.all_gather(moved, VOCAB, axis=0, tiled=False)

    own_rows, features = student_hidden.shape
    hidden = lax.all_to_all(
        jnp.broadcast_to(student_hidden[None], (16,) + student_hidden.shape),
        VOCAB,
        split_axis=0,
        concat_axis=0,
        tiled=True,
    )
    hidden = jnp.transpose(hidden, (1, 0, 2)).reshape(own_rows, 16 * features)
    student_logits = jnp.dot(hidden, student_head, preferred_element_type=jnp.float32)
    shard_width = student_head.shape[1]
    columns = lax.axis_index(VOCAB) * shard_width + lax.broadcasted_iota(
        jnp.int32, (own_rows, shard_width), 1
    )
    chosen = token_ids[:, None] == columns
    target_part = jnp.sum(jnp.where(chosen, student_logits, 0.0), axis=1)

    slabs = lax.rem(z + jnp.array(ORDER, jnp.int32) + NZ, NZ)
    where = jnp.stack([(1 - yh) * NZ + slabs, yh * NZ + slabs])
    parts = []
    for heads in ring_chunks(teacher_head):
        away, keep = chunk_logits(where, rows, heads)
        parts.append(keep + lax.ppermute(away, "yh", [(0, 1), (1, 0)]))
    teacher_logits = jnp.concatenate(parts, axis=1)

    near_teacher = jnp.max(teacher_logits, axis=1)
    near_student = jnp.max(student_logits, axis=1)
    teacher_exp = jnp.exp(teacher_logits - near_teacher[:, None])
    student_exp = jnp.exp(student_logits - near_student[:, None])
    stats = jnp.stack(
        [
            near_teacher,
            jnp.sum(teacher_exp, axis=1),
            jnp.sum(teacher_exp * (teacher_logits - student_logits), axis=1),
            near_student,
            jnp.sum(student_exp, axis=1),
            target_part,
            jnp.zeros_like(target_part),
            jnp.zeros_like(target_part),
        ]
    )
    stats = lax.all_to_all(
        jnp.broadcast_to(stats[None], (16,) + stats.shape),
        VOCAB,
        split_axis=0,
        concat_axis=0,
        tiled=True,
    )
    top_teacher = jnp.max(stats[:, 0], axis=0)
    top_student = jnp.max(stats[:, 3], axis=0)
    scale_teacher = jnp.exp(stats[:, 0] - top_teacher[None])
    scale_student = jnp.exp(stats[:, 3] - top_student[None])
    sum_teacher = jnp.sum(stats[:, 1] * scale_teacher, axis=0)
    weighted = jnp.sum(stats[:, 2] * scale_teacher, axis=0)
    sum_student = jnp.sum(stats[:, 4] * scale_student, axis=0)
    target = jnp.sum(stats[:, 5], axis=0)

    divergence = (
        weighted / sum_teacher
        - top_teacher
        - jnp.log(sum_teacher)
        + top_student
        + jnp.log(sum_student)
    )
    cross_rows = top_student + jnp.log(sum_student) - target
    live_mask = loss_mask.astype(jnp.float32)
    token_loss = live_mask * (divergence + CROSS_WEIGHT * cross_rows)
    teacher_prob = jnp.exp(teacher_logits - top_teacher[:, None]) / sum_teacher[:, None]
    student_prob = jnp.exp(student_logits - top_student[:, None]) / sum_student[:, None]
    logit_grad = (
        live_mask[:, None]
        * (
            (1.0 + CROSS_WEIGHT) * student_prob
            - teacher_prob
            - CROSS_WEIGHT * chosen.astype(jnp.float32)
        )
    ).astype(jnp.bfloat16)
    hidden_terms = lax.dot_general(
        logit_grad, student_head, (((1,), (1,)), ((), ())), preferred_element_type=jnp.float32
    ).astype(jnp.bfloat16)
    hidden_terms = jnp.transpose(hidden_terms.reshape(own_rows, 16, features), (1, 0, 2))
    hidden_terms = lax.all_to_all(hidden_terms, VOCAB, split_axis=0, concat_axis=0, tiled=True)
    grad_hidden = jnp.sum(hidden_terms.astype(jnp.float32), axis=0).astype(jnp.bfloat16)
    return (grad_hidden, token_loss)


def solution(mesh):
    fine = Mesh(mesh.devices.reshape(2, NZ, 2, 4, 2), GROUP + VOCAB)
    placed = (
        P(VOCAB, GROUP),
        P(GROUP, VOCAB),
        P(GROUP, VOCAB),
        P(GROUP, VOCAB),
        P(None, VOCAB),
        P(GROUP),
        P(GROUP),
    )
    return jax.shard_map(
        body,
        mesh=fine,
        in_specs=placed,
        out_specs=(P(GROUP, VOCAB), P(GROUP)),
        check_vma=False,
    )
```

time: 516 us -> 208 us (0.40)
  waiting for transfers between devices: 415 us -> 75.2 us
  starting transfers between devices: 0.16 us -> 84.2 us
  blocking collectives: 56.4 us -> 0 us
  matrix products: 19.8 us -> 9.03 us
  Pallas kernels: 0 us -> 9.77 us
  local copies, waits for them, and re-layouts: 1.84 us -> 11.1 us
    reduce_scatter x2 -> x0, waiting for transfers between devices: 343 us -> none  [the longest x1 286 us: body(): lax.psum_scatter(jnp.dot(teacher_rows, teacher_head, preferred_element_ty...]
    all_gather x2 -> x1, waiting for transfers between devices: 70.8 us -> 0.01 us  [body(): rows = lax.all_gather(moved, VOCAB, axis=0, tiled=False)]
    ppermute x0 -> x33, starting transfers between devices: none -> 56 us  [the longest x28 44.4 us: shift(): return lax.ppermute(x, 'z', [(i, (i + s) % NZ) for i in range(NZ)])]
    ppermute x0 -> x33, waiting for transfers between devices: none -> 53.8 us  [the longest x28 39.8 us: shift(): return lax.ppermute(x, 'z', [(i, (i + s) % NZ) for i in range(NZ)])]
    psum x1 -> x0, blocking collectives: 28.7 us -> none  [body(): lax.psum((jnp.sum(teacher_exp, axis=1), jnp.sum(student_exp, axis=1), jnp...]
    all_to_all x0 -> x3, starting transfers between devices: none -> 28.2 us  [the longest x1 15.4 us: body(): lax.all_to_all(jnp.broadcast_to(student_hidden[None], (16,) + student_hid...]
    pmax x1 -> x0, blocking collectives: 27.7 us -> none  [body(): lax.pmax((jnp.max(teacher_logits, axis=1), jnp.max(student_logits, axis=1...]
    all_to_all x0 -> x3, waiting for transfers between devices: none -> 21.4 us  [the longest x1 15.4 us: body(): lax.all_to_all(hidden_terms, VOCAB, split_axis=0, concat_axis=0, tiled=True)]
  transfers between devices with their start and end apart: 4 -> 37, of which waited for: 4 -> 14; matrix products, arithmetic and copies ran while one was open for 3% -> 4% of each run, Pallas kernels for 0% -> 5%
where the time goes in v1:
time: 208 us; the launch traced here: 207 us
  starting transfers between devices  84.2 us (40%)
  waiting for transfers between devices  75.2 us (36%)
  between operations  14.3 us (7%)
  local copies, waits for them, and re-layouts  11.1 us (5%)
  Pallas kernels  9.77 us (5%)
  matrix products  9.03 us (4%)
  other arithmetic  3.71 us (2%)
    ppermute x28, starting transfers between devices, shift(): return lax.ppermute(x, 'z', [(i, (i + s) % NZ) for i in range(NZ)])  44.4 us
    ppermute x28, waiting for transfers between devices, shift(): return lax.ppermute(x, 'z', [(i, (i + s) % NZ) for i in range(NZ)])  39.8 us
    all_to_all x1, starting transfers between devices, body(): lax.all_to_all(jnp.broadcast_to(student_hidden[None], (16,) + student_hid...  15.4 us
    all_to_all x1, waiting for transfers between devices, body(): lax.all_to_all(hidden_terms, VOCAB, split_axis=0, concat_axis=0, tiled=True)  15.4 us
    pallas_call x4, Pallas kernels, chunk_logits(): pl.pallas_call(chunk_kernel, out_shape=(out, out), in_specs=[pl.BlockSpec...  9.77 us
    ppermute x4, waiting for transfers between devices, body(): parts.append(keep + lax.ppermute(away, 'yh', [(0, 1), (1, 0)]))  9.55 us
    all_to_all x1, starting transfers between devices, body(): lax.all_to_all(jnp.broadcast_to(stats[None], (16,) + stats.shape), VOCAB,...  8.87 us
    ppermute x4, starting transfers between devices, body(): parts.append(keep + lax.ppermute(away, 'yh', [(0, 1), (1, 0)]))  6.59 us
  transfers between devices with their start and end apart: 37, of which 14 were waited for; matrix products, arithmetic and copies ran while one was open for 4% of the time, Pallas kernels for 5%

profile of v1, /device:TPU:1, one launch (start us, length us, event | category | flops | bytes accessed | tf_op | source)
XLA Modules:
  0.0 207.4 jit_solution(17730180430858570922)
XLA Ops:
  9.4 4.9 %collective-permute-start = (bf16[256,512]{1,0:T(8,128)(2,1)S(1)}, bf16[256,512]{1,0:T(8,128)(2,1)S(1)}, u32[]{:S(2)}, u32[]{:S(2)}) collective-permute-start(bf16[256,512]{1,0:T(8,128)(2,1)S(1)} %fusion.7), channel_id=1, source_target_pairs={{0,0},{1,16},{2,32},{3,48},{4,64},{5,80},{6,96},{7,112},{16,1},{17... | collective-permute-start | bytes 786440 | tf_op jit(solution)/shard_map/ppermute | solution.py:102
  14.4 4.4 %collective-permute-done = bf16[256,512]{1,0:T(8,128)(2,1)S(1)} collective-permute-done((bf16[256,512]{1,0:T(8,128)(2,1)S(1)}, bf16[256,512]{1,0:T(8,128)(2,1)S(1)}, u32[]{:S(2)}, u32[]{:S(2)}) %collective-permute-start) | collective-permute-done | bytes 262176 | tf_op jit(solution)/shard_map/ppermute | solution.py:102
  20.8 16.8 %collective-permute-start.2 = (bf16[512,256]{1,0:T(8,128)(2,1)S(1)}, bf16[512,256]{1,0:T(8,128)(2,1)S(1)}, u32[]{:S(2)}, u32[]{:S(2)}) collective-permute-start(bf16[512,256]{1,0:T(8,128)(2,1)S(1)} %get-tuple-element.51.refs_0_), channel_id=1, source_target_pairs={{0,112},{16,0},{32,16},{48,32},{64,48},{80,64},{96,80},{112,96},{1... | collective-permute-start | bytes 786440 | tf_op jit(solution)/shard_map/ppermute | solution.py:27
  37.7 2.7 %collective-permute-start.10 = (bf16[512,256]{1,0:T(8,128)(2,1)S(1)}, bf16[512,256]{1,0:T(8,128)(2,1)S(1)}, u32[]{:S(2)}, u32[]{:S(2)}) collective-permute-start(bf16[512,256]{1,0:T(8,128)(2,1)S(1)} %get-tuple-element.52.refs_0_), channel_id=1, source_target_pairs={{0,112},{16,0},{32,16},{48,32},{64,48},{80,64},{96,80},{112,96},{1... | collective-permute-start | bytes 786440 | tf_op jit(solution)/shard_map/ppermute | solution.py:27
  41.0 3.1 %collective-permute-start.4 = (bf16[512,256]{1,0:T(8,128)(2,1)S(1)}, bf16[512,256]{1,0:T(8,128)(2,1)S(1)}, u32[]{:S(2)}, u32[]{:S(2)}) collective-permute-start(bf16[512,256]{1,0:T(8,128)(2,1)S(1)} %collective-permute-done.2.refs_2_), channel_id=1, source_target_pairs={{0,112},{16,0},{32,16},{48,32},{64,48},{80,64},{96,80},{112,96},{1... | collective-permute-start | bytes 786440 | tf_op jit(solution)/shard_map/ppermute | solution.py:27
  47.1 3.1 %collective-permute-done.4.refs_4_ = bf16[512,256]{1,0:T(8,128)(2,1)S(1)} collective-permute-done((bf16[512,256]{1,0:T(8,128)(2,1)S(1)}, bf16[512,256]{1,0:T(8,128)(2,1)S(1)}, u32[]{:S(2)}, u32[]{:S(2)}) %collective-permute-start.4) | collective-permute-done | bytes 262176 | tf_op jit(solution)/shard_map/ppermute | solution.py:27
  50.1 3.4 %collective-permute-start.12 = (bf16[512,256]{1,0:T(8,128)(2,1)S(1)}, bf16[512,256]{1,0:T(8,128)(2,1)S(1)}, u32[]{:S(2)}, u32[]{:S(2)}) collective-permute-start(bf16[512,256]{1,0:T(8,128)(2,1)S(1)} %collective-permute-done.10.refs_2_), channel_id=1, source_target_pairs={{0,112},{16,0},{32,16},{48,32},{64,48},{80,64},{96,80},{112,96},{1... | collective-permute-start | bytes 786440 | tf_op jit(solution)/shard_map/ppermute | solution.py:27
  54.7 15.4 %all-to-all-start = ((bf16[16,256,128]{1,2,0:T(8,128)(2,1)}), bf16[16,256,128]{1,2,0:T(8,128)(2,1)}, u32[]{:S(2)}, u32[]{:S(2)}) async-start(bf16[16,256,128]{1,2,0:T(8,128)(2,1)} %broadcast_in_dim.8), calls=%async_computation | async-start | bytes 2097152 | tf_op jit(solution)/shard_map/all_to_all | solution.py:106
  70.3 2.7 %collective-permute-start.26 = (bf16[512,256]{1,0:T(8,128)(2,1)S(1)}, bf16[512,256]{1,0:T(8,128)(2,1)S(1)}, u32[]{:S(2)}, u32[]{:S(2)}) collective-permute-start(bf16[512,256]{1,0:T(8,128)(2,1)S(1)} %get-tuple-element.53.refs_0_), channel_id=1, source_target_pairs={{0,112},{16,0},{32,16},{48,32},{64,48},{80,64},{96,80},{112,96},{1... | collective-permute-start | bytes 786440 | tf_op jit(solution)/shard_map/ppermute | solution.py:27
  74.5 4.5 %collective-permute-done.17.refs_1_ = bf16[512,256]{1,0:T(8,128)(2,1)} collective-permute-done((bf16[512,256]{1,0:T(8,128)(2,1)S(1)}, bf16[512,256]{1,0:T(8,128)(2,1)}, u32[]{:S(2)}, u32[]{:S(2)}) %collective-permute-start.17) | collective-permute-done | bytes 262176 | tf_op jit(solution)/shard_map/ppermute | solution.py:27
  79.0 5.6 %collective-permute-done.11.refs_3_ = bf16[512,256]{1,0:T(8,128)(2,1)S(1)} collective-permute-done((bf16[512,256]{1,0:T(8,128)(2,1)S(1)}, bf16[512,256]{1,0:T(8,128)(2,1)S(1)}, u32[]{:S(2)}, u32[]{:S(2)}) %collective-permute-start.11) | collective-permute-done | bytes 262176 | tf_op jit(solution)/shard_map/ppermute | solution.py:27
  85.7 2.6 %collective-permute-start.28 = (bf16[512,256]{1,0:T(8,128)(2,1)S(1)}, bf16[512,256]{1,0:T(8,128)(2,1)}, u32[]{:S(2)}, u32[]{:S(2)}) collective-permute-start(bf16[512,256]{1,0:T(8,128)(2,1)S(1)} %collective-permute-done.26.refs_2_), channel_id=1, source_target_pairs={{0,112},{16,0},{32,16},{48,32},{64,48},{80,64},{96,80},{112,96},{1... | collective-permute-start | bytes 786440 | tf_op jit(solution)/shard_map/ppermute | solution.py:27
  90.2 5.6 %collective-permute-done.19.refs_3_ = bf16[512,256]{1,0:T(8,128)(2,1)} collective-permute-done((bf16[512,256]{1,0:T(8,128)(2,1)}, bf16[512,256]{1,0:T(8,128)(2,1)}, u32[]{:S(2)}, u32[]{:S(2)}) %collective-permute-start.19) | collective-permute-done | bytes 262176 | tf_op jit(solution)/shard_map/ppermute | solution.py:27
  95.9 5.5 %collective-permute-done.5.refs_5_ = bf16[512,256]{1,0:T(8,128)(2,1)S(1)} collective-permute-done((bf16[512,256]{1,0:T(8,128)(2,1)S(1)}, bf16[512,256]{1,0:T(8,128)(2,1)S(1)}, u32[]{:S(2)}, u32[]{:S(2)}) %collective-permute-start.5) | collective-permute-done | bytes 262176 | tf_op jit(solution)/shard_map/ppermute | solution.py:27
  101.4 2.7 %collective-permute-start.30 = (bf16[512,256]{1,0:T(8,128)(2,1)}, bf16[512,256]{1,0:T(8,128)(2,1)}, u32[]{:S(2)}, u32[]{:S(2)}) collective-permute-start(bf16[512,256]{1,0:T(8,128)(2,1)} %collective-permute-done.28.refs_4_), channel_id=1, source_target_pairs={{0,112},{16,0},{32,16},{48,32},{64,48},{80,64},{96,80},{112,96},{1... | collective-permute-start | bytes 786440 | tf_op jit(solution)/shard_map/ppermute | solution.py:27
  104.2 2.9 %collective-permute-done.13.refs_5_ = bf16[512,256]{1,0:T(8,128)(2,1)} collective-permute-done((bf16[512,256]{1,0:T(8,128)(2,1)}, bf16[512,256]{1,0:T(8,128)(2,1)}, u32[]{:S(2)}, u32[]{:S(2)}) %collective-permute-start.13) | collective-permute-done | bytes 262176 | tf_op jit(solution)/shard_map/ppermute | solution.py:27
  107.1 11.2 %collective-permute-done.21.refs_5_ = bf16[512,256]{1,0:T(8,128)(2,1)} collective-permute-done((bf16[512,256]{1,0:T(8,128)(2,1)}, bf16[512,256]{1,0:T(8,128)(2,1)}, u32[]{:S(2)}, u32[]{:S(2)}) %collective-permute-start.21) | collective-permute-done | bytes 262176 | tf_op jit(solution)/shard_map/ppermute | solution.py:27
  118.4 2.7 %collective-permute-start.31 = (bf16[512,256]{1,0:T(8,128)(2,1)}, bf16[512,256]{1,0:T(8,128)(2,1)}, u32[]{:S(2)}, u32[]{:S(2)}) collective-permute-start(bf16[512,256]{1,0:T(8,128)(2,1)} %collective-permute-done.30.refs_6_), channel_id=1, source_target_pairs={{0,112},{16,0},{32,16},{48,32},{64,48},{80,64},{96,80},{112,96},{1... | collective-permute-start | bytes 786440 | tf_op jit(solution)/shard_map/ppermute | solution.py:27
  121.1 4.8 %fusion.38 = (f32[256]{0:T(256)S(1)}, f32[256,1024]{1,0:T(8,128)}) fusion(bf16[256,2048]{0,1:T(8,128)(2,1)} %bitcast.1, bf16[2048,1024]{1,0:T(8,128)(2,1)} %param.12), kind=kOutput, calls=%fused_computation.61 | convolution fusion | flops 1074003712 | bytes 6292480 | tf_op jit(solution)/shard_map/dot_general | solution.py:114
  131.4 2.4 %shard_map.96 = (f32[256,256]{1,0:T(8,128)S(1)}, f32[256,256]{1,0:T(8,128)S(1)}) custom-call(s32[2,8]{1,0:T(2,128)S(1)} %pad_add_fusion.where, bf16[16,256,512]{2,1,0:T(8,128)(2,1)S(1)} %bitcast.63, bf16[512,256]{1,0:T(8,128)(2,1)S(1)} %get-tuple-element.52.refs_0_, bf16[512,256]{1,0:T(8,128)(2,1)S(1)} %collective-permute-done.9.refs_1_, ...), custom_call_target="tpu_custom_call" | custom-call | flops 1073741824 | bytes 6815744 | tf_op jit(solution)/shard_map/pallas_call | solution.py:57
  133.9 3.2 %collective-permute-start.16 = (f32[256,256]{1,0:T(8,128)S(1)}, f32[256,256]{1,0:T(8,128)S(1)}, u32[]{:S(2)}, u32[]{:S(2)}) collective-permute-start(f32[256,256]{1,0:T(8,128)S(1)} %get-tuple-element.21), channel_id=1, source_target_pairs={{0,128},{128,0},{1,129},{129,1},{2,130},{130,2},{3,131},{131,3},{4... | collective-permute-start | bytes 786440 | tf_op jit(solution)/shard_map/ppermute | solution.py:127
  137.1 2.5 %shard_map.97 = (f32[256,256]{1,0:T(8,128)S(1)}, f32[256,256]{1,0:T(8,128)S(1)}) custom-call(s32[2,8]{1,0:T(2,128)S(1)} %pad_add_fusion.where, bf16[16,256,512]{2,1,0:T(8,128)(2,1)S(1)} %bitcast.64, bf16[512,256]{1,0:T(8,128)(2,1)S(1)} %get-tuple-element.54.refs_0_, bf16[512,256]{1,0:T(8,128)(2,1)} %collective-permute-done.17.refs_1_, ...), custom_call_target="tpu_custom_call" | custom-call | flops 1073741824 | bytes 6815744 | tf_op jit(solution)/shard_map/pallas_call | solution.py:57
  139.8 2.6 %shard_map.98 = (f32[256,256]{1,0:T(8,128)S(1)}, f32[256,256]{1,0:T(8,128)S(1)}) custom-call(s32[2,8]{1,0:T(2,128)S(1)} %pad_add_fusion.where, bf16[16,256,512]{2,1,0:T(8,128)(2,1)S(1)} %bitcast.65, bf16[512,256]{1,0:T(8,128)(2,1)S(1)} %get-tuple-element.53.refs_0_, bf16[512,256]{1,0:T(8,128)(2,1)} %collective-permute-done.25.refs_1_, ...), custom_call_target="tpu_custom_call" | custom-call | flops 1073741824 | bytes 6815744 | tf_op jit(solution)/shard_map/pallas_call | solution.py:57
  142.4 3.0 %collective-permute-start.32 = (f32[256,256]{1,0:T(8,128)S(1)}, f32[256,256]{1,0:T(8,128)S(1)}, u32[]{:S(2)}, u32[]{:S(2)}) collective-permute-start(f32[256,256]{1,0:T(8,128)S(1)} %get-tuple-element.29), channel_id=1, source_target_pairs={{0,128},{128,0},{1,129},{129,1},{2,130},{130,2},{3,131},{131,3},{4... | collective-permute-start | bytes 786440 | tf_op jit(solution)/shard_map/ppermute | solution.py:127
  145.4 2.3 %shard_map.95 = (f32[256,256]{1,0:T(8,128)S(1)}, f32[256,256]{1,0:T(8,128)S(1)}) custom-call(s32[2,8]{1,0:T(2,128)S(1)} %pad_add_fusion.where, bf16[16,256,512]{2,1,0:T(8,128)(2,1)S(1)} %bitcast.66, bf16[512,256]{1,0:T(8,128)(2,1)S(1)} %get-tuple-element.51.refs_0_, bf16[512,256]{1,0:T(8,128)(2,1)S(1)} %collective-permute-done.1.refs_1_, ...), custom_call_target="tpu_custom_call" | custom-call | flops 1073741824 | bytes 6815744 | tf_op jit(solution)/shard_map/pallas_call | solution.py:57
  148.1 4.0 %collective-permute-done.32 = f32[256,256]{1,0:T(8,128)S(1)} collective-permute-done((f32[256,256]{1,0:T(8,128)S(1)}, f32[256,256]{1,0:T(8,128)S(1)}, u32[]{:S(2)}, u32[]{:S(2)}) %collective-permute-start.32) | collective-permute-done | bytes 262176 | tf_op jit(solution)/shard_map/ppermute | solution.py:127
  152.3 5.5 %collective-permute-done.8 = f32[256,256]{1,0:T(8,128)S(1)} collective-permute-done((f32[256,256]{1,0:T(8,128)S(1)}, f32[256,256]{1,0:T(8,128)S(1)}, u32[]{:S(2)}, u32[]{:S(2)}) %collective-permute-start.8) | collective-permute-done | bytes 262176 | tf_op jit(solution)/shard_map/ppermute | solution.py:127
  159.3 8.9 %all-to-all-start.1 = ((f32[16,8,256]{2,1,0:T(8,128)}), f32[16,8,256]{2,1,0:T(8,128)S(1)}, u32[]{:S(2)}, u32[]{:S(2)}) async-start(f32[16,8,256]{2,1,0:T(8,128)} %broadcast_in_dim.10), calls=%async_computation.1 | async-start | bytes 262144 | tf_op jit(solution)/shard_map/all_to_all | solution.py:146
  168.2 6.1 %all-to-all-done.1 = f32[16,8,256]{2,1,0:T(8,128)S(1)} async-done(((f32[16,8,256]{2,1,0:T(8,128)}), f32[16,8,256]{2,1,0:T(8,128)S(1)}, u32[]{:S(2)}, u32[]{:S(2)}) %all-to-all-start.1) | async-done | bytes 131104 | tf_op jit(solution)/shard_map/all_to_all | solution.py:146
  174.4 4.3 %fusion = bf16[32,16,8,128]{3,2,1,0:T(8,128)(2,1)S(1)} fusion(bf16[2048,1024]{1,0:T(8,128)(2,1)} %param.12, f32[256,1024]{1,0:T(8,128)} %get-tuple-element.64, f32[256]{0:T(256)S(1)} %get-tuple-element.40, f32[256]{0:T(256)S(1)} %get-tuple-element.59, f32[256]{0:T(256)S(1)} %get-tuple-element.65, f32[256]{0:T(256)S(1)} %get-tuple-element.60, ...), kind=kOutput, calls=%fused_computation.1 | convolution fusion | flops 1077936128 | bytes 7350272 | tf_op jit(solution)/shard_map/dot_general | solution.py:182
  180.0 3.9 %all-to-all-start.2 = ((bf16[16,256,128]{2,1,0:T(8,128)(2,1)}), bf16[16,256,128]{2,1,0:T(8,128)(2,1)S(1)}, u32[]{:S(2)}, u32[]{:S(2)}) async-start(bf16[16,256,128]{2,1,0:T(8,128)(2,1)} %bitcast.62), calls=%async_computation.2 | async-start | bytes 2097152 | tf_op jit(solution)/shard_map/all_to_all | solution.py:186
  184.4 15.4 %all-to-all-done.2 = bf16[16,256,128]{2,1,0:T(8,128)(2,1)S(1)} async-done(((bf16[16,256,128]{2,1,0:T(8,128)(2,1)}), bf16[16,256,128]{2,1,0:T(8,128)(2,1)S(1)}, u32[]{:S(2)}, u32[]{:S(2)}) %all-to-all-start.2) | async-done | bytes 1048608 | tf_op jit(solution)/shard_map/all_to_all | solution.py:186
  (100 shorter events, 24.3 us)
Async XLA Ops:
  7.2 120.2 %all-gather.3.cloned.1.call-start = ((), (), s32[]{:S(2)}) async-start(), calls=%async_computation.3 | async-start | bytes 4456448 | tf_op jit(solution)/shard_map/all_gather | solution.py:103
  20.8 20.1 %collective-permute-start.2 = (bf16[512,256]{1,0:T(8,128)(2,1)S(1)}, bf16[512,256]{1,0:T(8,128)(2,1)S(1)}, u32[]{:S(2)}, u32[]{:S(2)}) collective-permute-start(bf16[512,256]{1,0:T(8,128)(2,1)S(1)} %get-tuple-element.51.refs_0_), channel_id=1, source_target_pairs={{0,112},{16,0},{32,16},{48,32},{64,48},{80,64},{96,80},{112,96},{1... | collective-permute-start | bytes 786440 | tf_op jit(solution)/shard_map/ppermute | solution.py:27
  37.7 9.4 %collective-permute-start.10 = (bf16[512,256]{1,0:T(8,128)(2,1)S(1)}, bf16[512,256]{1,0:T(8,128)(2,1)S(1)}, u32[]{:S(2)}, u32[]{:S(2)}) collective-permute-start(bf16[512,256]{1,0:T(8,128)(2,1)S(1)} %get-tuple-element.52.refs_0_), channel_id=1, source_target_pairs={{0,112},{16,0},{32,16},{48,32},{64,48},{80,64},{96,80},{112,96},{1... | collective-permute-start | bytes 786440 | tf_op jit(solution)/shard_map/ppermute | solution.py:27
  44.1 26.1 %collective-permute-start.9 = (bf16[512,256]{1,0:T(8,128)(2,1)S(1)}, bf16[512,256]{1,0:T(8,128)(2,1)S(1)}, u32[]{:S(2)}, u32[]{:S(2)}) collective-permute-start(bf16[512,256]{1,0:T(8,128)(2,1)S(1)} %get-tuple-element.52.refs_0_), channel_id=1, source_target_pairs={{0,16},{16,32},{32,48},{48,64},{64,80},{80,96},{96,112},{112,0},{1... | collective-permute-start | bytes 786440 | tf_op jit(solution)/shard_map/ppermute | solution.py:27
  44.4 25.8 %collective-permute-start.3 = (bf16[512,256]{1,0:T(8,128)(2,1)S(1)}, bf16[512,256]{1,0:T(8,128)(2,1)S(1)}, u32[]{:S(2)}, u32[]{:S(2)}) collective-permute-start(bf16[512,256]{1,0:T(8,128)(2,1)S(1)} %collective-permute-done.1.refs_1_), channel_id=1, source_target_pairs={{0,16},{16,32},{32,48},{48,64},{64,80},{80,96},{96,112},{112,0},{1... | collective-permute-start | bytes 786440 | tf_op jit(solution)/shard_map/ppermute | solution.py:27
  46.3 26.6 %collective-permute-start.18 = (bf16[512,256]{1,0:T(8,128)(2,1)S(1)}, bf16[512,256]{1,0:T(8,128)(2,1)S(1)}, u32[]{:S(2)}, u32[]{:S(2)}) collective-permute-start(bf16[512,256]{1,0:T(8,128)(2,1)S(1)} %get-tuple-element.54.refs_0_), channel_id=1, source_target_pairs={{0,112},{16,0},{32,16},{48,32},{64,48},{80,64},{96,80},{112,96},{1... | collective-permute-start | bytes 786440 | tf_op jit(solution)/shard_map/ppermute | solution.py:27
  50.1 22.8 %collective-permute-start.12 = (bf16[512,256]{1,0:T(8,128)(2,1)S(1)}, bf16[512,256]{1,0:T(8,128)(2,1)S(1)}, u32[]{:S(2)}, u32[]{:S(2)}) collective-permute-start(bf16[512,256]{1,0:T(8,128)(2,1)S(1)} %collective-permute-done.10.refs_2_), channel_id=1, source_target_pairs={{0,112},{16,0},{32,16},{48,32},{64,48},{80,64},{96,80},{112,96},{1... | collective-permute-start | bytes 786440 | tf_op jit(solution)/shard_map/ppermute | solution.py:27
  54.7 66.4 %all-to-all-start = ((bf16[16,256,128]{1,2,0:T(8,128)(2,1)}), bf16[16,256,128]{1,2,0:T(8,128)(2,1)}, u32[]{:S(2)}, u32[]{:S(2)}) async-start(bf16[16,256,128]{1,2,0:T(8,128)(2,1)} %broadcast_in_dim.8), calls=%async_computation | async-start | bytes 2097152 | tf_op jit(solution)/shard_map/all_to_all | solution.py:106
  70.2 14.4 %collective-permute-start.11 = (bf16[512,256]{1,0:T(8,128)(2,1)S(1)}, bf16[512,256]{1,0:T(8,128)(2,1)S(1)}, u32[]{:S(2)}, u32[]{:S(2)}) collective-permute-start(bf16[512,256]{1,0:T(8,128)(2,1)S(1)} %collective-permute-done.9.refs_1_), channel_id=1, source_target_pairs={{0,16},{16,32},{32,48},{48,64},{64,80},{80,96},{96,112},{112,0},{1... | collective-permute-start | bytes 786440 | tf_op jit(solution)/shard_map/ppermute | solution.py:27
  70.3 14.6 %collective-permute-start.26 = (bf16[512,256]{1,0:T(8,128)(2,1)S(1)}, bf16[512,256]{1,0:T(8,128)(2,1)S(1)}, u32[]{:S(2)}, u32[]{:S(2)}) collective-permute-start(bf16[512,256]{1,0:T(8,128)(2,1)S(1)} %get-tuple-element.53.refs_0_), channel_id=1, source_target_pairs={{0,112},{16,0},{32,16},{48,32},{64,48},{80,64},{96,80},{112,96},{1... | collective-permute-start | bytes 786440 | tf_op jit(solution)/shard_map/ppermute | solution.py:27
  73.0 12.0 %collective-permute-start.20 = (bf16[512,256]{1,0:T(8,128)(2,1)S(1)}, bf16[512,256]{1,0:T(8,128)(2,1)S(1)}, u32[]{:S(2)}, u32[]{:S(2)}) collective-permute-start(bf16[512,256]{1,0:T(8,128)(2,1)S(1)} %collective-permute-done.18.refs_2_), channel_id=1, source_target_pairs={{0,112},{16,0},{32,16},{48,32},{64,48},{80,64},{96,80},{112,96},{1... | collective-permute-start | bytes 786440 | tf_op jit(solution)/shard_map/ppermute | solution.py:27
  74.4 15.8 %collective-permute-start.25 = (bf16[512,256]{1,0:T(8,128)(2,1)S(1)}, bf16[512,256]{1,0:T(8,128)(2,1)}, u32[]{:S(2)}, u32[]{:S(2)}) collective-permute-start(bf16[512,256]{1,0:T(8,128)(2,1)S(1)} %get-tuple-element.53.refs_0_), channel_id=1, source_target_pairs={{0,16},{16,32},{32,48},{48,64},{64,80},{80,96},{96,112},{112,0},{1... | collective-permute-start | bytes 786440 | tf_op jit(solution)/shard_map/ppermute | solution.py:27
  84.6 11.2 %collective-permute-start.19 = (bf16[512,256]{1,0:T(8,128)(2,1)}, bf16[512,256]{1,0:T(8,128)(2,1)}, u32[]{:S(2)}, u32[]{:S(2)}) collective-permute-start(bf16[512,256]{1,0:T(8,128)(2,1)} %collective-permute-done.17.refs_1_), channel_id=1, source_target_pairs={{0,16},{16,32},{32,48},{48,64},{64,80},{80,96},{96,112},{112,0},{1... | collective-permute-start | bytes 786440 | tf_op jit(solution)/shard_map/ppermute | solution.py:27
  84.6 16.7 %collective-permute-start.5 = (bf16[512,256]{1,0:T(8,128)(2,1)S(1)}, bf16[512,256]{1,0:T(8,128)(2,1)S(1)}, u32[]{:S(2)}, u32[]{:S(2)}) collective-permute-start(bf16[512,256]{1,0:T(8,128)(2,1)S(1)} %collective-permute-done.3.refs_3_), channel_id=1, source_target_pairs={{0,16},{16,32},{32,48},{48,64},{64,80},{80,96},{96,112},{112,0},{1... | collective-permute-start | bytes 786440 | tf_op jit(solution)/shard_map/ppermute | solution.py:27
  85.7 15.7 %collective-permute-start.28 = (bf16[512,256]{1,0:T(8,128)(2,1)S(1)}, bf16[512,256]{1,0:T(8,128)(2,1)}, u32[]{:S(2)}, u32[]{:S(2)}) collective-permute-start(bf16[512,256]{1,0:T(8,128)(2,1)S(1)} %collective-permute-done.26.refs_2_), channel_id=1, source_target_pairs={{0,112},{16,0},{32,16},{48,32},{64,48},{80,64},{96,80},{112,96},{1... | collective-permute-start | bytes 786440 | tf_op jit(solution)/shard_map/ppermute | solution.py:27
  88.3 15.8 %collective-permute-start.14 = (bf16[512,256]{1,0:T(8,128)(2,1)}, bf16[512,256]{1,0:T(8,128)(2,1)}, u32[]{:S(2)}, u32[]{:S(2)}) collective-permute-start(bf16[512,256]{1,0:T(8,128)(2,1)} %copy-done.1), channel_id=1, source_target_pairs={{0,112},{16,0},{32,16},{48,32},{64,48},{80,64},{96,80},{112,96},{1... | collective-permute-start | bytes 786440 | tf_op jit(solution)/shard_map/ppermute | solution.py:27
  90.2 16.9 %collective-permute-start.13 = (bf16[512,256]{1,0:T(8,128)(2,1)}, bf16[512,256]{1,0:T(8,128)(2,1)}, u32[]{:S(2)}, u32[]{:S(2)}) collective-permute-start(bf16[512,256]{1,0:T(8,128)(2,1)} %copy-done.5), channel_id=1, source_target_pairs={{0,16},{16,32},{32,48},{48,64},{64,80},{80,96},{96,112},{112,0},{1... | collective-permute-start | bytes 786440 | tf_op jit(solution)/shard_map/ppermute | solution.py:27
  95.9 22.5 %collective-permute-start.27 = (bf16[512,256]{1,0:T(8,128)(2,1)}, bf16[512,256]{1,0:T(8,128)(2,1)}, u32[]{:S(2)}, u32[]{:S(2)}) collective-permute-start(bf16[512,256]{1,0:T(8,128)(2,1)} %collective-permute-done.25.refs_1_), channel_id=1, source_target_pairs={{0,16},{16,32},{32,48},{48,64},{64,80},{80,96},{96,112},{112,0},{1... | collective-permute-start | bytes 786440 | tf_op jit(solution)/shard_map/ppermute | solution.py:27
  101.4 17.0 %collective-permute-start.21 = (bf16[512,256]{1,0:T(8,128)(2,1)}, bf16[512,256]{1,0:T(8,128)(2,1)}, u32[]{:S(2)}, u32[]{:S(2)}) collective-permute-start(bf16[512,256]{1,0:T(8,128)(2,1)} %collective-permute-done.19.refs_3_), channel_id=1, source_target_pairs={{0,16},{16,32},{32,48},{48,64},{64,80},{80,96},{96,112},{112,0},{1... | collective-permute-start | bytes 786440 | tf_op jit(solution)/shard_map/ppermute | solution.py:27
  101.4 17.0 %collective-permute-start.30 = (bf16[512,256]{1,0:T(8,128)(2,1)}, bf16[512,256]{1,0:T(8,128)(2,1)}, u32[]{:S(2)}, u32[]{:S(2)}) collective-permute-start(bf16[512,256]{1,0:T(8,128)(2,1)} %collective-permute-done.28.refs_4_), channel_id=1, source_target_pairs={{0,112},{16,0},{32,16},{48,32},{64,48},{80,64},{96,80},{112,96},{1... | collective-permute-start | bytes 786440 | tf_op jit(solution)/shard_map/ppermute | solution.py:27
  104.1 23.2 %collective-permute-start.22 = (bf16[512,256]{1,0:T(8,128)(2,1)}, bf16[512,256]{1,0:T(8,128)(2,1)}, u32[]{:S(2)}, u32[]{:S(2)}) collective-permute-start(bf16[512,256]{1,0:T(8,128)(2,1)} %copy-done.3), channel_id=1, source_target_pairs={{0,112},{16,0},{32,16},{48,32},{64,48},{80,64},{96,80},{112,96},{1... | collective-permute-start | bytes 786440 | tf_op jit(solution)/shard_map/ppermute | solution.py:27
  107.1 18.8 %collective-permute-start.15 = (bf16[512,256]{1,0:T(8,128)(2,1)}, bf16[512,256]{1,0:T(8,128)(2,1)}, u32[]{:S(2)}, u32[]{:S(2)}) collective-permute-start(bf16[512,256]{1,0:T(8,128)(2,1)} %collective-permute-done.14.refs_6_), channel_id=1, source_target_pairs={{0,112},{16,0},{32,16},{48,32},{64,48},{80,64},{96,80},{112,96},{1... | collective-permute-start | bytes 786440 | tf_op jit(solution)/shard_map/ppermute | solution.py:27
  118.3 15.5 %collective-permute-start.23 = (bf16[512,256]{1,0:T(8,128)(2,1)}, bf16[512,256]{1,0:T(8,128)(2,1)}, u32[]{:S(2)}, u32[]{:S(2)}) collective-permute-start(bf16[512,256]{1,0:T(8,128)(2,1)} %collective-permute-done.21.refs_5_), channel_id=1, source_target_pairs={{0,16},{16,32},{32,48},{48,64},{64,80},{80,96},{96,112},{112,0},{1... | collective-permute-start | bytes 786440 | tf_op jit(solution)/shard_map/ppermute | solution.py:27
  118.3 21.3 %collective-permute-start.29 = (bf16[512,256]{1,0:T(8,128)(2,1)}, bf16[512,256]{1,0:T(8,128)(2,1)}, u32[]{:S(2)}, u32[]{:S(2)}) collective-permute-start(bf16[512,256]{1,0:T(8,128)(2,1)} %collective-permute-done.27.refs_3_), channel_id=1, source_target_pairs={{0,16},{16,32},{32,48},{48,64},{64,80},{80,96},{96,112},{112,0},{1... | collective-permute-start | bytes 786440 | tf_op jit(solution)/shard_map/ppermute | solution.py:27
  118.4 21.4 %collective-permute-start.31 = (bf16[512,256]{1,0:T(8,128)(2,1)}, bf16[512,256]{1,0:T(8,128)(2,1)}, u32[]{:S(2)}, u32[]{:S(2)}) collective-permute-start(bf16[512,256]{1,0:T(8,128)(2,1)} %collective-permute-done.30.refs_6_), channel_id=1, source_target_pairs={{0,112},{16,0},{32,16},{48,32},{64,48},{80,64},{96,80},{112,96},{1... | collective-permute-start | bytes 786440 | tf_op jit(solution)/shard_map/ppermute | solution.py:27
  125.9 19.5 %collective-permute-start.6 = (bf16[512,256]{1,0:T(8,128)(2,1)S(1)}, bf16[512,256]{1,0:T(8,128)(2,1)}, u32[]{:S(2)}, u32[]{:S(2)}) collective-permute-start(bf16[512,256]{1,0:T(8,128)(2,1)S(1)} %collective-permute-done.4.refs_4_), channel_id=1, source_target_pairs={{0,112},{16,0},{32,16},{48,32},{64,48},{80,64},{96,80},{112,96},{1... | collective-permute-start | bytes 786440 | tf_op jit(solution)/shard_map/ppermute | solution.py:27
  127.3 18.1 %collective-permute-start.7 = (bf16[512,256]{1,0:T(8,128)(2,1)S(1)}, bf16[512,256]{1,0:T(8,128)(2,1)}, u32[]{:S(2)}, u32[]{:S(2)}) collective-permute-start(bf16[512,256]{1,0:T(8,128)(2,1)S(1)} %collective-permute-done.5.refs_5_), channel_id=1, source_target_pairs={{0,16},{16,32},{32,48},{48,64},{64,80},{80,96},{96,112},{112,0},{1... | collective-permute-start | bytes 786440 | tf_op jit(solution)/shard_map/ppermute | solution.py:27
  133.9 14.0 %collective-permute-start.16 = (f32[256,256]{1,0:T(8,128)S(1)}, f32[256,256]{1,0:T(8,128)S(1)}, u32[]{:S(2)}, u32[]{:S(2)}) collective-permute-start(f32[256,256]{1,0:T(8,128)S(1)} %get-tuple-element.21), channel_id=1, source_target_pairs={{0,128},{128,0},{1,129},{129,1},{2,130},{130,2},{3,131},{131,3},{4... | collective-permute-start | bytes 786440 | tf_op jit(solution)/shard_map/ppermute | solution.py:127
  142.4 9.8 %collective-permute-start.32 = (f32[256,256]{1,0:T(8,128)S(1)}, f32[256,256]{1,0:T(8,128)S(1)}, u32[]{:S(2)}, u32[]{:S(2)}) collective-permute-start(f32[256,256]{1,0:T(8,128)S(1)} %get-tuple-element.29), channel_id=1, source_target_pairs={{0,128},{128,0},{1,129},{129,1},{2,130},{130,2},{3,131},{131,3},{4... | collective-permute-start | bytes 786440 | tf_op jit(solution)/shard_map/ppermute | solution.py:127
  147.7 10.1 %collective-permute-start.8 = (f32[256,256]{1,0:T(8,128)S(1)}, f32[256,256]{1,0:T(8,128)S(1)}, u32[]{:S(2)}, u32[]{:S(2)}) collective-permute-start(f32[256,256]{1,0:T(8,128)S(1)} %get-tuple-element.17), channel_id=1, source_target_pairs={{0,128},{128,0},{1,129},{129,1},{2,130},{130,2},{3,131},{131,3},{4... | collective-permute-start | bytes 786440 | tf_op jit(solution)/shard_map/ppermute | solution.py:127
  159.3 15.0 %all-to-all-start.1 = ((f32[16,8,256]{2,1,0:T(8,128)}), f32[16,8,256]{2,1,0:T(8,128)S(1)}, u32[]{:S(2)}, u32[]{:S(2)}) async-start(f32[16,8,256]{2,1,0:T(8,128)} %broadcast_in_dim.10), calls=%async_computation.1 | async-start | bytes 262144 | tf_op jit(solution)/shard_map/all_to_all | solution.py:146
  180.0 19.9 %all-to-all-start.2 = ((bf16[16,256,128]{2,1,0:T(8,128)(2,1)}), bf16[16,256,128]{2,1,0:T(8,128)(2,1)S(1)}, u32[]{:S(2)}, u32[]{:S(2)}) async-start(bf16[16,256,128]{2,1,0:T(8,128)(2,1)} %bitcast.62), calls=%async_computation.2 | async-start | bytes 2097152 | tf_op jit(solution)/shard_map/all_to_all | solution.py:186
  (18 other events, 248.3 us)
Sparse Core Ops, SparseCore 0:
  19.7 62.6 all-gather.2

commit v2 on v1

--- a/solution.py
+++ b/solution.py
@@ -1,3 +1,5 @@
+import functools
+
 import jax
 import jax.numpy as jnp
 from jax import lax
@@ -11,7 +13,10 @@
 GROUP = ("yh", "z")
 VOCAB = ("yl", "x", "c")
 NZ = 8
-CHUNKS = 4
+OFFSETS = (0, 4, 1, -3, -1, 3, 2, -2)
+WIDTHS = (512, 512)
+LAST = (+1, -1)
+FIRST = ((0, 1, +1), (0, 1, -1), (1, 1, +1), (1, 1, -1))
 
 
 def dequantize(codes, scales):
@@ -27,91 +32,137 @@
     return lax.ppermute(x, "z", [(i, (i + s) % NZ) for i in range(NZ)])
 
 
-def after(x, gate):
-    return lax.optimization_barrier((x, gate))[0]
-
-
-def swap_rows_features():
-    pairs = []
-    for z in range(NZ):
-        for x in range(4):
-            for c in range(2):
-                pairs.append(((z * 4 + x) * 2 + c, ((2 * x + c) * 4 + z // 2) * 2 + z % 2))
-    return pairs
-
-
-def chunk_kernel(where, rows, *refs):
-    heads, (away, keep) = refs[:NZ], refs[NZ:]
-    for side, out in ((0, away), (1, keep)):
-        total = None
-        for s in range(NZ):
-            part = jnp.dot(rows[where[side, s]], heads[s][...], preferred_element_type=jnp.float32)
-            total = part if total is None else total + part
-        out[...] = total
-
-
-def chunk_logits(where, rows, heads):
+def order(later, earlier):
+    return lax.optimization_barrier((later, earlier))
+
+
+def swap_rows_features(rows):
+    beside, along = [], []
+    for slab in range(NZ):
+        for place in range(NZ):
+            slot = OFFSETS.index((slab - place + 3) % NZ - 3)
+            beside.append((slab * NZ + place, slab * NZ + slot))
+            along.append((slab * NZ + slot, place * NZ + slot))
+    rows = lax.ppermute(rows, ("z", "x", "c"), beside)
+    return lax.ppermute(rows, ("z", "x", "c"), along)
+
+
+def chunk_kernel(places, held, where, rows, *refs):
+    heads, refs = refs[: len(places)], refs[len(places) :]
+    sums, (away, keep, rows_in, heads_in, sems) = refs[:held], refs[held:]
+    copies = []
+    for i, ((slot, start), head) in enumerate(zip(places, heads)):
+        depth = head.shape[0]
+        span = pl.ds(0, depth)
+        mine = [pltpu.make_async_copy(head, heads_in.at[i, span], sems.at[i, 2])]
+        for side in (0, 1):
+            block = rows.at[where[side] * NZ + slot, :, pl.ds(start, depth)]
+            mine.append(pltpu.make_async_copy(block, rows_in.at[i, side, :, span], sems.at[i, side]))
+        for copy in mine:
+            copy.start()
+        copies.append(mine)
+    totals = [s[...] for s in sums] or [None, None]
+    for i, mine in enumerate(copies):
+        depth = heads[i].shape[0]
+        for copy in mine:
+            copy.wait()
+        for side in (0, 1):
+            part = jnp.dot(
+                rows_in[i, side, :, :depth],
+                heads_in[i, :depth],
+                preferred_element_type=jnp.float32,
+            )
+            totals[side] = part if totals[side] is None else totals[side] + part
+    away[...], keep[...] = totals
+
+
+def chunk_logits(where, rows, blocks, sums=()):
+    places, heads = zip(*blocks)
     tokens, width = rows.shape[1], heads[0].shape[1]
+    depth, size = max(h.shape[0] for h in heads), sum(h.size for h in heads)
     out = jax.ShapeDtypeStruct((tokens, width), jnp.float32)
-    vmem = pl.BlockSpec(memory_space=pltpu.VMEM)
+    vmem, loose = pl.BlockSpec(memory_space=pltpu.VMEM), pl.BlockSpec(memory_space=pl.ANY)
     return pl.pallas_call(
-        chunk_kernel,
+        functools.partial(chunk_kernel, places, len(sums)),
         out_shape=(out, out),
-        in_specs=[pl.BlockSpec(memory_space=pltpu.SMEM)] + [vmem] * (1 + NZ),
+        in_specs=[pl.BlockSpec(memory_space=pltpu.SMEM)]
+        + [loose] * (1 + len(heads))
+        + [vmem] * len(sums),
         out_specs=(vmem, vmem),
-        compiler_params=pltpu.CompilerParams(vmem_limit_bytes=24 * 2**20),
+        scratch_shapes=[
+            pltpu.VMEM((len(heads), 2, tokens, depth), jnp.bfloat16),
+            pltpu.VMEM((len(heads), depth, width), jnp.bfloat16),
+            pltpu.SemaphoreType.DMA((len(heads), 3)),
+        ],
+        compiler_params=pltpu.CompilerParams(vmem_limit_bytes=28 * 2**20),
         cost_estimate=pl.CostEstimate(
-            flops=4 * tokens * width * NZ * rows.shape[2],
-            bytes_accessed=rows.size * 2 + NZ * heads[0].size * 2 + 8 * tokens * width,
+            flops=4 * tokens * size,
+            bytes_accessed=rows.size * 2 + size * 2 + 8 * tokens * width,
             transcendentals=0,
         ),
-    )(where, rows, *heads)
-
-
-def ring_chunks(head):
-    width = head.shape[1] // CHUNKS
-    results, gate = [], None
-    for k in range(CHUNKS):
-        own = head[:, k * width : (k + 1) * width]
-        plus, minus = [own], [own]
-        next_gate = None
-        for s in range(1, 5):
-            if s == 2 and gate is not None:
-                plus[-1] = after(plus[-1], gate[0])
-                minus[-1] = after(minus[-1], gate[1])
-            if s < 4 or k % 2 == 0:
-                plus.append(shift(plus[-1], 1))
-            if s < 4 or k % 2 == 1:
-                minus.append(shift(minus[-1], -1))
-            if s == 2:
-                next_gate = (plus[-1], minus[-1])
-        gate = next_gate
-        last = plus[4] if k % 2 == 0 else minus[4]
-        results.append([own, plus[1], minus[1], plus[2], minus[2], plus[3], minus[3], last])
-    return results
-
-
-ORDER = (0, -1, 1, -2, 2, -3, 3, 4)
+    )(where, rows, *heads, *sums)
+
+
+class Ring:
+    def __init__(self, own):
+        self.block = {(k, 0, way): x for k, x in enumerate(own) for way in (+1, -1)}
+
+    def send(self, k, s):
+        for way in (+1, -1):
+            if s < 4 or way == LAST[k]:
+                self.block[k, s, way] = shift(self.block[k, s - 1, way], way)
+
+    def hold(self, later, keys):
+        later, blocks = order(later, [self.block[key] for key in keys])
+        self.block.update(zip(keys, blocks))
+        return later
+
+    def blocks(self, k, steps):
+        found = []
+        for s in steps:
+            for way in (+1, -1) if s else (+1,):
+                if s < 4 or way == LAST[k]:
+                    slot = OFFSETS.index(-way * s if s < 4 else 4)
+                    found.append(((slot, 0), self.block[k, s, way]))
+        return found
+
+
+def swap_halves(x):
+    return lax.ppermute(x, "yh", [(0, 1), (1, 0)])
 
 
 def body(
     teacher_codes, block_scales, teacher_head, student_hidden, student_head, token_ids, loss_mask
 ):
-    yh, z = lax.axis_index("yh"), lax.axis_index("z")
+    yh = lax.axis_index("yh")
+    starts = [sum(WIDTHS[:k]) for k in range(len(WIDTHS))]
     local_rows = dequantize(teacher_codes, block_scales)
-    moved = lax.ppermute(local_rows, ("z", "x", "c"), swap_rows_features())
+    head, local_rows = order(teacher_head, local_rows)
+    own = [head[:, a : a + w] for a, w in zip(starts, WIDTHS)]
+    own_rows, features = student_hidden.shape
+    ring = Ring(own)
+    moved = swap_rows_features(local_rows)
+    for k in (0, 1):
+        ring.send(k, 1)
+    moved = ring.hold(moved, FIRST)
+    moved = jnp.concatenate([moved, student_hidden], axis=1)
     rows = lax.all_gather(moved, VOCAB, axis=0, tiled=False)
-
-    own_rows, features = student_hidden.shape
-    hidden = lax.all_to_all(
-        jnp.broadcast_to(student_hidden[None], (16,) + student_hidden.shape),
-        VOCAB,
-        split_axis=0,
-        concat_axis=0,
-        tiled=True,
-    )
-    hidden = jnp.transpose(hidden, (1, 0, 2)).reshape(own_rows, 16 * features)
+    for s in (2, 3):
+        for k in (0, 1):
+            ring.send(k, s)
+
+    where = jnp.stack([1 - yh, yh]).astype(jnp.int32)
+    where = ring.hold(where, [(0, 3, -1), (0, 3, +1)])
+    for k in (0, 1):
+        ring.send(k, 4)
+    sums = [chunk_logits(where, rows, ring.blocks(k, range(3))) for k in (0, 1)]
+    products = [chunk_logits(where, rows, ring.blocks(k, (3, 4)), sums[k]) for k in (0, 1)]
+    hidden, products[1] = order(rows, products[1])
+    hidden = jnp.transpose(hidden[:, :, teacher_codes.shape[1] :], (1, 0, 2))
+    hidden = hidden.reshape(own_rows, 16 * features)
     student_logits = jnp.dot(hidden, student_head, preferred_element_type=jnp.float32)
+    parts = [keep + swap_halves(away) for away, keep in products]
+
     shard_width = student_head.shape[1]
     columns = lax.axis_index(VOCAB) * shard_width + lax.broadcasted_iota(
         jnp.int32, (own_rows, shard_width), 1
@@ -119,12 +170,6 @@
     chosen = token_ids[:, None] == columns
     target_part = jnp.sum(jnp.where(chosen, student_logits, 0.0), axis=1)
 
-    slabs = lax.rem(z + jnp.array(ORDER, jnp.int32) + NZ, NZ)
-    where = jnp.stack([(1 - yh) * NZ + slabs, yh * NZ + slabs])
-    parts = []
-    for heads in ring_chunks(teacher_head):
-        away, keep = chunk_logits(where, rows, heads)
-        parts.append(keep + lax.ppermute(away, "yh", [(0, 1), (1, 0)]))
     teacher_logits = jnp.concatenate(parts, axis=1)
 
     near_teacher = jnp.max(teacher_logits, axis=1)

time: 208 us -> 184 us (0.88)
  starting transfers between devices: 84.2 us -> 52.3 us
  waiting for transfers between devices: 75.2 us -> 81.3 us
  other arithmetic: 3.71 us -> 7.68 us
  local copies, waits for them, and re-layouts: 11.1 us -> 8.38 us
    ppermute x28 -> x14, starting transfers between devices: 44.4 us -> 26 us  [shift(): return lax.ppermute(x, 'z', [(i, (i + s) % NZ) for i in range(NZ)])]
    all_to_all x1 -> x0, starting transfers between devices: 15.4 us -> none  [body(): lax.all_to_all(jnp.broadcast_to(student_hidden[None], (16,) + student_hid...]
    ppermute x28 -> x14, waiting for transfers between devices: 39.8 us -> 45.4 us  [shift(): return lax.ppermute(x, 'z', [(i, (i + s) % NZ) for i in range(NZ)])]
    ppermute x5 -> x4, starting transfers between devices: 11.5 us -> 15.6 us  [the longest x1 6.04 us: swap_rows_features(): rows = lax.ppermute(rows, ('z', 'x', 'c'), beside)]
    unnamed x27 -> x8, local copies, waits for them, and re-layouts: 5.7 us -> 2.5 us
    reduce_max x5 -> x3, other arithmetic: 0.46 us -> 2.73 us  [body(): near_teacher = jnp.max(teacher_logits, axis=1)]
    all_to_all x1, starting transfers between devices: 8.87 us -> 6.77 us  [body(): lax.all_to_all(jnp.broadcast_to(stats[None], (16,) + stats.shape), VOCAB,...]
    ppermute x5 -> x4, waiting for transfers between devices: 14 us -> 14.4 us  [the longest x2 6.31 us: swap_halves(): return lax.ppermute(x, 'yh', [(0, 1), (1, 0)])]
  transfers between devices with their start and end apart: 37 -> 21, of which waited for: 14 -> 14; matrix products, arithmetic and copies ran while one was open for 4% -> 4% of each run, Pallas kernels for 5% -> 6%
where the time goes in v2:
time: 184 us; the launch traced here: 183 us
  waiting for transfers between devices  81.3 us (44%)
  starting transfers between devices  52.3 us (28%)
  between operations  14.2 us (8%)
  Pallas kernels  11 us (6%)
  local copies, waits for them, and re-layouts  8.38 us (5%)
  matrix products  8.14 us (4%)
  other arithmetic  7.68 us (4%)
    ppermute x14, waiting for transfers between devices, shift(): return lax.ppermute(x, 'z', [(i, (i + s) % NZ) for i in range(NZ)])  45.4 us
    ppermute x14, starting transfers between devices, shift(): return lax.ppermute(x, 'z', [(i, (i + s) % NZ) for i in range(NZ)])  26 us
    all_to_all x1, waiting for transfers between devices, body(): lax.all_to_all(hidden_terms, VOCAB, split_axis=0, concat_axis=0, tiled=True)  15.4 us
    pallas_call x4, Pallas kernels, chunk_logits(): pl.pallas_call(functools.partial(chunk_kernel, places, len(sums)), out_sh...  11 us
    all_to_all x1, starting transfers between devices, body(): lax.all_to_all(jnp.broadcast_to(stats[None], (16,) + stats.shape), VOCAB,...  6.77 us
    ppermute x2, waiting for transfers between devices, swap_halves(): return lax.ppermute(x, 'yh', [(0, 1), (1, 0)])  6.31 us
    all_to_all x1, waiting for transfers between devices, body(): lax.all_to_all(jnp.broadcast_to(stats[None], (16,) + stats.shape), VOCAB,...  6.07 us
    ppermute x1, starting transfers between devices, swap_rows_features(): rows = lax.ppermute(rows, ('z', 'x', 'c'), beside)  6.04 us
  transfers between devices with their start and end apart: 21, of which 14 were waited for; matrix products, arithmetic and copies ran while one was open for 4% of the time, Pallas kernels for 6%

profile of v2, /device:TPU:1, one launch (start us, length us, event | category | flops | bytes accessed | tf_op | source)
XLA Modules:
  0.0 183.0 jit_solution(12436580094372692686)
XLA Ops:
  10.7 2.5 %collective-permute-start.2 = (bf16[512,512]{1,0:T(8,128)(2,1)S(1)}, bf16[512,512]{1,0:T(8,128)(2,1)S(1)}, u32[]{:S(2)}, u32[]{:S(2)}) collective-permute-start(bf16[512,512]{1,0:T(8,128)(2,1)S(1)} %get-tuple-element.60.refs_0_), channel_id=1, source_target_pairs={{0,16},{16,32},{32,48},{48,64},{64,80},{80,96},{96,112},{112,0},{1... | collective-permute-start | bytes 1572872 | tf_op jit(solution)/shard_map/ppermute | solution.py:32
  13.2 4.0 %collective-permute-start.3 = (bf16[512,512]{1,0:T(8,128)(2,1)S(1)}, bf16[512,512]{1,0:T(8,128)(2,1)S(1)}, u32[]{:S(2)}, u32[]{:S(2)}) collective-permute-start(bf16[512,512]{1,0:T(8,128)(2,1)S(1)} %get-tuple-element.60.refs_0_), channel_id=1, source_target_pairs={{0,112},{16,0},{32,16},{48,32},{64,48},{80,64},{96,80},{112,96},{1... | collective-permute-start | bytes 1572872 | tf_op jit(solution)/shard_map/ppermute | solution.py:32
  17.3 2.7 %collective-permute-start.5 = (bf16[512,512]{1,0:T(8,128)(2,1)S(1)}, bf16[512,512]{1,0:T(8,128)(2,1)S(1)}, u32[]{:S(2)}, u32[]{:S(2)}) collective-permute-start(bf16[512,512]{1,0:T(8,128)(2,1)S(1)} %get-tuple-element.59.refs_0_), channel_id=1, source_target_pairs={{0,112},{16,0},{32,16},{48,32},{64,48},{80,64},{96,80},{112,96},{1... | collective-permute-start | bytes 1572872 | tf_op jit(solution)/shard_map/ppermute | solution.py:32
  19.9 6.0 %collective-permute-start = (bf16[256,512]{1,0:T(8,128)(2,1)S(1)}, bf16[256,512]{1,0:T(8,128)(2,1)S(1)}, u32[]{:S(2)}, u32[]{:S(2)}) collective-permute-start(bf16[256,512]{1,0:T(8,128)(2,1)S(1)} %fusion.7), channel_id=1, source_target_pairs={{0,0},{1,4},{2,7},{3,3},{4,1},{5,5},{6,6},{7,2},{16,18},{17,16},{1... | collective-permute-start | bytes 786440 | tf_op jit(solution)/shard_map/ppermute | solution.py:46
  26.0 4.0 %collective-permute-done = bf16[256,512]{1,0:T(8,128)(2,1)S(1)} collective-permute-done((bf16[256,512]{1,0:T(8,128)(2,1)S(1)}, bf16[256,512]{1,0:T(8,128)(2,1)S(1)}, u32[]{:S(2)}, u32[]{:S(2)}) %collective-permute-start) | collective-permute-done | bytes 262176 | tf_op jit(solution)/shard_map/ppermute | solution.py:46
  30.0 3.7 %collective-permute-start.1 = (bf16[256,512]{1,0:T(8,128)(2,1)S(1)}, bf16[256,512]{1,0:T(8,128)(2,1)S(1)}, u32[]{:S(2)}, u32[]{:S(2)}) collective-permute-start(bf16[256,512]{1,0:T(8,128)(2,1)S(1)} %collective-permute-done), channel_id=1, source_target_pairs={{0,0},{4,20},{7,39},{3,51},{1,65},{5,85},{6,102},{2,114},{18,2},{1... | collective-permute-start | bytes 786440 | tf_op jit(solution)/shard_map/ppermute | solution.py:47
  33.7 6.3 %collective-permute-done.4.refs_1_ = bf16[512,512]{1,0:T(8,128)(2,1)S(1)} collective-permute-done((bf16[512,512]{1,0:T(8,128)(2,1)S(1)}, bf16[512,512]{1,0:T(8,128)(2,1)S(1)}, u32[]{:S(2)}, u32[]{:S(2)}) %collective-permute-start.4) | collective-permute-done | bytes 524320 | tf_op jit(solution)/shard_map/ppermute | solution.py:32
  40.0 2.5 %collective-permute-done.5.refs_2_ = bf16[512,512]{1,0:T(8,128)(2,1)S(1)} collective-permute-done((bf16[512,512]{1,0:T(8,128)(2,1)S(1)}, bf16[512,512]{1,0:T(8,128)(2,1)S(1)}, u32[]{:S(2)}, u32[]{:S(2)}) %collective-permute-start.5) | collective-permute-done | bytes 524320 | tf_op jit(solution)/shard_map/ppermute | solution.py:32
  42.6 4.1 %collective-permute-done.1 = bf16[256,512]{1,0:T(8,128)(2,1)S(1)} collective-permute-done((bf16[256,512]{1,0:T(8,128)(2,1)S(1)}, bf16[256,512]{1,0:T(8,128)(2,1)S(1)}, u32[]{:S(2)}, u32[]{:S(2)}) %collective-permute-start.1) | collective-permute-done | bytes 262176 | tf_op jit(solution)/shard_map/ppermute | solution.py:47
  48.3 3.6 %collective-permute-start.6 = (bf16[512,512]{1,0:T(8,128)(2,1)S(1)}, bf16[512,512]{1,0:T(8,128)(2,1)}, u32[]{:S(2)}, u32[]{:S(2)}) collective-permute-start(bf16[512,512]{1,0:T(8,128)(2,1)S(1)} %collective-permute-done.3.refs_2_), channel_id=1, source_target_pairs={{0,112},{16,0},{32,16},{48,32},{64,48},{80,64},{96,80},{112,96},{1... | collective-permute-start | bytes 1572872 | tf_op jit(solution)/shard_map/ppermute | solution.py:32
  51.9 2.7 %collective-permute-start.12 = (bf16[512,512]{1,0:T(8,128)(2,1)S(1)}, bf16[512,512]{1,0:T(8,128)(2,1)}, u32[]{:S(2)}, u32[]{:S(2)}) collective-permute-start(bf16[512,512]{1,0:T(8,128)(2,1)S(1)} %collective-permute-done.5.refs_2_), channel_id=1, source_target_pairs={{0,112},{16,0},{32,16},{48,32},{64,48},{80,64},{96,80},{112,96},{1... | collective-permute-start | bytes 1572872 | tf_op jit(solution)/shard_map/ppermute | solution.py:32
  54.6 9.1 %collective-permute-done.6.refs_4_ = bf16[512,512]{1,0:T(8,128)(2,1)} collective-permute-done((bf16[512,512]{1,0:T(8,128)(2,1)S(1)}, bf16[512,512]{1,0:T(8,128)(2,1)}, u32[]{:S(2)}, u32[]{:S(2)}) %collective-permute-start.6) | collective-permute-done | bytes 524320 | tf_op jit(solution)/shard_map/ppermute | solution.py:32
  63.7 3.5 %collective-permute-start.7 = (bf16[512,512]{1,0:T(8,128)(2,1)}, bf16[512,512]{1,0:T(8,128)(2,1)}, u32[]{:S(2)}, u32[]{:S(2)}) collective-permute-start(bf16[512,512]{1,0:T(8,128)(2,1)} %collective-permute-done.6.refs_4_), channel_id=1, source_target_pairs={{0,112},{16,0},{32,16},{48,32},{64,48},{80,64},{96,80},{112,96},{1... | collective-permute-start | bytes 1572872 | tf_op jit(solution)/shard_map/ppermute | solution.py:32
  67.2 7.7 %collective-permute-done.12.refs_4_ = bf16[512,512]{1,0:T(8,128)(2,1)} collective-permute-done((bf16[512,512]{1,0:T(8,128)(2,1)S(1)}, bf16[512,512]{1,0:T(8,128)(2,1)}, u32[]{:S(2)}, u32[]{:S(2)}) %collective-permute-start.12) | collective-permute-done | bytes 524320 | tf_op jit(solution)/shard_map/ppermute | solution.py:32
  74.9 3.5 %collective-permute-start.13 = (bf16[512,512]{1,0:T(8,128)(2,1)}, bf16[512,512]{1,0:T(8,128)(2,1)}, u32[]{:S(2)}, u32[]{:S(2)}) collective-permute-start(bf16[512,512]{1,0:T(8,128)(2,1)} %collective-permute-done.12.refs_4_), channel_id=1, source_target_pairs={{0,112},{16,0},{32,16},{48,32},{64,48},{80,64},{96,80},{112,96},{1... | collective-permute-start | bytes 1572872 | tf_op jit(solution)/shard_map/ppermute | solution.py:32
  78.5 7.7 %collective-permute-done.7.refs_1_ = bf16[512,512]{1,0:T(8,128)(2,1)} collective-permute-done((bf16[512,512]{1,0:T(8,128)(2,1)}, bf16[512,512]{1,0:T(8,128)(2,1)}, u32[]{:S(2)}, u32[]{:S(2)}) %collective-permute-start.7) | collective-permute-done | bytes 524320 | tf_op jit(solution)/shard_map/ppermute | solution.py:32
  86.6 7.3 %collective-permute-done.10.refs_3_ = bf16[512,512]{1,0:T(8,128)(2,1)} collective-permute-done((bf16[512,512]{1,0:T(8,128)(2,1)S(1)}, bf16[512,512]{1,0:T(8,128)(2,1)}, u32[]{:S(2)}, u32[]{:S(2)}) %collective-permute-start.10) | collective-permute-done | bytes 524320 | tf_op jit(solution)/shard_map/ppermute | solution.py:32
  96.3 3.1 %collective-permute-start.14 = (bf16[512,512]{1,0:T(8,128)(2,1)}, bf16[512,512]{1,0:T(8,128)(2,1)}, u32[]{:S(2)}, u32[]{:S(2)}) collective-permute-start(bf16[512,512]{1,0:T(8,128)(2,1)} %collective-permute-done.13.refs_1_), channel_id=1, source_target_pairs={{0,112},{16,0},{32,16},{48,32},{64,48},{80,64},{96,80},{112,96},{1... | collective-permute-start | bytes 1572872 | tf_op jit(solution)/shard_map/ppermute | solution.py:32
  99.4 2.5 %copy-done = bf16[4096,640]{1,0:T(8,128)(2,1)S(1)} copy-done((bf16[4096,640]{1,0:T(8,128)(2,1)S(1)}, bf16[4096,640]{1,0:T(8,128)(2,1)}, u32[]{:S(2)}) %copy-start) | copy-done | bytes 5242904
  101.9 2.7 %shard_map.88 = (f32[256,512]{1,0:T(8,128)S(1)}, f32[256,512]{1,0:T(8,128)S(1)}) custom-call(s32[2]{0:T(128)S(1)} %pad_add_fusion.where, bf16[16,256,640]{2,1,0:T(8,128)(2,1)S(1)} %bitcast.61, bf16[512,512]{1,0:T(8,128)(2,1)S(1)} %get-tuple-element.60.refs_0_, bf16[512,512]{1,0:T(8,128)(2,1)S(1)} %collective-permute-done.2.refs_1_, ...), custom_call_target="tpu_custom_call" | custom-call | flops 1342177280 | bytes 8912896 | tf_op jit(solution)/shard_map/pallas_call | solution.py:85
  105.1 2.8 %shard_map.89 = (f32[256,512]{1,0:T(8,128)S(1)}, f32[256,512]{1,0:T(8,128)S(1)}) custom-call(s32[2]{0:T(128)S(1)} %pad_add_fusion.where, bf16[16,256,640]{2,1,0:T(8,128)(2,1)S(1)} %bitcast.62, bf16[512,512]{1,0:T(8,128)(2,1)} %collective-permute-done.9.refs_0_, bf16[512,512]{1,0:T(8,128)(2,1)} %collective-permute-done.7.refs_1_, ...), custom_call_target="tpu_custom_call" | custom-call | flops 805306368 | bytes 7864320 | tf_op jit(solution)/shard_map/pallas_call | solution.py:85
  107.9 3.0 %collective-permute-start.16 = (f32[256,512]{1,0:T(8,128)S(1)}, f32[256,512]{1,0:T(8,128)}, u32[]{:S(2)}, u32[]{:S(2)}) collective-permute-start(f32[256,512]{1,0:T(8,128)S(1)} %get-tuple-element.41), channel_id=1, source_target_pairs={{0,128},{128,0},{1,129},{129,1},{2,130},{130,2},{3,131},{131,3},{4... | collective-permute-start | bytes 1572872 | tf_op jit(solution)/shard_map/ppermute | solution.py:131
  110.9 2.7 %shard_map.86 = (f32[256,512]{1,0:T(8,128)S(1)}, f32[256,512]{1,0:T(8,128)S(1)}) custom-call(s32[2]{0:T(128)S(1)} %pad_add_fusion.where, bf16[16,256,640]{2,1,0:T(8,128)(2,1)S(1)} %bitcast.63, bf16[512,512]{1,0:T(8,128)(2,1)S(1)} %get-tuple-element.59.refs_0_, bf16[512,512]{1,0:T(8,128)(2,1)S(1)} %collective-permute-done.4.refs_1_, ...), custom_call_target="tpu_custom_call" | custom-call | flops 1342177280 | bytes 8912896 | tf_op jit(solution)/shard_map/pallas_call | solution.py:85
  115.5 2.8 %shard_map.87 = (f32[256,512]{1,0:T(8,128)S(1)}, f32[256,512]{1,0:T(8,128)S(1)}) custom-call(s32[2]{0:T(128)S(1)} %pad_add_fusion.where, bf16[16,256,640]{2,1,0:T(8,128)(2,1)S(1)} %bitcast.64, bf16[512,512]{1,0:T(8,128)(2,1)} %collective-permute-done.11.refs_0_, bf16[512,512]{1,0:T(8,128)(2,1)} %collective-permute-done.13.refs_1_, ...), custom_call_target="tpu_custom_call" | custom-call | flops 805306368 | bytes 7864320 | tf_op jit(solution)/shard_map/pallas_call | solution.py:85
  118.2 2.9 %collective-permute-start.17 = (f32[256,512]{1,0:T(8,128)S(1)}, f32[256,512]{1,0:T(8,128)}, u32[]{:S(2)}, u32[]{:S(2)}) collective-permute-start(f32[256,512]{1,0:T(8,128)S(1)} %get-tuple-element.43), channel_id=1, source_target_pairs={{0,128},{128,0},{1,129},{129,1},{2,130},{130,2},{3,131},{131,3},{4... | collective-permute-start | bytes 1572872 | tf_op jit(solution)/shard_map/ppermute | solution.py:131
  122.6 3.9 %fusion.35 = (f32[256]{0:T(256)S(1)}, f32[256,1024]{1,0:T(8,128)S(1)}) fusion(bf16[256,2048]{0,1:T(8,128)(2,1)} %bitcast.67, bf16[2048,1024]{1,0:T(8,128)(2,1)} %param.11), kind=kOutput, calls=%fused_computation.55 | convolution fusion | flops 1074003712 | bytes 6292480 | tf_op jit(solution)/shard_map/dot_general | solution.py:163
  128.1 6.3 %collective-permute-done.17 = f32[256,512]{1,0:T(8,128)} collective-permute-done((f32[256,512]{1,0:T(8,128)S(1)}, f32[256,512]{1,0:T(8,128)}, u32[]{:S(2)}, u32[]{:S(2)}) %collective-permute-start.17) | collective-permute-done | bytes 524320 | tf_op jit(solution)/shard_map/ppermute | solution.py:131
  137.0 6.8 %all-to-all-start = ((f32[16,8,256]{2,1,0:T(8,128)}), f32[16,8,256]{2,1,0:T(8,128)S(1)}, u32[]{:S(2)}, u32[]{:S(2)}) async-start(f32[16,8,256]{2,1,0:T(8,128)} %broadcast_in_dim.7), calls=%async_computation | async-start | bytes 262144 | tf_op jit(solution)/shard_map/all_to_all | solution.py:191
  143.8 6.1 %all-to-all-done = f32[16,8,256]{2,1,0:T(8,128)S(1)} async-done(((f32[16,8,256]{2,1,0:T(8,128)}), f32[16,8,256]{2,1,0:T(8,128)S(1)}, u32[]{:S(2)}, u32[]{:S(2)}) %all-to-all-start) | async-done | bytes 131104 | tf_op jit(solution)/shard_map/all_to_all | solution.py:191
  150.0 4.3 %fusion = bf16[32,16,8,128]{3,2,1,0:T(8,128)(2,1)S(1)} fusion(bf16[2048,1024]{1,0:T(8,128)(2,1)} %param.11, f32[256,1024]{1,0:T(8,128)} %copy-done.1, f32[256,512]{1,0:T(8,128)S(1)} %get-tuple-element.56, f32[256,512]{1,0:T(8,128)S(1)} %get-tuple-element.58, f32[256]{0:T(256)S(1)} %get-tuple-element.54, f32[256]{0:T(256)S(1)} %get-tuple-element.65, ...), kind=kOutput, calls=%fused_computation.1 | convolution fusion | flops 1077411840 | bytes 7350272 | tf_op jit(solution)/shard_map/dot_general | solution.py:227
  155.5 3.9 %all-to-all-start.1 = ((bf16[16,256,128]{2,1,0:T(8,128)(2,1)}), bf16[16,256,128]{2,1,0:T(8,128)(2,1)S(1)}, u32[]{:S(2)}, u32[]{:S(2)}) async-start(bf16[16,256,128]{2,1,0:T(8,128)(2,1)} %bitcast.60), calls=%async_computation.1 | async-start | bytes 2097152 | tf_op jit(solution)/shard_map/all_to_all | solution.py:231
  160.0 15.4 %all-to-all-done.1 = bf16[16,256,128]{2,1,0:T(8,128)(2,1)S(1)} async-done(((bf16[16,256,128]{2,1,0:T(8,128)(2,1)}), bf16[16,256,128]{2,1,0:T(8,128)(2,1)S(1)}, u32[]{:S(2)}, u32[]{:S(2)}) %all-to-all-start.1) | async-done | bytes 1048608 | tf_op jit(solution)/shard_map/all_to_all | solution.py:231
  (47 shorter events, 18.7 us)
Async XLA Ops:
  7.2 92.3 %all-gather.3.cloned.1.call-start = ((), (), s32[]{:S(2)}) async-start(), calls=%async_computation.2 | async-start | bytes 5570560 | tf_op jit(solution)/shard_map/all_gather | solution.py:149
  10.7 23.0 %collective-permute-start.2 = (bf16[512,512]{1,0:T(8,128)(2,1)S(1)}, bf16[512,512]{1,0:T(8,128)(2,1)S(1)}, u32[]{:S(2)}, u32[]{:S(2)}) collective-permute-start(bf16[512,512]{1,0:T(8,128)(2,1)S(1)} %get-tuple-element.60.refs_0_), channel_id=1, source_target_pairs={{0,16},{16,32},{32,48},{48,64},{64,80},{80,96},{96,112},{112,0},{1... | collective-permute-start | bytes 1572872 | tf_op jit(solution)/shard_map/ppermute | solution.py:32
  13.2 20.5 %collective-permute-start.3 = (bf16[512,512]{1,0:T(8,128)(2,1)S(1)}, bf16[512,512]{1,0:T(8,128)(2,1)S(1)}, u32[]{:S(2)}, u32[]{:S(2)}) collective-permute-start(bf16[512,512]{1,0:T(8,128)(2,1)S(1)} %get-tuple-element.60.refs_0_), channel_id=1, source_target_pairs={{0,112},{16,0},{32,16},{48,32},{64,48},{80,64},{96,80},{112,96},{1... | collective-permute-start | bytes 1572872 | tf_op jit(solution)/shard_map/ppermute | solution.py:32
  17.3 22.8 %collective-permute-start.4 = (bf16[512,512]{1,0:T(8,128)(2,1)S(1)}, bf16[512,512]{1,0:T(8,128)(2,1)S(1)}, u32[]{:S(2)}, u32[]{:S(2)}) collective-permute-start(bf16[512,512]{1,0:T(8,128)(2,1)S(1)} %get-tuple-element.59.refs_0_), channel_id=1, source_target_pairs={{0,16},{16,32},{32,48},{48,64},{64,80},{80,96},{96,112},{112,0},{1... | collective-permute-start | bytes 1572872 | tf_op jit(solution)/shard_map/ppermute | solution.py:32
  17.3 25.3 %collective-permute-start.5 = (bf16[512,512]{1,0:T(8,128)(2,1)S(1)}, bf16[512,512]{1,0:T(8,128)(2,1)S(1)}, u32[]{:S(2)}, u32[]{:S(2)}) collective-permute-start(bf16[512,512]{1,0:T(8,128)(2,1)S(1)} %get-tuple-element.59.refs_0_), channel_id=1, source_target_pairs={{0,112},{16,0},{32,16},{48,32},{64,48},{80,64},{96,80},{112,96},{1... | collective-permute-start | bytes 1572872 | tf_op jit(solution)/shard_map/ppermute | solution.py:32
  19.9 10.1 %collective-permute-start = (bf16[256,512]{1,0:T(8,128)(2,1)S(1)}, bf16[256,512]{1,0:T(8,128)(2,1)S(1)}, u32[]{:S(2)}, u32[]{:S(2)}) collective-permute-start(bf16[256,512]{1,0:T(8,128)(2,1)S(1)} %fusion.7), channel_id=1, source_target_pairs={{0,0},{1,4},{2,7},{3,3},{4,1},{5,5},{6,6},{7,2},{16,18},{17,16},{1... | collective-permute-start | bytes 786440 | tf_op jit(solution)/shard_map/ppermute | solution.py:46
  30.0 16.6 %collective-permute-start.1 = (bf16[256,512]{1,0:T(8,128)(2,1)S(1)}, bf16[256,512]{1,0:T(8,128)(2,1)S(1)}, u32[]{:S(2)}, u32[]{:S(2)}) collective-permute-start(bf16[256,512]{1,0:T(8,128)(2,1)S(1)} %collective-permute-done), channel_id=1, source_target_pairs={{0,0},{4,20},{7,39},{3,51},{1,65},{5,85},{6,102},{2,114},{18,2},{1... | collective-permute-start | bytes 786440 | tf_op jit(solution)/shard_map/ppermute | solution.py:47
  48.3 15.4 %collective-permute-start.6 = (bf16[512,512]{1,0:T(8,128)(2,1)S(1)}, bf16[512,512]{1,0:T(8,128)(2,1)}, u32[]{:S(2)}, u32[]{:S(2)}) collective-permute-start(bf16[512,512]{1,0:T(8,128)(2,1)S(1)} %collective-permute-done.3.refs_2_), channel_id=1, source_target_pairs={{0,112},{16,0},{32,16},{48,32},{64,48},{80,64},{96,80},{112,96},{1... | collective-permute-start | bytes 1572872 | tf_op jit(solution)/shard_map/ppermute | solution.py:32
  51.9 15.3 %collective-permute-start.8 = (bf16[512,512]{1,0:T(8,128)(2,1)S(1)}, bf16[512,512]{1,0:T(8,128)(2,1)}, u32[]{:S(2)}, u32[]{:S(2)}) collective-permute-start(bf16[512,512]{1,0:T(8,128)(2,1)S(1)} %collective-permute-done.2.refs_1_), channel_id=1, source_target_pairs={{0,16},{16,32},{32,48},{48,64},{64,80},{80,96},{96,112},{112,0},{1... | collective-permute-start | bytes 1572872 | tf_op jit(solution)/shard_map/ppermute | solution.py:32
  51.9 23.0 %collective-permute-start.12 = (bf16[512,512]{1,0:T(8,128)(2,1)S(1)}, bf16[512,512]{1,0:T(8,128)(2,1)}, u32[]{:S(2)}, u32[]{:S(2)}) collective-permute-start(bf16[512,512]{1,0:T(8,128)(2,1)S(1)} %collective-permute-done.5.refs_2_), channel_id=1, source_target_pairs={{0,112},{16,0},{32,16},{48,32},{64,48},{80,64},{96,80},{112,96},{1... | collective-permute-start | bytes 1572872 | tf_op jit(solution)/shard_map/ppermute | solution.py:32
  63.7 22.6 %collective-permute-start.7 = (bf16[512,512]{1,0:T(8,128)(2,1)}, bf16[512,512]{1,0:T(8,128)(2,1)}, u32[]{:S(2)}, u32[]{:S(2)}) collective-permute-start(bf16[512,512]{1,0:T(8,128)(2,1)} %collective-permute-done.6.refs_4_), channel_id=1, source_target_pairs={{0,112},{16,0},{32,16},{48,32},{64,48},{80,64},{96,80},{112,96},{1... | collective-permute-start | bytes 1572872 | tf_op jit(solution)/shard_map/ppermute | solution.py:32
  67.2 19.1 %collective-permute-start.9 = (bf16[512,512]{1,0:T(8,128)(2,1)}, bf16[512,512]{1,0:T(8,128)(2,1)}, u32[]{:S(2)}, u32[]{:S(2)}) collective-permute-start(bf16[512,512]{1,0:T(8,128)(2,1)} %collective-permute-done.8.refs_3_), channel_id=1, source_target_pairs={{0,16},{16,32},{32,48},{48,64},{64,80},{80,96},{96,112},{112,0},{1... | collective-permute-start | bytes 1572872 | tf_op jit(solution)/shard_map/ppermute | solution.py:32
  67.2 26.7 %collective-permute-start.10 = (bf16[512,512]{1,0:T(8,128)(2,1)S(1)}, bf16[512,512]{1,0:T(8,128)(2,1)}, u32[]{:S(2)}, u32[]{:S(2)}) collective-permute-start(bf16[512,512]{1,0:T(8,128)(2,1)S(1)} %collective-permute-done.4.refs_1_), channel_id=1, source_target_pairs={{0,16},{16,32},{32,48},{48,64},{64,80},{80,96},{96,112},{112,0},{1... | collective-permute-start | bytes 1572872 | tf_op jit(solution)/shard_map/ppermute | solution.py:32
  74.9 21.4 %collective-permute-start.13 = (bf16[512,512]{1,0:T(8,128)(2,1)}, bf16[512,512]{1,0:T(8,128)(2,1)}, u32[]{:S(2)}, u32[]{:S(2)}) collective-permute-start(bf16[512,512]{1,0:T(8,128)(2,1)} %collective-permute-done.12.refs_4_), channel_id=1, source_target_pairs={{0,112},{16,0},{32,16},{48,32},{64,48},{80,64},{96,80},{112,96},{1... | collective-permute-start | bytes 1572872 | tf_op jit(solution)/shard_map/ppermute | solution.py:32
  86.3 18.9 %collective-permute-start.15 = (bf16[512,512]{1,0:T(8,128)(2,1)}, bf16[512,512]{1,0:T(8,128)(2,1)}, u32[]{:S(2)}, u32[]{:S(2)}) collective-permute-start(bf16[512,512]{1,0:T(8,128)(2,1)} %collective-permute-done.9.refs_0_), channel_id=1, source_target_pairs={{0,16},{16,32},{32,48},{48,64},{64,80},{80,96},{96,112},{112,0},{1... | collective-permute-start | bytes 1572872 | tf_op jit(solution)/shard_map/ppermute | solution.py:32
  93.9 21.6 %collective-permute-start.11 = (bf16[512,512]{1,0:T(8,128)(2,1)}, bf16[512,512]{1,0:T(8,128)(2,1)}, u32[]{:S(2)}, u32[]{:S(2)}) collective-permute-start(bf16[512,512]{1,0:T(8,128)(2,1)} %collective-permute-done.10.refs_3_), channel_id=1, source_target_pairs={{0,16},{16,32},{32,48},{48,64},{64,80},{80,96},{96,112},{112,0},{1... | collective-permute-start | bytes 1572872 | tf_op jit(solution)/shard_map/ppermute | solution.py:32
  96.3 19.1 %collective-permute-start.14 = (bf16[512,512]{1,0:T(8,128)(2,1)}, bf16[512,512]{1,0:T(8,128)(2,1)}, u32[]{:S(2)}, u32[]{:S(2)}) collective-permute-start(bf16[512,512]{1,0:T(8,128)(2,1)} %collective-permute-done.13.refs_1_), channel_id=1, source_target_pairs={{0,112},{16,0},{32,16},{48,32},{64,48},{80,64},{96,80},{112,96},{1... | collective-permute-start | bytes 1572872 | tf_op jit(solution)/shard_map/ppermute | solution.py:32
  99.4 2.5 %copy-start = (bf16[4096,640]{1,0:T(8,128)(2,1)S(1)}, bf16[4096,640]{1,0:T(8,128)(2,1)}, u32[]{:S(2)}) copy-start(bf16[4096,640]{1,0:T(8,128)(2,1)} %all-gather.3.cloned.1.call-done) | copy-start | bytes 15728644
  107.9 18.6 %collective-permute-start.16 = (f32[256,512]{1,0:T(8,128)S(1)}, f32[256,512]{1,0:T(8,128)}, u32[]{:S(2)}, u32[]{:S(2)}) collective-permute-start(f32[256,512]{1,0:T(8,128)S(1)} %get-tuple-element.41), channel_id=1, source_target_pairs={{0,128},{128,0},{1,129},{129,1},{2,130},{130,2},{3,131},{131,3},{4... | collective-permute-start | bytes 1572872 | tf_op jit(solution)/shard_map/ppermute | solution.py:131
  118.2 16.1 %collective-permute-start.17 = (f32[256,512]{1,0:T(8,128)S(1)}, f32[256,512]{1,0:T(8,128)}, u32[]{:S(2)}, u32[]{:S(2)}) collective-permute-start(f32[256,512]{1,0:T(8,128)S(1)} %get-tuple-element.43), channel_id=1, source_target_pairs={{0,128},{128,0},{1,129},{129,1},{2,130},{130,2},{3,131},{131,3},{4... | collective-permute-start | bytes 1572872 | tf_op jit(solution)/shard_map/ppermute | solution.py:131
  122.6 13.0 %copy-start.3 = (s32[256]{0:T(256)S(1)}, s32[256]{0:T(256)}, u32[]{:S(2)}) copy-start(s32[256]{0:T(256)} %param.12) | copy-start | bytes 3076
  126.5 9.1 %copy-start.1 = (f32[256,1024]{1,0:T(8,128)}, f32[256,1024]{1,0:T(8,128)S(1)}, u32[]{:S(2)}) copy-start(f32[256,1024]{1,0:T(8,128)S(1)} %get-tuple-element.70) | copy-start | bytes 3145732
  126.5 17.3 %copy-start.2 = (s32[256]{0:T(256)S(1)}, s32[256]{0:T(256)}, u32[]{:S(2)}) copy-start(s32[256]{0:T(256)} %param.13) | copy-start | bytes 3076
  137.0 12.9 %all-to-all-start = ((f32[16,8,256]{2,1,0:T(8,128)}), f32[16,8,256]{2,1,0:T(8,128)S(1)}, u32[]{:S(2)}, u32[]{:S(2)}) async-start(f32[16,8,256]{2,1,0:T(8,128)} %broadcast_in_dim.7), calls=%async_computation | async-start | bytes 262144 | tf_op jit(solution)/shard_map/all_to_all | solution.py:191
  155.5 19.9 %all-to-all-start.1 = ((bf16[16,256,128]{2,1,0:T(8,128)(2,1)}), bf16[16,256,128]{2,1,0:T(8,128)(2,1)S(1)}, u32[]{:S(2)}, u32[]{:S(2)}) async-start(bf16[16,256,128]{2,1,0:T(8,128)(2,1)} %bitcast.60), calls=%async_computation.1 | async-start | bytes 2097152 | tf_op jit(solution)/shard_map/all_to_all | solution.py:231
Sparse Core Ops, SparseCore 0:
  48.4 44.7 all-gather.2

commit v3 on v2

--- a/solution.py
+++ b/solution.py
@@ -47,54 +47,62 @@
     return lax.ppermute(rows, ("z", "x", "c"), along)
 
 
-def chunk_kernel(places, held, where, rows, *refs):
-    heads, refs = refs[: len(places)], refs[len(places) :]
-    sums, (away, keep, rows_in, heads_in, sems) = refs[:held], refs[held:]
+def chunk_kernel(places, chunks, where, rows, *refs):
+    steps = len(places)
+    heads, refs = refs[: chunks * steps], refs[chunks * steps :]
+    (rows_in, heads_in, rows_sems, heads_sems), refs = refs[-4:], refs[:-4]
+    sums, outs = refs[: -2 * chunks], refs[-2 * chunks :]
     copies = []
-    for i, ((slot, start), head) in enumerate(zip(places, heads)):
-        depth = head.shape[0]
-        span = pl.ds(0, depth)
-        mine = [pltpu.make_async_copy(head, heads_in.at[i, span], sems.at[i, 2])]
+    for i, (slot, start) in enumerate(places):
+        depth = heads[i].shape[0]
+        mine = []
         for side in (0, 1):
             block = rows.at[where[side] * NZ + slot, :, pl.ds(start, depth)]
-            mine.append(pltpu.make_async_copy(block, rows_in.at[i, side, :, span], sems.at[i, side]))
+            mine.append(pltpu.make_async_copy(block, rows_in.at[i, side], rows_sems.at[i, side]))
+        for k in range(chunks):
+            j = k * steps + i
+            mine.append(pltpu.make_async_copy(heads[j], heads_in.at[j], heads_sems.at[j]))
         for copy in mine:
             copy.start()
         copies.append(mine)
-    totals = [s[...] for s in sums] or [None, None]
+    totals = [s[...] for s in sums] or [None] * (2 * chunks)
     for i, mine in enumerate(copies):
-        depth = heads[i].shape[0]
         for copy in mine:
             copy.wait()
-        for side in (0, 1):
-            part = jnp.dot(
-                rows_in[i, side, :, :depth],
-                heads_in[i, :depth],
-                preferred_element_type=jnp.float32,
-            )
-            totals[side] = part if totals[side] is None else totals[side] + part
-    away[...], keep[...] = totals
-
-
-def chunk_logits(where, rows, blocks, sums=()):
-    places, heads = zip(*blocks)
-    tokens, width = rows.shape[1], heads[0].shape[1]
-    depth, size = max(h.shape[0] for h in heads), sum(h.size for h in heads)
+        for k in range(chunks):
+            for side in (0, 1):
+                part = jnp.dot(
+                    rows_in[i, side],
+                    heads_in[k * steps + i],
+                    preferred_element_type=jnp.float32,
+                )
+                total = totals[2 * k + side]
+                totals[2 * k + side] = part if total is None else total + part
+    for out, total in zip(outs, totals):
+        out[...] = total
+
+
+def chunk_logits(where, rows, chunks, sums=()):
+    places = [place for place, _ in chunks[0]]
+    heads = [head for blocks in chunks for _, head in blocks]
+    tokens, (depth, width) = rows.shape[1], heads[0].shape
+    size = sum(h.size for h in heads)
     out = jax.ShapeDtypeStruct((tokens, width), jnp.float32)
     vmem, loose = pl.BlockSpec(memory_space=pltpu.VMEM), pl.BlockSpec(memory_space=pl.ANY)
     return pl.pallas_call(
-        functools.partial(chunk_kernel, places, len(sums)),
-        out_shape=(out, out),
+        functools.partial(chunk_kernel, places, len(chunks)),
+        out_shape=(out,) * (2 * len(chunks)),
         in_specs=[pl.BlockSpec(memory_space=pltpu.SMEM)]
         + [loose] * (1 + len(heads))
         + [vmem] * len(sums),
-        out_specs=(vmem, vmem),
+        out_specs=(vmem,) * (2 * len(chunks)),
         scratch_shapes=[
-            pltpu.VMEM((len(heads), 2, tokens, depth), jnp.bfloat16),
+            pltpu.VMEM((len(places), 2, tokens, depth), jnp.bfloat16),
             pltpu.VMEM((len(heads), depth, width), jnp.bfloat16),
-            pltpu.SemaphoreType.DMA((len(heads), 3)),
+            pltpu.SemaphoreType.DMA((len(places), 2)),
+            pltpu.SemaphoreType.DMA((len(heads),)),
         ],
-        compiler_params=pltpu.CompilerParams(vmem_limit_bytes=28 * 2**20),
+        compiler_params=pltpu.CompilerParams(vmem_limit_bytes=50 * 2**20),
         cost_estimate=pl.CostEstimate(
             flops=4 * tokens * size,
             bytes_accessed=rows.size * 2 + size * 2 + 8 * tokens * width,
@@ -125,6 +133,52 @@
                     slot = OFFSETS.index(-way * s if s < 4 else 4)
                     found.append(((slot, 0), self.block[k, s, way]))
         return found
+
+
+def gradient_kernel(first, per_row, ids, teacher, student, head, out, grad):
+    @pl.when(pl.program_id(0) == 0)
+    def _():
+        rows = per_row[...]
+        teacher_part = rows[:, 1:2] * jnp.exp(teacher[...] - rows[:, 0:1])
+        student_part = rows[:, 3:4] * jnp.exp(student[...] - rows[:, 2:3])
+        columns = lax.broadcasted_iota(jnp.int32, teacher.shape, 1) + first[0]
+        chosen = jnp.where(ids[...] == columns, rows[:, 4:5], 0.0)
+        grad[...] = (student_part - teacher_part - chosen).astype(grad.dtype)
+
+    terms = lax.dot_general(
+        grad[...], head[...], (((1,), (1,)), ((), ())), preferred_element_type=jnp.float32
+    )
+    width = out.shape[2]
+    for k in range(out.shape[0]):
+        out[k] = terms[:, k * width : (k + 1) * width].astype(out.dtype)
+
+
+def gradient_terms(first, per_row, ids, teacher, student, head, width):
+    tokens, shard = teacher.shape
+    features, step = head.shape[0], 4
+    smem = pl.BlockSpec(memory_space=pltpu.SMEM)
+    whole = pl.BlockSpec((tokens, shard), lambda i: (0, 0))
+    return pl.pallas_call(
+        gradient_kernel,
+        grid=(features // (step * width),),
+        out_shape=jax.ShapeDtypeStruct((features // width, tokens, width), jnp.bfloat16),
+        in_specs=[
+            smem,
+            pl.BlockSpec(per_row.shape, lambda i: (0, 0)),
+            pl.BlockSpec(ids.shape, lambda i: (0, 0)),
+            whole,
+            whole,
+            pl.BlockSpec((step * width, shard), lambda i: (i, 0)),
+        ],
+        out_specs=pl.BlockSpec((step, tokens, width), lambda i: (i, 0, 0)),
+        scratch_shapes=[pltpu.VMEM((tokens, shard), jnp.bfloat16)],
+        compiler_params=pltpu.CompilerParams(vmem_limit_bytes=24 * 2**20),
+        cost_estimate=pl.CostEstimate(
+            flops=2 * tokens * shard * features,
+            bytes_accessed=head.size * 2 + 8 * tokens * shard + 2 * tokens * features,
+            transcendentals=2 * tokens * shard,
+        ),
+    )(first, per_row, ids, teacher, student, head)
 
 
 def swap_halves(x):
@@ -152,11 +206,12 @@
             ring.send(k, s)
 
     where = jnp.stack([1 - yh, yh]).astype(jnp.int32)
-    where = ring.hold(where, [(0, 3, -1), (0, 3, +1)])
     for k in (0, 1):
         ring.send(k, 4)
-    sums = [chunk_logits(where, rows, ring.blocks(k, range(3))) for k in (0, 1)]
-    products = [chunk_logits(where, rows, ring.blocks(k, (3, 4)), sums[k]) for k in (0, 1)]
+    sums = chunk_logits(where, rows, [ring.blocks(k, range(3)) for k in (0, 1)])
+    products = [
+        chunk_logits(where, rows, [ring.blocks(k, (3, 4))], sums[2 * k : 2 * k + 2]) for k in (0, 1)
+    ]
     hidden, products[1] = order(rows, products[1])
     hidden = jnp.transpose(hidden[:, :, teacher_codes.shape[1] :], (1, 0, 2))
     hidden = hidden.reshape(own_rows, 16 * features)
@@ -214,20 +269,28 @@
     cross_rows = top_student + jnp.log(sum_student) - target
     live_mask = loss_mask.astype(jnp.float32)
     token_loss = live_mask * (divergence + CROSS_WEIGHT * cross_rows)
-    teacher_prob = jnp.exp(teacher_logits - top_teacher[:, None]) / sum_teacher[:, None]
-    student_prob = jnp.exp(student_logits - top_student[:, None]) / sum_student[:, None]
-    logit_grad = (
-        live_mask[:, None]
-        * (
-            (1.0 + CROSS_WEIGHT) * student_prob
-            - teacher_prob
-            - CROSS_WEIGHT * chosen.astype(jnp.float32)
-        )
-    ).astype(jnp.bfloat16)
-    hidden_terms = lax.dot_general(
-        logit_grad, student_head, (((1,), (1,)), ((), ())), preferred_element_type=jnp.float32
-    ).astype(jnp.bfloat16)
-    hidden_terms = jnp.transpose(hidden_terms.reshape(own_rows, 16, features), (1, 0, 2))
+    zero = jnp.zeros_like(live_mask)
+    per_row = jnp.stack(
+        [
+            top_teacher,
+            live_mask / sum_teacher,
+            top_student,
+            (1.0 + CROSS_WEIGHT) * live_mask / sum_student,
+            CROSS_WEIGHT * live_mask,
+            zero,
+            zero,
+            zero,
+        ]
+    )
+    hidden_terms = gradient_terms(
+        (lax.axis_index(VOCAB) * shard_width).astype(jnp.int32)[None],
+        jnp.transpose(per_row),
+        token_ids[:, None],
+        teacher_logits,
+        student_logits,
+        student_head,
+        features,
+    )
     hidden_terms = lax.all_to_all(hidden_terms, VOCAB, split_axis=0, concat_axis=0, tiled=True)
     grad_hidden = jnp.sum(hidden_terms.astype(jnp.float32), axis=0).astype(jnp.bfloat16)
     return (grad_hidden, token_loss)

time: 184 us -> 178 us (0.967)
  blocking collectives: 0 us -> 18.5 us
  waiting for transfers between devices: 81.3 us -> 65.9 us
  starting transfers between devices: 52.3 us -> 43.6 us
  matrix products: 8.14 us -> 1.36 us
  local copies, waits for them, and re-layouts: 8.38 us -> 12.8 us
  Pallas kernels: 11 us -> 14.4 us
    all_to_all x0 -> x1, blocking collectives: none -> 18.5 us  [body(): lax.all_to_all(hidden_terms, VOCAB, split_axis=0, concat_axis=0, tiled=True)]
    all_to_all x1 -> x0, waiting for transfers between devices: 15.4 us -> none  [body(): lax.all_to_all(hidden_terms, VOCAB, split_axis=0, concat_axis=0, tiled=True)]
    ppermute x14, waiting for transfers between devices: 45.4 us -> 38.4 us  [shift(): return lax.ppermute(x, 'z', [(i, (i + s) % NZ) for i in range(NZ)])]
    ppermute x2, waiting for transfers between devices: 6.31 us -> 12.4 us  [swap_halves(): return lax.ppermute(x, 'yh', [(0, 1), (1, 0)])]
    unnamed x8 -> x38, local copies, waits for them, and re-layouts: 2.5 us -> 6.78 us
    dot_general x1 -> x0, matrix products: 4.26 us -> none  [body(): lax.dot_general(logit_grad, student_head, (((1,), (1,)), ((), ())), prefe...]
    all_to_all x1 -> x0, starting transfers between devices: 3.9 us -> none  [body(): lax.all_to_all(hidden_terms, VOCAB, split_axis=0, concat_axis=0, tiled=True)]
    pallas_call x4, Pallas kernels: 11 us -> 14.4 us  [the longest x3 11.9 us: chunk_logits(): pl.pallas_call(functools.partial(chunk_kernel, places, len(chunks)), out_...]
  transfers between devices with their start and end apart: 21 -> 20, of which waited for: 14 -> 14; matrix products, arithmetic and copies ran while one was open for 4% -> 3% of each run, Pallas kernels for 6% -> 7%
where the time goes in v3:
time: 178 us; the launch traced here: 177 us
  waiting for transfers between devices  65.9 us (37%)
  starting transfers between devices  43.6 us (24%)
  blocking collectives  18.5 us (10%)
  Pallas kernels  14.4 us (8%)
  between operations  14.3 us (8%)
  local copies, waits for them, and re-layouts  12.8 us (7%)
  other arithmetic  6.32 us (4%)
    ppermute x14, waiting for transfers between devices, shift(): return lax.ppermute(x, 'z', [(i, (i + s) % NZ) for i in range(NZ)])  38.4 us
    ppermute x14, starting transfers between devices, shift(): return lax.ppermute(x, 'z', [(i, (i + s) % NZ) for i in range(NZ)])  23.1 us
    all_to_all x1, blocking collectives, body(): lax.all_to_all(hidden_terms, VOCAB, split_axis=0, concat_axis=0, tiled=True)  18.5 us
    ppermute x2, waiting for transfers between devices, swap_halves(): return lax.ppermute(x, 'yh', [(0, 1), (1, 0)])  12.4 us
    pallas_call x3, Pallas kernels, chunk_logits(): pl.pallas_call(functools.partial(chunk_kernel, places, len(chunks)), out_...  11.9 us
    unnamed x38, local copies, waits for them, and re-layouts  6.78 us
    ppermute x1, starting transfers between devices, swap_rows_features(): rows = lax.ppermute(rows, ('z', 'x', 'c'), beside)  6.04 us
    all_to_all x1, waiting for transfers between devices, body(): lax.all_to_all(jnp.broadcast_to(stats[None], (16,) + stats.shape), VOCAB,...  5.95 us
  transfers between devices with their start and end apart: 20, of which 14 were waited for; matrix products, arithmetic and copies ran while one was open for 3% of the time, Pallas kernels for 7%

profile of v3, /device:TPU:1, one launch (start us, length us, event | category | flops | bytes accessed | tf_op | source)
XLA Modules:
  0.0 177.1 jit_solution(10509312981175520578)
XLA Ops:
  10.7 2.5 %collective-permute-start.2 = (bf16[512,512]{1,0:T(8,128)(2,1)S(1)}, bf16[512,512]{1,0:T(8,128)(2,1)S(1)}, u32[]{:S(2)}, u32[]{:S(2)}) collective-permute-start(bf16[512,512]{1,0:T(8,128)(2,1)S(1)} %get-tuple-element.55.refs_0_), channel_id=1, source_target_pairs={{0,16},{16,32},{32,48},{48,64},{64,80},{80,96},{96,112},{112,0},{1... | collective-permute-start | bytes 1572872 | tf_op jit(solution)/shard_map/ppermute | solution.py:32
  13.2 4.0 %collective-permute-start.3 = (bf16[512,512]{1,0:T(8,128)(2,1)S(1)}, bf16[512,512]{1,0:T(8,128)(2,1)S(1)}, u32[]{:S(2)}, u32[]{:S(2)}) collective-permute-start(bf16[512,512]{1,0:T(8,128)(2,1)S(1)} %get-tuple-element.55.refs_0_), channel_id=1, source_target_pairs={{0,112},{16,0},{32,16},{48,32},{64,48},{80,64},{96,80},{112,96},{1... | collective-permute-start | bytes 1572872 | tf_op jit(solution)/shard_map/ppermute | solution.py:32
  17.3 2.7 %collective-permute-start.5 = (bf16[512,512]{1,0:T(8,128)(2,1)S(1)}, bf16[512,512]{1,0:T(8,128)(2,1)S(1)}, u32[]{:S(2)}, u32[]{:S(2)}) collective-permute-start(bf16[512,512]{1,0:T(8,128)(2,1)S(1)} %get-tuple-element.54.refs_5_), channel_id=1, source_target_pairs={{0,112},{16,0},{32,16},{48,32},{64,48},{80,64},{96,80},{112,96},{1... | collective-permute-start | bytes 1572872 | tf_op jit(solution)/shard_map/ppermute | solution.py:32
  19.9 6.0 %collective-permute-start = (bf16[256,512]{1,0:T(8,128)(2,1)S(1)}, bf16[256,512]{1,0:T(8,128)(2,1)S(1)}, u32[]{:S(2)}, u32[]{:S(2)}) collective-permute-start(bf16[256,512]{1,0:T(8,128)(2,1)S(1)} %fusion.1), channel_id=1, source_target_pairs={{0,0},{1,4},{2,7},{3,3},{4,1},{5,5},{6,6},{7,2},{16,18},{17,16},{1... | collective-permute-start | bytes 786440 | tf_op jit(solution)/shard_map/ppermute | solution.py:46
  26.0 4.0 %collective-permute-done = bf16[256,512]{1,0:T(8,128)(2,1)S(1)} collective-permute-done((bf16[256,512]{1,0:T(8,128)(2,1)S(1)}, bf16[256,512]{1,0:T(8,128)(2,1)S(1)}, u32[]{:S(2)}, u32[]{:S(2)}) %collective-permute-start) | collective-permute-done | bytes 262176 | tf_op jit(solution)/shard_map/ppermute | solution.py:46
  30.0 3.7 %collective-permute-start.1 = (bf16[256,512]{1,0:T(8,128)(2,1)S(1)}, bf16[256,512]{1,0:T(8,128)(2,1)S(1)}, u32[]{:S(2)}, u32[]{:S(2)}) collective-permute-start(bf16[256,512]{1,0:T(8,128)(2,1)S(1)} %collective-permute-done), channel_id=1, source_target_pairs={{0,0},{4,20},{7,39},{3,51},{1,65},{5,85},{6,102},{2,114},{18,2},{1... | collective-permute-start | bytes 786440 | tf_op jit(solution)/shard_map/ppermute | solution.py:47
  33.7 6.3 %collective-permute-done.4.refs_6_ = bf16[512,512]{1,0:T(8,128)(2,1)S(1)} collective-permute-done((bf16[512,512]{1,0:T(8,128)(2,1)S(1)}, bf16[512,512]{1,0:T(8,128)(2,1)S(1)}, u32[]{:S(2)}, u32[]{:S(2)}) %collective-permute-start.4) | collective-permute-done | bytes 524320 | tf_op jit(solution)/shard_map/ppermute | solution.py:32
  40.1 2.5 %collective-permute-done.5.refs_7_ = bf16[512,512]{1,0:T(8,128)(2,1)S(1)} collective-permute-done((bf16[512,512]{1,0:T(8,128)(2,1)S(1)}, bf16[512,512]{1,0:T(8,128)(2,1)S(1)}, u32[]{:S(2)}, u32[]{:S(2)}) %collective-permute-start.5) | collective-permute-done | bytes 524320 | tf_op jit(solution)/shard_map/ppermute | solution.py:32
  42.6 4.1 %collective-permute-done.1 = bf16[256,512]{1,0:T(8,128)(2,1)S(1)} collective-permute-done((bf16[256,512]{1,0:T(8,128)(2,1)S(1)}, bf16[256,512]{1,0:T(8,128)(2,1)S(1)}, u32[]{:S(2)}, u32[]{:S(2)}) %collective-permute-start.1) | collective-permute-done | bytes 262176 | tf_op jit(solution)/shard_map/ppermute | solution.py:47
  46.7 1.6 pad_maximum_fusion.1
  48.3 3.6 %collective-permute-start.12 = (bf16[512,512]{1,0:T(8,128)(2,1)S(1)}, bf16[512,512]{1,0:T(8,128)(2,1)S(1)}, u32[]{:S(2)}, u32[]{:S(2)}) collective-permute-start(bf16[512,512]{1,0:T(8,128)(2,1)S(1)} %collective-permute-done.5.refs_7_), channel_id=1, source_target_pairs={{0,112},{16,0},{32,16},{48,32},{64,48},{80,64},{96,80},{112,96},{1... | collective-permute-start | bytes 1572872 | tf_op jit(solution)/shard_map/ppermute | solution.py:32
  52.0 10.6 %collective-permute-done.12.refs_9_ = bf16[512,512]{1,0:T(8,128)(2,1)S(1)} collective-permute-done((bf16[512,512]{1,0:T(8,128)(2,1)S(1)}, bf16[512,512]{1,0:T(8,128)(2,1)S(1)}, u32[]{:S(2)}, u32[]{:S(2)}) %collective-permute-start.12) | collective-permute-done | bytes 524320 | tf_op jit(solution)/shard_map/ppermute | solution.py:32
  62.6 3.1 %collective-permute-start.15 = (bf16[512,512]{1,0:T(8,128)(2,1)S(1)}, bf16[512,512]{1,0:T(8,128)(2,1)S(1)}, u32[]{:S(2)}, u32[]{:S(2)}) collective-permute-start(bf16[512,512]{1,0:T(8,128)(2,1)S(1)} %collective-permute-done.12.refs_9_), channel_id=1, source_target_pairs={{0,112},{16,0},{32,16},{48,32},{64,48},{80,64},{96,80},{112,96},{1... | collective-permute-start | bytes 1572872 | tf_op jit(solution)/shard_map/ppermute | solution.py:32
  68.0 10.3 %collective-permute-done.11.refs_8_ = bf16[512,512]{1,0:T(8,128)(2,1)} collective-permute-done((bf16[512,512]{1,0:T(8,128)(2,1)S(1)}, bf16[512,512]{1,0:T(8,128)(2,1)}, u32[]{:S(2)}, u32[]{:S(2)}) %collective-permute-start.11) | collective-permute-done | bytes 524320 | tf_op jit(solution)/shard_map/ppermute | solution.py:32
  78.3 2.7 %collective-permute-start.16 = (bf16[512,512]{1,0:T(8,128)(2,1)S(1)}, bf16[512,512]{1,0:T(8,128)(2,1)S(1)}, u32[]{:S(2)}, u32[]{:S(2)}) collective-permute-start(bf16[512,512]{1,0:T(8,128)(2,1)S(1)} %collective-permute-done.15.refs_1_), channel_id=1, source_target_pairs={{0,112},{16,0},{32,16},{48,32},{64,48},{80,64},{96,80},{112,96},{1... | collective-permute-start | bytes 1572872 | tf_op jit(solution)/shard_map/ppermute | solution.py:32
  81.1 7.5 %collective-permute-done.8.refs_4_ = bf16[512,512]{1,0:T(8,128)(2,1)} collective-permute-done((bf16[512,512]{1,0:T(8,128)(2,1)S(1)}, bf16[512,512]{1,0:T(8,128)(2,1)}, u32[]{:S(2)}, u32[]{:S(2)}) %collective-permute-start.8) | collective-permute-done | bytes 524320 | tf_op jit(solution)/shard_map/ppermute | solution.py:32
  88.6 3.5 %collective-permute-start.9 = (bf16[512,512]{1,0:T(8,128)(2,1)}, bf16[512,512]{1,0:T(8,128)(2,1)S(1)}, u32[]{:S(2)}, u32[]{:S(2)}) collective-permute-start(bf16[512,512]{1,0:T(8,128)(2,1)} %collective-permute-done.8.refs_4_), channel_id=1, source_target_pairs={{0,112},{16,0},{32,16},{48,32},{64,48},{80,64},{96,80},{112,96},{1... | collective-permute-start | bytes 1572872 | tf_op jit(solution)/shard_map/ppermute | solution.py:32
  95.3 5.3 %shard_map.86 = (f32[256,512]{1,0:T(8,128)S(1)}, f32[256,512]{1,0:T(8,128)S(1)}, f32[256,512]{1,0:T(8,128)S(1)}, f32[256,512]{1,0:T(8,128)S(1)}) custom-call(s32[2]{0:T(128)S(1)} %pad_add_fusion.where, bf16[16,256,640]{2,1,0:T(8,128)(2,1)} %bitcast.61, bf16[512,512]{1,0:T(8,128)(2,1)S(1)} %get-tuple-element.55.refs_0_, bf16[512,512]{1,0:T(8,128)(2,1)S(1)} %copy-done.9, ...), custom_call_target="tpu_custom_call" | custom-call | flops 2684354560 | bytes 11534336 | tf_op jit(solution)/shard_map/pallas_call | solution.py:92
  101.5 3.4 %shard_map.88 = (f32[256,512]{1,0:T(8,128)}, f32[256,512]{1,0:T(8,128)S(1)}) custom-call(s32[2]{0:T(128)S(1)} %pad_add_fusion.where, bf16[16,256,640]{2,1,0:T(8,128)(2,1)} %bitcast.62, bf16[512,512]{1,0:T(8,128)(2,1)S(1)} %collective-permute-done.14.refs_0_, bf16[512,512]{1,0:T(8,128)(2,1)S(1)} %collective-permute-done.15.refs_1_, ...), custom_call_target="tpu_custom_call" | custom-call | flops 805306368 | bytes 7864320 | tf_op jit(solution)/shard_map/pallas_call | solution.py:92
  105.8 2.6 %collective-permute-start.17 = (f32[256,512]{1,0:T(8,128)}, f32[256,512]{1,0:T(8,128)}, u32[]{:S(2)}, u32[]{:S(2)}) collective-permute-start(f32[256,512]{1,0:T(8,128)} %get-tuple-element.36), channel_id=1, source_target_pairs={{0,128},{128,0},{1,129},{129,1},{2,130},{130,2},{3,131},{131,3},{4... | collective-permute-start | bytes 1572872 | tf_op jit(solution)/shard_map/ppermute | solution.py:185
  108.3 1.3 slice_bitcast_fusion
  109.6 1.3 copy.44
  111.3 3.2 %shard_map.87 = (f32[256,512]{1,0:T(8,128)S(1)}, f32[256,512]{1,0:T(8,128)S(1)}) custom-call(s32[2]{0:T(128)S(1)} %pad_add_fusion.where, bf16[16,256,640]{2,1,0:T(8,128)(2,1)} %bitcast.64, bf16[512,512]{1,0:T(8,128)(2,1)S(1)} %collective-permute-done.7.refs_0_, bf16[512,512]{1,0:T(8,128)(2,1)S(1)} %collective-permute-done.9.refs_1_, ...), custom_call_target="tpu_custom_call" | custom-call | flops 805306368 | bytes 7864320 | tf_op jit(solution)/shard_map/pallas_call | solution.py:92
  114.5 2.5 %collective-permute-start.13 = (f32[256,512]{1,0:T(8,128)S(1)}, f32[256,512]{1,0:T(8,128)S(1)}, u32[]{:S(2)}, u32[]{:S(2)}) collective-permute-start(f32[256,512]{1,0:T(8,128)S(1)} %get-tuple-element.30), channel_id=1, source_target_pairs={{0,128},{128,0},{1,129},{129,1},{2,130},{130,2},{3,131},{131,3},{4... | collective-permute-start | bytes 1572872 | tf_op jit(solution)/shard_map/ppermute | solution.py:185
  117.0 1.4 fusion.15
  118.4 2.5 %collective-permute-done.17 = f32[256,512]{1,0:T(8,128)} collective-permute-done((f32[256,512]{1,0:T(8,128)}, f32[256,512]{1,0:T(8,128)}, u32[]{:S(2)}, u32[]{:S(2)}) %collective-permute-start.17) | collective-permute-done | bytes 524320 | tf_op jit(solution)/shard_map/ppermute | solution.py:185
  122.0 9.9 %collective-permute-done.13 = f32[256,512]{1,0:T(8,128)S(1)} collective-permute-done((f32[256,512]{1,0:T(8,128)S(1)}, f32[256,512]{1,0:T(8,128)S(1)}, u32[]{:S(2)}, u32[]{:S(2)}) %collective-permute-start.13) | collective-permute-done | bytes 524320 | tf_op jit(solution)/shard_map/ppermute | solution.py:185
  133.6 5.8 %all-to-all-start = ((f32[16,8,256]{2,1,0:T(8,128)}), f32[16,8,256]{2,1,0:T(8,128)S(1)}, u32[]{:S(2)}, u32[]{:S(2)}) async-start(f32[16,8,256]{2,1,0:T(8,128)} %broadcast_in_dim.12), calls=%async_computation | async-start | bytes 262144 | tf_op jit(solution)/shard_map/all_to_all | solution.py:246
  139.5 5.9 %all-to-all-done = f32[16,8,256]{2,1,0:T(8,128)S(1)} async-done(((f32[16,8,256]{2,1,0:T(8,128)}), f32[16,8,256]{2,1,0:T(8,128)S(1)}, u32[]{:S(2)}, u32[]{:S(2)}) %all-to-all-start) | async-done | bytes 131104 | tf_op jit(solution)/shard_map/all_to_all | solution.py:246
  146.3 2.2 %copy-done.1 = bf16[2048,1024]{1,0:T(8,128)(2,1)S(1)} copy-done((bf16[2048,1024]{1,0:T(8,128)(2,1)S(1)}, bf16[2048,1024]{1,0:T(8,128)(2,1)}, u32[]{:S(2)}) %copy-start.1) | copy-done | bytes 4194328
  148.5 2.5 %shard_map.89 = bf16[16,256,128]{2,1,0:T(8,128)(2,1)S(1)} custom-call(s32[1]{0:T(128)} %bitcast.first, f32[256,8]{1,0:T(8,128)S(1)} %bitcast.60, s32[256,1]{1,0:T(8,128)S(1)} %copy.49.ids, f32[256,1024]{1,0:T(8,128)S(1)} %get-tuple-element.53.teacher, f32[256,1024]{1,0:T(8,128)S(1)} %get-tuple-element.69.student, bf16[2048,1024]{1,0:T(8,128)(2,1)S(1)} %copy-done.1), custom_call_target="tpu_custom_call" | custom-call | flops 1073741824 | bytes 7340032 | tf_op jit(solution)/shard_map/pallas_call | solution.py:161
  151.0 18.5 %all_to_all.10 = bf16[16,256,128]{2,1,0:T(8,128)(2,1)S(1)} all-to-all(bf16[16,256,128]{2,1,0:T(8,128)(2,1)S(1)} %shard_map.89), channel_id=1, replica_groups=mesh['yh'=2,'z'=8,'yl'=2,'x'=4,'c'=2] {'yl','x','c'}, dimensions={0} | all-to-all | bytes 2097152 | tf_op jit(solution)/shard_map/all_to_all | solution.py:294
  (77 shorter events, 15.7 us)
Async XLA Ops:
  7.2 86.1 %all-gather.3.cloned.1.call-start = ((), (), s32[]{:S(2)}) async-start(), calls=%async_computation.2 | async-start | bytes 5570560 | tf_op jit(solution)/shard_map/all_gather | solution.py:203
  10.7 41.3 %copy-start.12 = (bf16[512,512]{1,0:T(8,128)(2,1)}, bf16[512,512]{1,0:T(8,128)(2,1)S(1)}, u32[]{:S(2)}) copy-start(bf16[512,512]{1,0:T(8,128)(2,1)S(1)} %get-tuple-element.54.refs_5_) | copy-start | bytes 1572868
  10.7 23.0 %collective-permute-start.2 = (bf16[512,512]{1,0:T(8,128)(2,1)S(1)}, bf16[512,512]{1,0:T(8,128)(2,1)S(1)}, u32[]{:S(2)}, u32[]{:S(2)}) collective-permute-start(bf16[512,512]{1,0:T(8,128)(2,1)S(1)} %get-tuple-element.55.refs_0_), channel_id=1, source_target_pairs={{0,16},{16,32},{32,48},{48,64},{64,80},{80,96},{96,112},{112,0},{1... | collective-permute-start | bytes 1572872 | tf_op jit(solution)/shard_map/ppermute | solution.py:32
  13.2 20.5 %collective-permute-start.3 = (bf16[512,512]{1,0:T(8,128)(2,1)S(1)}, bf16[512,512]{1,0:T(8,128)(2,1)S(1)}, u32[]{:S(2)}, u32[]{:S(2)}) collective-permute-start(bf16[512,512]{1,0:T(8,128)(2,1)S(1)} %get-tuple-element.55.refs_0_), channel_id=1, source_target_pairs={{0,112},{16,0},{32,16},{48,32},{64,48},{80,64},{96,80},{112,96},{1... | collective-permute-start | bytes 1572872 | tf_op jit(solution)/shard_map/ppermute | solution.py:32
  17.3 22.8 %collective-permute-start.4 = (bf16[512,512]{1,0:T(8,128)(2,1)S(1)}, bf16[512,512]{1,0:T(8,128)(2,1)S(1)}, u32[]{:S(2)}, u32[]{:S(2)}) collective-permute-start(bf16[512,512]{1,0:T(8,128)(2,1)S(1)} %get-tuple-element.54.refs_5_), channel_id=1, source_target_pairs={{0,16},{16,32},{32,48},{48,64},{64,80},{80,96},{96,112},{112,0},{1... | collective-permute-start | bytes 1572872 | tf_op jit(solution)/shard_map/ppermute | solution.py:32
  17.3 25.3 %collective-permute-start.5 = (bf16[512,512]{1,0:T(8,128)(2,1)S(1)}, bf16[512,512]{1,0:T(8,128)(2,1)S(1)}, u32[]{:S(2)}, u32[]{:S(2)}) collective-permute-start(bf16[512,512]{1,0:T(8,128)(2,1)S(1)} %get-tuple-element.54.refs_5_), channel_id=1, source_target_pairs={{0,112},{16,0},{32,16},{48,32},{64,48},{80,64},{96,80},{112,96},{1... | collective-permute-start | bytes 1572872 | tf_op jit(solution)/shard_map/ppermute | solution.py:32
  19.9 10.1 %collective-permute-start = (bf16[256,512]{1,0:T(8,128)(2,1)S(1)}, bf16[256,512]{1,0:T(8,128)(2,1)S(1)}, u32[]{:S(2)}, u32[]{:S(2)}) collective-permute-start(bf16[256,512]{1,0:T(8,128)(2,1)S(1)} %fusion.1), channel_id=1, source_target_pairs={{0,0},{1,4},{2,7},{3,3},{4,1},{5,5},{6,6},{7,2},{16,18},{17,16},{1... | collective-permute-start | bytes 786440 | tf_op jit(solution)/shard_map/ppermute | solution.py:46
  30.0 16.6 %collective-permute-start.1 = (bf16[256,512]{1,0:T(8,128)(2,1)S(1)}, bf16[256,512]{1,0:T(8,128)(2,1)S(1)}, u32[]{:S(2)}, u32[]{:S(2)}) collective-permute-start(bf16[256,512]{1,0:T(8,128)(2,1)S(1)} %collective-permute-done), channel_id=1, source_target_pairs={{0,0},{4,20},{7,39},{3,51},{1,65},{5,85},{6,102},{2,114},{18,2},{1... | collective-permute-start | bytes 786440 | tf_op jit(solution)/shard_map/ppermute | solution.py:47
  33.7 32.0 %copy-start.8 = (bf16[512,512]{1,0:T(8,128)(2,1)}, bf16[512,512]{1,0:T(8,128)(2,1)S(1)}, u32[]{:S(2)}) copy-start(bf16[512,512]{1,0:T(8,128)(2,1)S(1)} %collective-permute-done.2.refs_1_) | copy-start | bytes 1572868
  40.1 27.9 %copy-start.14 = (bf16[512,512]{1,0:T(8,128)(2,1)}, bf16[512,512]{1,0:T(8,128)(2,1)S(1)}, u32[]{:S(2)}) copy-start(bf16[512,512]{1,0:T(8,128)(2,1)S(1)} %collective-permute-done.4.refs_6_) | copy-start | bytes 1572868
  42.6 35.7 %copy-start.15 = (bf16[512,512]{1,0:T(8,128)(2,1)}, bf16[512,512]{1,0:T(8,128)(2,1)S(1)}, u32[]{:S(2)}) copy-start(bf16[512,512]{1,0:T(8,128)(2,1)S(1)} %collective-permute-done.5.refs_7_) | copy-start | bytes 1572868
  48.3 14.3 %collective-permute-start.12 = (bf16[512,512]{1,0:T(8,128)(2,1)S(1)}, bf16[512,512]{1,0:T(8,128)(2,1)S(1)}, u32[]{:S(2)}, u32[]{:S(2)}) collective-permute-start(bf16[512,512]{1,0:T(8,128)(2,1)S(1)} %collective-permute-done.5.refs_7_), channel_id=1, source_target_pairs={{0,112},{16,0},{32,16},{48,32},{64,48},{80,64},{96,80},{112,96},{1... | collective-permute-start | bytes 1572872 | tf_op jit(solution)/shard_map/ppermute | solution.py:32
  51.9 15.2 %collective-permute-start.6 = (bf16[512,512]{1,0:T(8,128)(2,1)S(1)}, bf16[512,512]{1,0:T(8,128)(2,1)}, u32[]{:S(2)}, u32[]{:S(2)}) collective-permute-start(bf16[512,512]{1,0:T(8,128)(2,1)S(1)} %collective-permute-done.2.refs_1_), channel_id=1, source_target_pairs={{0,16},{16,32},{32,48},{48,64},{64,80},{80,96},{96,112},{112,0},{1... | collective-permute-start | bytes 1572872 | tf_op jit(solution)/shard_map/ppermute | solution.py:32
  51.9 26.4 %collective-permute-start.11 = (bf16[512,512]{1,0:T(8,128)(2,1)S(1)}, bf16[512,512]{1,0:T(8,128)(2,1)}, u32[]{:S(2)}, u32[]{:S(2)}) collective-permute-start(bf16[512,512]{1,0:T(8,128)(2,1)S(1)} %collective-permute-done.4.refs_6_), channel_id=1, source_target_pairs={{0,16},{16,32},{32,48},{48,64},{64,80},{80,96},{96,112},{112,0},{1... | collective-permute-start | bytes 1572872 | tf_op jit(solution)/shard_map/ppermute | solution.py:32
  62.6 15.7 %copy-start.16 = (bf16[512,512]{1,0:T(8,128)(2,1)}, bf16[512,512]{1,0:T(8,128)(2,1)S(1)}, u32[]{:S(2)}) copy-start(bf16[512,512]{1,0:T(8,128)(2,1)S(1)} %collective-permute-done.12.refs_9_) | copy-start | bytes 1572868
  62.6 15.7 %collective-permute-start.15 = (bf16[512,512]{1,0:T(8,128)(2,1)S(1)}, bf16[512,512]{1,0:T(8,128)(2,1)S(1)}, u32[]{:S(2)}, u32[]{:S(2)}) collective-permute-start(bf16[512,512]{1,0:T(8,128)(2,1)S(1)} %collective-permute-done.12.refs_9_), channel_id=1, source_target_pairs={{0,112},{16,0},{32,16},{48,32},{64,48},{80,64},{96,80},{112,96},{1... | collective-permute-start | bytes 1572872 | tf_op jit(solution)/shard_map/ppermute | solution.py:32
  65.7 23.0 %collective-permute-start.8 = (bf16[512,512]{1,0:T(8,128)(2,1)S(1)}, bf16[512,512]{1,0:T(8,128)(2,1)}, u32[]{:S(2)}, u32[]{:S(2)}) collective-permute-start(bf16[512,512]{1,0:T(8,128)(2,1)S(1)} %collective-permute-done.3.refs_2_), channel_id=1, source_target_pairs={{0,112},{16,0},{32,16},{48,32},{64,48},{80,64},{96,80},{112,96},{1... | collective-permute-start | bytes 1572872 | tf_op jit(solution)/shard_map/ppermute | solution.py:32
  67.2 25.0 %collective-permute-start.7 = (bf16[512,512]{1,0:T(8,128)(2,1)}, bf16[512,512]{1,0:T(8,128)(2,1)S(1)}, u32[]{:S(2)}, u32[]{:S(2)}) collective-permute-start(bf16[512,512]{1,0:T(8,128)(2,1)} %collective-permute-done.6.refs_3_), channel_id=1, source_target_pairs={{0,16},{16,32},{32,48},{48,64},{64,80},{80,96},{96,112},{112,0},{1... | collective-permute-start | bytes 1572872 | tf_op jit(solution)/shard_map/ppermute | solution.py:32
  78.3 23.2 %collective-permute-start.14 = (bf16[512,512]{1,0:T(8,128)(2,1)}, bf16[512,512]{1,0:T(8,128)(2,1)S(1)}, u32[]{:S(2)}, u32[]{:S(2)}) collective-permute-start(bf16[512,512]{1,0:T(8,128)(2,1)} %collective-permute-done.11.refs_8_), channel_id=1, source_target_pairs={{0,16},{16,32},{32,48},{48,64},{64,80},{80,96},{96,112},{112,0},{1... | collective-permute-start | bytes 1572872 | tf_op jit(solution)/shard_map/ppermute | solution.py:32
  78.3 23.1 %collective-permute-start.16 = (bf16[512,512]{1,0:T(8,128)(2,1)S(1)}, bf16[512,512]{1,0:T(8,128)(2,1)S(1)}, u32[]{:S(2)}, u32[]{:S(2)}) collective-permute-start(bf16[512,512]{1,0:T(8,128)(2,1)S(1)} %collective-permute-done.15.refs_1_), channel_id=1, source_target_pairs={{0,112},{16,0},{32,16},{48,32},{64,48},{80,64},{96,80},{112,96},{1... | collective-permute-start | bytes 1572872 | tf_op jit(solution)/shard_map/ppermute | solution.py:32
  88.6 22.6 %collective-permute-start.9 = (bf16[512,512]{1,0:T(8,128)(2,1)}, bf16[512,512]{1,0:T(8,128)(2,1)S(1)}, u32[]{:S(2)}, u32[]{:S(2)}) collective-permute-start(bf16[512,512]{1,0:T(8,128)(2,1)} %collective-permute-done.8.refs_4_), channel_id=1, source_target_pairs={{0,112},{16,0},{32,16},{48,32},{64,48},{80,64},{96,80},{112,96},{1... | collective-permute-start | bytes 1572872 | tf_op jit(solution)/shard_map/ppermute | solution.py:32
  92.2 19.1 %collective-permute-start.10 = (bf16[512,512]{1,0:T(8,128)(2,1)S(1)}, bf16[512,512]{1,0:T(8,128)(2,1)}, u32[]{:S(2)}, u32[]{:S(2)}) collective-permute-start(bf16[512,512]{1,0:T(8,128)(2,1)S(1)} %collective-permute-done.7.refs_0_), channel_id=1, source_target_pairs={{0,16},{16,32},{32,48},{48,64},{64,80},{80,96},{96,112},{112,0},{1... | collective-permute-start | bytes 1572872 | tf_op jit(solution)/shard_map/ppermute | solution.py:32
  101.5 9.8 %copy-start.3 = (f32[256,512]{1,0:T(8,128)S(1)}, f32[256,512]{1,0:T(8,128)}, u32[]{:S(2)}) copy-start(f32[256,512]{1,0:T(8,128)} %copy-done.2) | copy-start | bytes 1572868
  105.8 5.6 %copy-start.5 = (f32[256,512]{1,0:T(8,128)S(1)}, f32[256,512]{1,0:T(8,128)}, u32[]{:S(2)}) copy-start(f32[256,512]{1,0:T(8,128)} %copy-done.4) | copy-start | bytes 1572868
  105.8 15.1 %collective-permute-start.17 = (f32[256,512]{1,0:T(8,128)}, f32[256,512]{1,0:T(8,128)}, u32[]{:S(2)}, u32[]{:S(2)}) collective-permute-start(f32[256,512]{1,0:T(8,128)} %get-tuple-element.36), channel_id=1, source_target_pairs={{0,128},{128,0},{1,129},{129,1},{2,130},{130,2},{3,131},{131,3},{4... | collective-permute-start | bytes 1572872 | tf_op jit(solution)/shard_map/ppermute | solution.py:185
  110.9 6.1 %copy-start = (bf16[2048,1024]{1,0:T(8,128)(2,1)S(1)}, bf16[2048,1024]{1,0:T(8,128)(2,1)}, u32[]{:S(2)}) copy-start(bf16[2048,1024]{1,0:T(8,128)(2,1)} %head.1) | copy-start | bytes 12582916
  110.9 6.1 %copy-start.13 = (bf16[256,16,128]{0,2,1:T(8,128)(2,1)S(1)}, bf16[256,16,128]{0,2,1:T(8,128)(2,1)}, u32[]{:S(2)}) copy-start(bf16[256,16,128]{0,2,1:T(8,128)(2,1)} %copy.44) | copy-start | bytes 3145732
  114.5 6.3 %copy-start.7 = (f32[256,512]{1,0:T(8,128)S(1)}, f32[256,512]{1,0:T(8,128)}, u32[]{:S(2)}) copy-start(f32[256,512]{1,0:T(8,128)} %copy-done.6) | copy-start | bytes 1572868
  114.5 17.4 %collective-permute-start.13 = (f32[256,512]{1,0:T(8,128)S(1)}, f32[256,512]{1,0:T(8,128)S(1)}, u32[]{:S(2)}, u32[]{:S(2)}) collective-permute-start(f32[256,512]{1,0:T(8,128)S(1)} %get-tuple-element.30), channel_id=1, source_target_pairs={{0,128},{128,0},{1,129},{129,1},{2,130},{130,2},{3,131},{131,3},{4... | collective-permute-start | bytes 1572872 | tf_op jit(solution)/shard_map/ppermute | solution.py:185
  117.0 15.1 %copy-start.17 = (s32[256]{0:T(256)S(1)}, s32[256]{0:T(256)}, u32[]{:S(2)}) copy-start(s32[256]{0:T(256)} %param.12) | copy-start | bytes 3076
  118.4 27.2 %copy-start.18 = (s32[256]{0:T(256)S(1)}, s32[256]{0:T(256)}, u32[]{:S(2)}) copy-start(s32[256]{0:T(256)} %param.13) | copy-start | bytes 3076
  133.6 11.9 %all-to-all-start = ((f32[16,8,256]{2,1,0:T(8,128)}), f32[16,8,256]{2,1,0:T(8,128)S(1)}, u32[]{:S(2)}, u32[]{:S(2)}) async-start(f32[16,8,256]{2,1,0:T(8,128)} %broadcast_in_dim.12), calls=%async_computation | async-start | bytes 262144 | tf_op jit(solution)/shard_map/all_to_all | solution.py:246
  (7 other events, 10.2 us)
Sparse Core Ops, SparseCore 0:
  48.4 44.7 all-gather.2

commit v4 on v3

--- a/solution.py
+++ b/solution.py
@@ -16,7 +16,6 @@
 OFFSETS = (0, 4, 1, -3, -1, 3, 2, -2)
 WIDTHS = (512, 512)
 LAST = (+1, -1)
-FIRST = ((0, 1, +1), (0, 1, -1), (1, 1, +1), (1, 1, -1))
 
 
 def dequantize(codes, scales):
@@ -112,8 +111,13 @@
 
 
 class Ring:
-    def __init__(self, own):
-        self.block = {(k, 0, way): x for k, x in enumerate(own) for way in (+1, -1)}
+    def __init__(self, own, first):
+        self.block = {}
+        for k, width in enumerate(WIDTHS):
+            columns = slice(sum(WIDTHS[:k]), sum(WIDTHS[:k]) + width)
+            for way, arrived in zip((+1, -1), first):
+                self.block[k, 0, way] = own[:, columns]
+                self.block[k, 1, way] = arrived[:, columns]
 
     def send(self, k, s):
         for way in (+1, -1):
@@ -189,16 +193,12 @@
     teacher_codes, block_scales, teacher_head, student_hidden, student_head, token_ids, loss_mask
 ):
     yh = lax.axis_index("yh")
-    starts = [sum(WIDTHS[:k]) for k in range(len(WIDTHS))]
     local_rows = dequantize(teacher_codes, block_scales)
-    head, local_rows = order(teacher_head, local_rows)
-    own = [head[:, a : a + w] for a, w in zip(starts, WIDTHS)]
     own_rows, features = student_hidden.shape
-    ring = Ring(own)
+    first = [shift(teacher_head, way) for way in (+1, -1)]
     moved = swap_rows_features(local_rows)
-    for k in (0, 1):
-        ring.send(k, 1)
-    moved = ring.hold(moved, FIRST)
+    moved, first = order(moved, first)
+    ring = Ring(teacher_head, first)
     moved = jnp.concatenate([moved, student_hidden], axis=1)
     rows = lax.all_gather(moved, VOCAB, axis=0, tiled=False)
     for s in (2, 3):

time: 178 us -> 176 us (0.989)
  starting transfers between devices: 43.6 us -> 41.1 us
    ppermute x1, waiting for transfers between devices: 4.07 us -> 13.6 us  [swap_rows_features(): return lax.ppermute(rows, ('z', 'x', 'c'), along)]
    ppermute x14 -> x12, waiting for transfers between devices: 38.4 us -> 29.3 us  [shift(): return lax.ppermute(x, 'z', [(i, (i + s) % NZ) for i in range(NZ)])]
    ppermute x14 -> x12, starting transfers between devices: 23.1 us -> 19.7 us  [shift(): return lax.ppermute(x, 'z', [(i, (i + s) % NZ) for i in range(NZ)])]
    unnamed x38 -> x26, local copies, waits for them, and re-layouts: 6.78 us -> 3.83 us
    slice x1 -> x3, local copies, waits for them, and re-layouts: 1.27 us -> 3.44 us  [the longest x1 2.09 us: __init__(): self.block[k, 0, way] = own[:, columns]]
    transpose x2, local copies, waits for them, and re-layouts: 2.6 us -> 4.57 us  [body(): hidden = jnp.transpose(hidden[:, :, teacher_codes.shape[1]:], (1, 0, 2))]
  transfers between devices with their start and end apart: 20 -> 18, of which waited for: 14 -> 11; matrix products, arithmetic and copies ran while one was open for 3% -> 7% of each run, Pallas kernels for 7% -> 7%
where the time goes in v4:
time: 176 us; the launch traced here: 175 us
  waiting for transfers between devices  64.9 us (37%)
  starting transfers between devices  41.1 us (23%)
  blocking collectives  18.5 us (11%)
  Pallas kernels  14.5 us (8%)
  between operations  14.3 us (8%)
  local copies, waits for them, and re-layouts  14 us (8%)
  other arithmetic  6.33 us (4%)
    ppermute x12, waiting for transfers between devices, shift(): return lax.ppermute(x, 'z', [(i, (i + s) % NZ) for i in range(NZ)])  29.3 us
    ppermute x12, starting transfers between devices, shift(): return lax.ppermute(x, 'z', [(i, (i + s) % NZ) for i in range(NZ)])  19.7 us
    all_to_all x1, blocking collectives, body(): lax.all_to_all(hidden_terms, VOCAB, split_axis=0, concat_axis=0, tiled=True)  18.5 us
    ppermute x1, waiting for transfers between devices, swap_rows_features(): return lax.ppermute(rows, ('z', 'x', 'c'), along)  13.6 us
    pallas_call x3, Pallas kernels, chunk_logits(): pl.pallas_call(functools.partial(chunk_kernel, places, len(chunks)), out_...  12 us
    ppermute x2, waiting for transfers between devices, swap_halves(): return lax.ppermute(x, 'yh', [(0, 1), (1, 0)])  10.8 us
    all_to_all x1, starting transfers between devices, body(): lax.all_to_all(jnp.broadcast_to(stats[None], (16,) + stats.shape), VOCAB,...  7.17 us
    all_to_all x1, waiting for transfers between devices, body(): lax.all_to_all(jnp.broadcast_to(stats[None], (16,) + stats.shape), VOCAB,...  5.95 us
  transfers between devices with their start and end apart: 18, of which 11 were waited for; matrix products, arithmetic and copies ran while one was open for 7% of the time, Pallas kernels for 7%

profile of v4, /device:TPU:1, one launch (start us, length us, event | category | flops | bytes accessed | tf_op | source)
XLA Modules:
  0.0 174.9 jit_solution(5865525306928040696)
XLA Ops:
  7.2 2.5 %collective-permute-start.2 = (bf16[512,1024]{1,0:T(8,128)(2,1)}, bf16[512,1024]{1,0:T(8,128)(2,1)S(1)}, u32[]{:S(2)}, u32[]{:S(2)}) collective-permute-start(bf16[512,1024]{1,0:T(8,128)(2,1)} %param.9), channel_id=1, source_target_pairs={{0,16},{16,32},{32,48},{48,64},{64,80},{80,96},{96,112},{112,0},{1... | collective-permute-start | bytes 3145736 | tf_op jit(solution)/shard_map/ppermute | solution.py:31
  9.8 4.0 %collective-permute-start.3 = (bf16[512,1024]{1,0:T(8,128)(2,1)}, bf16[512,1024]{1,0:T(8,128)(2,1)S(1)}, u32[]{:S(2)}, u32[]{:S(2)}) collective-permute-start(bf16[512,1024]{1,0:T(8,128)(2,1)} %param.9), channel_id=1, source_target_pairs={{0,112},{16,0},{32,16},{48,32},{64,48},{80,64},{96,80},{112,96},{1... | collective-permute-start | bytes 3145736 | tf_op jit(solution)/shard_map/ppermute | solution.py:31
  16.0 5.5 %collective-permute-start = (bf16[256,512]{1,0:T(8,128)(2,1)S(1)}, bf16[256,512]{1,0:T(8,128)(2,1)S(1)}, u32[]{:S(2)}, u32[]{:S(2)}) collective-permute-start(bf16[256,512]{1,0:T(8,128)(2,1)S(1)} %fusion.1), channel_id=1, source_target_pairs={{0,0},{1,4},{2,7},{3,3},{4,1},{5,5},{6,6},{7,2},{16,18},{17,16},{1... | collective-permute-start | bytes 786440 | tf_op jit(solution)/shard_map/ppermute | solution.py:45
  21.5 4.0 %collective-permute-done = bf16[256,512]{1,0:T(8,128)(2,1)S(1)} collective-permute-done((bf16[256,512]{1,0:T(8,128)(2,1)S(1)}, bf16[256,512]{1,0:T(8,128)(2,1)S(1)}, u32[]{:S(2)}, u32[]{:S(2)}) %collective-permute-start) | collective-permute-done | bytes 262176 | tf_op jit(solution)/shard_map/ppermute | solution.py:45
  25.5 4.2 %collective-permute-start.1 = (bf16[256,512]{1,0:T(8,128)(2,1)S(1)}, bf16[256,512]{1,0:T(8,128)(2,1)S(1)}, u32[]{:S(2)}, u32[]{:S(2)}) collective-permute-start(bf16[256,512]{1,0:T(8,128)(2,1)S(1)} %collective-permute-done), channel_id=1, source_target_pairs={{0,0},{4,20},{7,39},{3,51},{1,65},{5,85},{6,102},{2,114},{18,2},{1... | collective-permute-start | bytes 786440 | tf_op jit(solution)/shard_map/ppermute | solution.py:46
  29.8 13.6 %collective-permute-done.1 = bf16[256,512]{1,0:T(8,128)(2,1)S(1)} collective-permute-done((bf16[256,512]{1,0:T(8,128)(2,1)S(1)}, bf16[256,512]{1,0:T(8,128)(2,1)S(1)}, u32[]{:S(2)}, u32[]{:S(2)}) %collective-permute-start.1) | collective-permute-done | bytes 262176 | tf_op jit(solution)/shard_map/ppermute | solution.py:46
  43.4 1.7 pad_maximum_fusion.1
  45.2 3.7 %collective-permute-start.10 = (bf16[512,512]{1,0:T(8,128)(2,1)S(1)}, bf16[512,512]{1,0:T(8,128)(2,1)S(1)}, u32[]{:S(2)}, u32[]{:S(2)}) collective-permute-start(bf16[512,512]{1,0:T(8,128)(2,1)S(1)} %get-tuple-element.46.refs_7_), channel_id=1, source_target_pairs={{0,112},{16,0},{32,16},{48,32},{64,48},{80,64},{96,80},{112,96},{1... | collective-permute-start | bytes 1572872 | tf_op jit(solution)/shard_map/ppermute | solution.py:31
  50.3 9.0 %collective-permute-done.10.refs_9_ = bf16[512,512]{1,0:T(8,128)(2,1)S(1)} collective-permute-done((bf16[512,512]{1,0:T(8,128)(2,1)S(1)}, bf16[512,512]{1,0:T(8,128)(2,1)S(1)}, u32[]{:S(2)}, u32[]{:S(2)}) %collective-permute-start.10) | collective-permute-done | bytes 524320 | tf_op jit(solution)/shard_map/ppermute | solution.py:31
  59.3 3.1 %collective-permute-start.13 = (bf16[512,512]{1,0:T(8,128)(2,1)S(1)}, bf16[512,512]{1,0:T(8,128)(2,1)S(1)}, u32[]{:S(2)}, u32[]{:S(2)}) collective-permute-start(bf16[512,512]{1,0:T(8,128)(2,1)S(1)} %collective-permute-done.10.refs_9_), channel_id=1, source_target_pairs={{0,112},{16,0},{32,16},{48,32},{64,48},{80,64},{96,80},{112,96},{1... | collective-permute-start | bytes 1572872 | tf_op jit(solution)/shard_map/ppermute | solution.py:31
  62.4 3.0 %collective-permute-done.4.refs_3_ = bf16[512,512]{1,0:T(8,128)(2,1)} collective-permute-done((bf16[512,512]{1,0:T(8,128)(2,1)S(1)}, bf16[512,512]{1,0:T(8,128)(2,1)}, u32[]{:S(2)}, u32[]{:S(2)}) %collective-permute-start.4) | collective-permute-done | bytes 524320 | tf_op jit(solution)/shard_map/ppermute | solution.py:31
  65.5 11.1 %collective-permute-done.9.refs_8_ = bf16[512,512]{1,0:T(8,128)(2,1)} collective-permute-done((bf16[512,512]{1,0:T(8,128)(2,1)S(1)}, bf16[512,512]{1,0:T(8,128)(2,1)}, u32[]{:S(2)}, u32[]{:S(2)}) %collective-permute-start.9) | collective-permute-done | bytes 524320 | tf_op jit(solution)/shard_map/ppermute | solution.py:31
  76.6 2.7 %collective-permute-start.14 = (bf16[512,512]{1,0:T(8,128)(2,1)S(1)}, bf16[512,512]{1,0:T(8,128)(2,1)}, u32[]{:S(2)}, u32[]{:S(2)}) collective-permute-start(bf16[512,512]{1,0:T(8,128)(2,1)S(1)} %collective-permute-done.13.refs_1_), channel_id=1, source_target_pairs={{0,112},{16,0},{32,16},{48,32},{64,48},{80,64},{96,80},{112,96},{1... | collective-permute-start | bytes 1572872 | tf_op jit(solution)/shard_map/ppermute | solution.py:31
  79.4 2.1 %fusion.15 = (bf16[512,512]{1,0:T(8,128)(2,1)}, bf16[512,512]{1,0:T(8,128)(2,1)S(1)}) fusion(bf16[512,1024]{1,0:T(8,128)(2,1)} %param.9), kind=kLoop, calls=%fused_computation.36 | loop fusion | bytes 2097152 | tf_op jit(solution)/shard_map/slice | solution.py:119
  81.5 3.9 %collective-permute-done.6.refs_4_ = bf16[512,512]{1,0:T(8,128)(2,1)} collective-permute-done((bf16[512,512]{1,0:T(8,128)(2,1)S(1)}, bf16[512,512]{1,0:T(8,128)(2,1)}, u32[]{:S(2)}, u32[]{:S(2)}) %collective-permute-start.6) | collective-permute-done | bytes 524320 | tf_op jit(solution)/shard_map/ppermute | solution.py:31
  85.4 3.5 %collective-permute-start.7 = (bf16[512,512]{1,0:T(8,128)(2,1)}, bf16[512,512]{1,0:T(8,128)(2,1)S(1)}, u32[]{:S(2)}, u32[]{:S(2)}) collective-permute-start(bf16[512,512]{1,0:T(8,128)(2,1)} %collective-permute-done.6.refs_4_), channel_id=1, source_target_pairs={{0,112},{16,0},{32,16},{48,32},{64,48},{80,64},{96,80},{112,96},{1... | collective-permute-start | bytes 1572872 | tf_op jit(solution)/shard_map/ppermute | solution.py:31
  90.0 5.3 %shard_map.86 = (f32[256,512]{1,0:T(8,128)S(1)}, f32[256,512]{1,0:T(8,128)S(1)}, f32[256,512]{1,0:T(8,128)S(1)}, f32[256,512]{1,0:T(8,128)S(1)}) custom-call(s32[2]{0:T(128)S(1)} %pad_add_fusion.where, bf16[16,256,640]{2,1,0:T(8,128)(2,1)} %bitcast.61, bf16[512,512]{1,0:T(8,128)(2,1)S(1)} %get-tuple-element.51.refs_0_, ...), custom_call_target="tpu_custom_call" | custom-call | flops 2684354560 | bytes 11534336 | tf_op jit(solution)/shard_map/pallas_call | solution.py:91
  97.0 2.2 %collective-permute-done.12.refs_0_ = bf16[512,512]{1,0:T(8,128)(2,1)} collective-permute-done((bf16[512,512]{1,0:T(8,128)(2,1)}, bf16[512,512]{1,0:T(8,128)(2,1)}, u32[]{:S(2)}, u32[]{:S(2)}) %collective-permute-start.12) | collective-permute-done | bytes 524320 | tf_op jit(solution)/shard_map/ppermute | solution.py:31
  99.2 3.7 %shard_map.88 = (f32[256,512]{1,0:T(8,128)}, f32[256,512]{1,0:T(8,128)S(1)}) custom-call(s32[2]{0:T(128)S(1)} %pad_add_fusion.where, bf16[16,256,640]{2,1,0:T(8,128)(2,1)} %bitcast.62, bf16[512,512]{1,0:T(8,128)(2,1)} %collective-permute-done.12.refs_0_, bf16[512,512]{1,0:T(8,128)(2,1)S(1)} %collective-permute-done.13.refs_1_, ...), custom_call_target="tpu_custom_call" | custom-call | flops 805306368 | bytes 7864320 | tf_op jit(solution)/shard_map/pallas_call | solution.py:91
  102.9 3.0 %collective-permute-start.15 = (f32[256,512]{1,0:T(8,128)}, f32[256,512]{1,0:T(8,128)}, u32[]{:S(2)}, u32[]{:S(2)}) collective-permute-start(f32[256,512]{1,0:T(8,128)} %get-tuple-element.28), channel_id=1, source_target_pairs={{0,128},{128,0},{1,129},{129,1},{2,130},{130,2},{3,131},{131,3},{4... | collective-permute-start | bytes 1572872 | tf_op jit(solution)/shard_map/ppermute | solution.py:189
  105.9 2.3 %slice_bitcast_fusion = bf16[256,16,128]{2,0,1:T(8,128)(2,1)} fusion(bf16[16,256,640]{2,1,0:T(8,128)(2,1)} %bitcast.63), kind=kLoop, calls=%fused_computation.4 | loop fusion | bytes 2097152 | tf_op jit(solution)/shard_map/transpose | solution.py:216
  108.2 2.3 %copy.44 = bf16[256,16,128]{0,2,1:T(8,128)(2,1)} copy(bf16[256,16,128]{2,0,1:T(8,128)(2,1)} %slice_bitcast_fusion) | data formatting | bytes 2097152 | tf_op jit(solution)/shard_map/transpose | solution.py:216
  110.5 3.0 %shard_map.87 = (f32[256,512]{1,0:T(8,128)S(1)}, f32[256,512]{1,0:T(8,128)S(1)}) custom-call(s32[2]{0:T(128)S(1)} %pad_add_fusion.where, bf16[16,256,640]{2,1,0:T(8,128)(2,1)} %bitcast.64, bf16[512,512]{1,0:T(8,128)(2,1)S(1)} %collective-permute-done.5.refs_0_, bf16[512,512]{1,0:T(8,128)(2,1)S(1)} %collective-permute-done.7.refs_1_, ...), custom_call_target="tpu_custom_call" | custom-call | flops 805306368 | bytes 7864320 | tf_op jit(solution)/shard_map/pallas_call | solution.py:91
  113.5 1.4 collective-permute-start.11
  115.0 1.4 fusion.17
  116.4 1.5 collective-permute-done.15
  119.0 9.3 %collective-permute-done.11 = f32[256,512]{1,0:T(8,128)S(1)} collective-permute-done((f32[256,512]{1,0:T(8,128)S(1)}, f32[256,512]{1,0:T(8,128)S(1)}, u32[]{:S(2)}, u32[]{:S(2)}) %collective-permute-start.11) | collective-permute-done | bytes 524320 | tf_op jit(solution)/shard_map/ppermute | solution.py:189
  130.0 7.2 %all-to-all-start = ((f32[16,8,256]{2,1,0:T(8,128)}), f32[16,8,256]{2,1,0:T(8,128)S(1)}, u32[]{:S(2)}, u32[]{:S(2)}) async-start(f32[16,8,256]{2,1,0:T(8,128)} %broadcast_in_dim.12), calls=%async_computation | async-start | bytes 262144 | tf_op jit(solution)/shard_map/all_to_all | solution.py:246
  137.3 5.9 %all-to-all-done = f32[16,8,256]{2,1,0:T(8,128)S(1)} async-done(((f32[16,8,256]{2,1,0:T(8,128)}), f32[16,8,256]{2,1,0:T(8,128)S(1)}, u32[]{:S(2)}, u32[]{:S(2)}) %all-to-all-start) | async-done | bytes 131104 | tf_op jit(solution)/shard_map/all_to_all | solution.py:246
  144.1 2.2 %copy-done.1 = bf16[2048,1024]{1,0:T(8,128)(2,1)S(1)} copy-done((bf16[2048,1024]{1,0:T(8,128)(2,1)S(1)}, bf16[2048,1024]{1,0:T(8,128)(2,1)}, u32[]{:S(2)}) %copy-start.1) | copy-done | bytes 4194328
  146.3 2.5 %shard_map.89 = bf16[16,256,128]{2,1,0:T(8,128)(2,1)S(1)} custom-call(s32[1]{0:T(128)} %bitcast.first, f32[256,8]{1,0:T(8,128)S(1)} %bitcast.60, s32[256,1]{1,0:T(8,128)S(1)} %copy.49.ids, f32[256,1024]{1,0:T(8,128)S(1)} %get-tuple-element.45.teacher, f32[256,1024]{1,0:T(8,128)S(1)} %get-tuple-element.65.student, bf16[2048,1024]{1,0:T(8,128)(2,1)S(1)} %copy-done.1), custom_call_target="tpu_custom_call" | custom-call | flops 1073741824 | bytes 7340032 | tf_op jit(solution)/shard_map/pallas_call | solution.py:165
  148.8 18.5 %all_to_all.10 = bf16[16,256,128]{2,1,0:T(8,128)(2,1)S(1)} all-to-all(bf16[16,256,128]{2,1,0:T(8,128)(2,1)S(1)} %shard_map.89), channel_id=1, replica_groups=mesh['yh'=2,'z'=8,'yl'=2,'x'=4,'c'=2] {'yl','x','c'}, dimensions={0} | all-to-all | bytes 2097152 | tf_op jit(solution)/shard_map/all_to_all | solution.py:294
  (63 shorter events, 11.2 us)
Async XLA Ops:
  7.2 82.9 %all-gather.3.cloned.1.call-start = ((), (), s32[]{:S(2)}) async-start(), calls=%async_computation.2 | async-start | bytes 5570560 | tf_op jit(solution)/shard_map/all_gather | solution.py:203
  7.2 36.2 %collective-permute-start.2 = (bf16[512,1024]{1,0:T(8,128)(2,1)}, bf16[512,1024]{1,0:T(8,128)(2,1)S(1)}, u32[]{:S(2)}, u32[]{:S(2)}) collective-permute-start(bf16[512,1024]{1,0:T(8,128)(2,1)} %param.9), channel_id=1, source_target_pairs={{0,16},{16,32},{32,48},{48,64},{64,80},{80,96},{96,112},{112,0},{1... | collective-permute-start | bytes 3145736 | tf_op jit(solution)/shard_map/ppermute | solution.py:31
  9.8 33.7 %collective-permute-start.3 = (bf16[512,1024]{1,0:T(8,128)(2,1)}, bf16[512,1024]{1,0:T(8,128)(2,1)S(1)}, u32[]{:S(2)}, u32[]{:S(2)}) collective-permute-start(bf16[512,1024]{1,0:T(8,128)(2,1)} %param.9), channel_id=1, source_target_pairs={{0,112},{16,0},{32,16},{48,32},{64,48},{80,64},{96,80},{112,96},{1... | collective-permute-start | bytes 3145736 | tf_op jit(solution)/shard_map/ppermute | solution.py:31
  16.0 9.5 %collective-permute-start = (bf16[256,512]{1,0:T(8,128)(2,1)S(1)}, bf16[256,512]{1,0:T(8,128)(2,1)S(1)}, u32[]{:S(2)}, u32[]{:S(2)}) collective-permute-start(bf16[256,512]{1,0:T(8,128)(2,1)S(1)} %fusion.1), channel_id=1, source_target_pairs={{0,0},{1,4},{2,7},{3,3},{4,1},{5,5},{6,6},{7,2},{16,18},{17,16},{1... | collective-permute-start | bytes 786440 | tf_op jit(solution)/shard_map/ppermute | solution.py:45
  25.5 17.9 %collective-permute-start.1 = (bf16[256,512]{1,0:T(8,128)(2,1)S(1)}, bf16[256,512]{1,0:T(8,128)(2,1)S(1)}, u32[]{:S(2)}, u32[]{:S(2)}) collective-permute-start(bf16[256,512]{1,0:T(8,128)(2,1)S(1)} %collective-permute-done), channel_id=1, source_target_pairs={{0,0},{4,20},{7,39},{3,51},{1,65},{5,85},{6,102},{2,114},{18,2},{1... | collective-permute-start | bytes 786440 | tf_op jit(solution)/shard_map/ppermute | solution.py:46
  43.4 1.7 copy-start.8
  45.2 20.3 %copy-start.6 = (bf16[512,512]{1,0:T(8,128)(2,1)}, bf16[512,512]{1,0:T(8,128)(2,1)S(1)}, u32[]{:S(2)}) copy-start(bf16[512,512]{1,0:T(8,128)(2,1)S(1)} %get-tuple-element.46.refs_7_) | copy-start | bytes 1572868
  45.2 14.1 %collective-permute-start.10 = (bf16[512,512]{1,0:T(8,128)(2,1)S(1)}, bf16[512,512]{1,0:T(8,128)(2,1)S(1)}, u32[]{:S(2)}, u32[]{:S(2)}) collective-permute-start(bf16[512,512]{1,0:T(8,128)(2,1)S(1)} %get-tuple-element.46.refs_7_), channel_id=1, source_target_pairs={{0,112},{16,0},{32,16},{48,32},{64,48},{80,64},{96,80},{112,96},{1... | collective-permute-start | bytes 1572872 | tf_op jit(solution)/shard_map/ppermute | solution.py:31
  50.1 29.2 %copy-start.7 = (bf16[512,512]{1,0:T(8,128)(2,1)}, bf16[512,512]{1,0:T(8,128)(2,1)S(1)}, u32[]{:S(2)}) copy-start(bf16[512,512]{1,0:T(8,128)(2,1)S(1)} %get-tuple-element.48.refs_6_) | copy-start | bytes 1572868
  50.1 15.3 %collective-permute-start.4 = (bf16[512,512]{1,0:T(8,128)(2,1)S(1)}, bf16[512,512]{1,0:T(8,128)(2,1)}, u32[]{:S(2)}, u32[]{:S(2)}) collective-permute-start(bf16[512,512]{1,0:T(8,128)(2,1)S(1)} %get-tuple-element.49.refs_1_), channel_id=1, source_target_pairs={{0,16},{16,32},{32,48},{48,64},{64,80},{80,96},{96,112},{112,0},{1... | collective-permute-start | bytes 1572872 | tf_op jit(solution)/shard_map/ppermute | solution.py:31
  50.2 26.4 %collective-permute-start.9 = (bf16[512,512]{1,0:T(8,128)(2,1)S(1)}, bf16[512,512]{1,0:T(8,128)(2,1)}, u32[]{:S(2)}, u32[]{:S(2)}) collective-permute-start(bf16[512,512]{1,0:T(8,128)(2,1)S(1)} %get-tuple-element.48.refs_6_), channel_id=1, source_target_pairs={{0,16},{16,32},{32,48},{48,64},{64,80},{80,96},{96,112},{112,0},{1... | collective-permute-start | bytes 1572872 | tf_op jit(solution)/shard_map/ppermute | solution.py:31
  59.3 20.0 %copy-start.10 = (bf16[512,512]{1,0:T(8,128)(2,1)}, bf16[512,512]{1,0:T(8,128)(2,1)S(1)}, u32[]{:S(2)}) copy-start(bf16[512,512]{1,0:T(8,128)(2,1)S(1)} %collective-permute-done.10.refs_9_) | copy-start | bytes 1572868
  59.3 17.3 %collective-permute-start.13 = (bf16[512,512]{1,0:T(8,128)(2,1)S(1)}, bf16[512,512]{1,0:T(8,128)(2,1)S(1)}, u32[]{:S(2)}, u32[]{:S(2)}) collective-permute-start(bf16[512,512]{1,0:T(8,128)(2,1)S(1)} %collective-permute-done.10.refs_9_), channel_id=1, source_target_pairs={{0,112},{16,0},{32,16},{48,32},{64,48},{80,64},{96,80},{112,96},{1... | collective-permute-start | bytes 1572872 | tf_op jit(solution)/shard_map/ppermute | solution.py:31
  62.4 23.0 %collective-permute-start.6 = (bf16[512,512]{1,0:T(8,128)(2,1)S(1)}, bf16[512,512]{1,0:T(8,128)(2,1)}, u32[]{:S(2)}, u32[]{:S(2)}) collective-permute-start(bf16[512,512]{1,0:T(8,128)(2,1)S(1)} %get-tuple-element.47.refs_2_), channel_id=1, source_target_pairs={{0,112},{16,0},{32,16},{48,32},{64,48},{80,64},{96,80},{112,96},{1... | collective-permute-start | bytes 1572872 | tf_op jit(solution)/shard_map/ppermute | solution.py:31
  65.5 23.4 %collective-permute-start.5 = (bf16[512,512]{1,0:T(8,128)(2,1)}, bf16[512,512]{1,0:T(8,128)(2,1)S(1)}, u32[]{:S(2)}, u32[]{:S(2)}) collective-permute-start(bf16[512,512]{1,0:T(8,128)(2,1)} %collective-permute-done.4.refs_3_), channel_id=1, source_target_pairs={{0,16},{16,32},{32,48},{48,64},{64,80},{80,96},{96,112},{112,0},{1... | collective-permute-start | bytes 1572872 | tf_op jit(solution)/shard_map/ppermute | solution.py:31
  76.6 22.6 %collective-permute-start.12 = (bf16[512,512]{1,0:T(8,128)(2,1)}, bf16[512,512]{1,0:T(8,128)(2,1)}, u32[]{:S(2)}, u32[]{:S(2)}) collective-permute-start(bf16[512,512]{1,0:T(8,128)(2,1)} %collective-permute-done.9.refs_8_), channel_id=1, source_target_pairs={{0,16},{16,32},{32,48},{48,64},{64,80},{80,96},{96,112},{112,0},{1... | collective-permute-start | bytes 1572872 | tf_op jit(solution)/shard_map/ppermute | solution.py:31
  76.6 22.6 %collective-permute-start.14 = (bf16[512,512]{1,0:T(8,128)(2,1)S(1)}, bf16[512,512]{1,0:T(8,128)(2,1)}, u32[]{:S(2)}, u32[]{:S(2)}) collective-permute-start(bf16[512,512]{1,0:T(8,128)(2,1)S(1)} %collective-permute-done.13.refs_1_), channel_id=1, source_target_pairs={{0,112},{16,0},{32,16},{48,32},{64,48},{80,64},{96,80},{112,96},{1... | collective-permute-start | bytes 1572872 | tf_op jit(solution)/shard_map/ppermute | solution.py:31
  85.4 25.1 %collective-permute-start.7 = (bf16[512,512]{1,0:T(8,128)(2,1)}, bf16[512,512]{1,0:T(8,128)(2,1)S(1)}, u32[]{:S(2)}, u32[]{:S(2)}) collective-permute-start(bf16[512,512]{1,0:T(8,128)(2,1)} %collective-permute-done.6.refs_4_), channel_id=1, source_target_pairs={{0,112},{16,0},{32,16},{48,32},{64,48},{80,64},{96,80},{112,96},{1... | collective-permute-start | bytes 1572872 | tf_op jit(solution)/shard_map/ppermute | solution.py:31
  88.9 21.6 %collective-permute-start.8 = (bf16[512,512]{1,0:T(8,128)(2,1)S(1)}, bf16[512,512]{1,0:T(8,128)(2,1)}, u32[]{:S(2)}, u32[]{:S(2)}) collective-permute-start(bf16[512,512]{1,0:T(8,128)(2,1)S(1)} %collective-permute-done.5.refs_0_), channel_id=1, source_target_pairs={{0,16},{16,32},{32,48},{48,64},{64,80},{80,96},{96,112},{112,0},{1... | collective-permute-start | bytes 1572872 | tf_op jit(solution)/shard_map/ppermute | solution.py:31
  95.3 0.8 copy-start.2
  96.2 0.8 copy-start.4
  99.2 11.3 %copy-start.3 = (f32[256,512]{1,0:T(8,128)S(1)}, f32[256,512]{1,0:T(8,128)}, u32[]{:S(2)}) copy-start(f32[256,512]{1,0:T(8,128)} %copy-done.2) | copy-start | bytes 1572868
  99.2 11.3 %copy-start.5 = (f32[256,512]{1,0:T(8,128)S(1)}, f32[256,512]{1,0:T(8,128)}, u32[]{:S(2)}) copy-start(f32[256,512]{1,0:T(8,128)} %copy-done.4) | copy-start | bytes 1572868
  102.9 15.0 %collective-permute-start.15 = (f32[256,512]{1,0:T(8,128)}, f32[256,512]{1,0:T(8,128)}, u32[]{:S(2)}, u32[]{:S(2)}) collective-permute-start(f32[256,512]{1,0:T(8,128)} %get-tuple-element.28), channel_id=1, source_target_pairs={{0,128},{128,0},{1,129},{129,1},{2,130},{130,2},{3,131},{131,3},{4... | collective-permute-start | bytes 1572872 | tf_op jit(solution)/shard_map/ppermute | solution.py:189
  110.5 4.5 %copy-start = (bf16[2048,1024]{1,0:T(8,128)(2,1)S(1)}, bf16[2048,1024]{1,0:T(8,128)(2,1)}, u32[]{:S(2)}) copy-start(bf16[2048,1024]{1,0:T(8,128)(2,1)} %head.1) | copy-start | bytes 12582916
  110.5 4.5 %copy-start.9 = (bf16[256,16,128]{0,2,1:T(8,128)(2,1)S(1)}, bf16[256,16,128]{0,2,1:T(8,128)(2,1)}, u32[]{:S(2)}) copy-start(bf16[256,16,128]{0,2,1:T(8,128)(2,1)} %copy.44) | copy-start | bytes 3145732
  113.5 14.8 %collective-permute-start.11 = (f32[256,512]{1,0:T(8,128)S(1)}, f32[256,512]{1,0:T(8,128)S(1)}, u32[]{:S(2)}, u32[]{:S(2)}) collective-permute-start(f32[256,512]{1,0:T(8,128)S(1)} %get-tuple-element.22), channel_id=1, source_target_pairs={{0,128},{128,0},{1,129},{129,1},{2,130},{130,2},{3,131},{131,3},{4... | collective-permute-start | bytes 1572872 | tf_op jit(solution)/shard_map/ppermute | solution.py:189
  115.0 13.5 %copy-start.11 = (s32[256]{0:T(256)S(1)}, s32[256]{0:T(256)}, u32[]{:S(2)}) copy-start(s32[256]{0:T(256)} %param.12) | copy-start | bytes 3076
  116.4 27.0 %copy-start.12 = (s32[256]{0:T(256)S(1)}, s32[256]{0:T(256)}, u32[]{:S(2)}) copy-start(s32[256]{0:T(256)} %param.13) | copy-start | bytes 3076
  130.0 13.3 %all-to-all-start = ((f32[16,8,256]{2,1,0:T(8,128)}), f32[16,8,256]{2,1,0:T(8,128)S(1)}, u32[]{:S(2)}, u32[]{:S(2)}) async-start(f32[16,8,256]{2,1,0:T(8,128)} %broadcast_in_dim.12), calls=%async_computation | async-start | bytes 262144 | tf_op jit(solution)/shard_map/all_to_all | solution.py:246
  144.1 2.2 %copy-start.1 = (bf16[2048,1024]{1,0:T(8,128)(2,1)S(1)}, bf16[2048,1024]{1,0:T(8,128)(2,1)}, u32[]{:S(2)}) copy-start(bf16[2048,1024]{1,0:T(8,128)(2,1)} %head.1) | copy-start | bytes 12582916
Sparse Core Ops, SparseCore 0:
  45.2 44.7 all-gather.2

commit v5 on v4

--- a/solution.py
+++ b/solution.py
@@ -139,7 +139,7 @@
         return found
 
 
-def gradient_kernel(first, per_row, ids, teacher, student, head, out, grad):
+def gradient_kernel(first, per_row, ids, teacher, student, head, mine, other, grad):
     @pl.when(pl.program_id(0) == 0)
     def _():
         rows = per_row[...]
@@ -152,9 +152,12 @@
     terms = lax.dot_general(
         grad[...], head[...], (((1,), (1,)), ((), ())), preferred_element_type=jnp.float32
     )
-    width = out.shape[2]
-    for k in range(out.shape[0]):
-        out[k] = terms[:, k * width : (k + 1) * width].astype(out.dtype)
+    width = mine.shape[2]
+    for k in range(mine.shape[0]):
+        even = terms[:, 2 * k * width : (2 * k + 1) * width]
+        odd = terms[:, (2 * k + 1) * width : (2 * k + 2) * width]
+        mine[k] = jnp.where(first[1] == 0, even, odd)
+        other[k] = jnp.where(first[1] == 0, odd, even)
 
 
 def gradient_terms(first, per_row, ids, teacher, student, head, width):
@@ -165,7 +168,7 @@
     return pl.pallas_call(
         gradient_kernel,
         grid=(features // (step * width),),
-        out_shape=jax.ShapeDtypeStruct((features // width, tokens, width), jnp.bfloat16),
+        out_shape=(jax.ShapeDtypeStruct((features // width // 2, tokens, width), jnp.float32),) * 2,
         in_specs=[
             smem,
             pl.BlockSpec(per_row.shape, lambda i: (0, 0)),
@@ -174,7 +177,7 @@
             whole,
             pl.BlockSpec((step * width, shard), lambda i: (i, 0)),
         ],
-        out_specs=pl.BlockSpec((step, tokens, width), lambda i: (i, 0, 0)),
+        out_specs=(pl.BlockSpec((step // 2, tokens, width), lambda i: (i, 0, 0)),) * 2,
         scratch_shapes=[pltpu.VMEM((tokens, shard), jnp.bfloat16)],
         compiler_params=pltpu.CompilerParams(vmem_limit_bytes=24 * 2**20),
         cost_estimate=pl.CostEstimate(
@@ -282,8 +285,8 @@
             zero,
         ]
     )
-    hidden_terms = gradient_terms(
-        (lax.axis_index(VOCAB) * shard_width).astype(jnp.int32)[None],
+    mine, other = gradient_terms(
+        jnp.stack([lax.axis_index(VOCAB) * shard_width, lax.axis_index("c")]).astype(jnp.int32),
         jnp.transpose(per_row),
         token_ids[:, None],
         teacher_logits,
@@ -291,7 +294,10 @@
         student_head,
         features,
     )
-    hidden_terms = lax.all_to_all(hidden_terms, VOCAB, split_axis=0, concat_axis=0, tiled=True)
+    mine = mine + lax.ppermute(other, "c", [(0, 1), (1, 0)])
+    hidden_terms = lax.all_to_all(
+        mine.astype(jnp.bfloat16), ("yl", "x"), split_axis=0, concat_axis=0, tiled=True
+    )
     grad_hidden = jnp.sum(hidden_terms.astype(jnp.float32), axis=0).astype(jnp.bfloat16)
     return (grad_hidden, token_loss)
 

time: 176 us -> 173 us (0.983)
  blocking collectives: 18.5 us -> 12.6 us
  waiting for transfers between devices: 64.9 us -> 67.1 us
    all_to_all x1, blocking collectives: 18.5 us -> 12.6 us  [body(): lax.all_to_all(mine.astype(jnp.bfloat16), ('yl', 'x'), split_axis=0, conc...]
    ppermute x0 -> x1, waiting for transfers between devices: none -> 2.29 us  [body(): mine = mine + lax.ppermute(other, 'c', [(0, 1), (1, 0)])]
  transfers between devices with their start and end apart: 18 -> 19, of which waited for: 11 -> 12; matrix products, arithmetic and copies ran while one was open for 7% -> 8% of each run, Pallas kernels for 7% -> 7%
where the time goes in v5:
time: 173 us
  waiting for transfers between devices  67.1 us (39%)
  starting transfers between devices  41.7 us (24%)
  Pallas kernels  15.1 us (9%)
  between operations  14.3 us (8%)
  local copies, waits for them, and re-layouts  14 us (8%)
  blocking collectives  12.6 us (7%)
  other arithmetic  6.45 us (4%)
    ppermute x12, waiting for transfers between devices, shift(): return lax.ppermute(x, 'z', [(i, (i + s) % NZ) for i in range(NZ)])  29.3 us
    ppermute x12, starting transfers between devices, shift(): return lax.ppermute(x, 'z', [(i, (i + s) % NZ) for i in range(NZ)])  19.7 us
    ppermute x1, waiting for transfers between devices, swap_rows_features(): return lax.ppermute(rows, ('z', 'x', 'c'), along)  13.6 us
    all_to_all x1, blocking collectives, body(): lax.all_to_all(mine.astype(jnp.bfloat16), ('yl', 'x'), split_axis=0, conc...  12.6 us
    pallas_call x3, Pallas kernels, chunk_logits(): pl.pallas_call(functools.partial(chunk_kernel, places, len(chunks)), out_...  12 us
    ppermute x2, waiting for transfers between devices, swap_halves(): return lax.ppermute(x, 'yh', [(0, 1), (1, 0)])  10.8 us
    all_to_all x1, starting transfers between devices, body(): lax.all_to_all(jnp.broadcast_to(stats[None], (16,) + stats.shape), VOCAB,...  7.17 us
    all_to_all x1, waiting for transfers between devices, body(): lax.all_to_all(jnp.broadcast_to(stats[None], (16,) + stats.shape), VOCAB,...  5.87 us
  transfers between devices with their start and end apart: 19, of which 12 were waited for; matrix products, arithmetic and copies ran while one was open for 8% of the time, Pallas kernels for 7%

profile of v5, /device:TPU:1, one launch (start us, length us, event | category | flops | bytes accessed | tf_op | source)
XLA Modules:
  0.0 172.5 jit_solution(16695587903765008875)
XLA Ops:
  7.2 2.5 %collective-permute-start.2 = (bf16[512,1024]{1,0:T(8,128)(2,1)}, bf16[512,1024]{1,0:T(8,128)(2,1)S(1)}, u32[]{:S(2)}, u32[]{:S(2)}) collective-permute-start(bf16[512,1024]{1,0:T(8,128)(2,1)} %param.9), channel_id=1, source_target_pairs={{0,16},{16,32},{32,48},{48,64},{64,80},{80,96},{96,112},{112,0},{1... | collective-permute-start | bytes 3145736 | tf_op jit(solution)/shard_map/ppermute | solution.py:31
  9.8 4.0 %collective-permute-start.3 = (bf16[512,1024]{1,0:T(8,128)(2,1)}, bf16[512,1024]{1,0:T(8,128)(2,1)S(1)}, u32[]{:S(2)}, u32[]{:S(2)}) collective-permute-start(bf16[512,1024]{1,0:T(8,128)(2,1)} %param.9), channel_id=1, source_target_pairs={{0,112},{16,0},{32,16},{48,32},{64,48},{80,64},{96,80},{112,96},{1... | collective-permute-start | bytes 3145736 | tf_op jit(solution)/shard_map/ppermute | solution.py:31
  16.0 5.5 %collective-permute-start = (bf16[256,512]{1,0:T(8,128)(2,1)S(1)}, bf16[256,512]{1,0:T(8,128)(2,1)S(1)}, u32[]{:S(2)}, u32[]{:S(2)}) collective-permute-start(bf16[256,512]{1,0:T(8,128)(2,1)S(1)} %fusion.1), channel_id=1, source_target_pairs={{0,0},{1,4},{2,7},{3,3},{4,1},{5,5},{6,6},{7,2},{16,18},{17,16},{1... | collective-permute-start | bytes 786440 | tf_op jit(solution)/shard_map/ppermute | solution.py:45
  21.5 4.0 %collective-permute-done = bf16[256,512]{1,0:T(8,128)(2,1)S(1)} collective-permute-done((bf16[256,512]{1,0:T(8,128)(2,1)S(1)}, bf16[256,512]{1,0:T(8,128)(2,1)S(1)}, u32[]{:S(2)}, u32[]{:S(2)}) %collective-permute-start) | collective-permute-done | bytes 262176 | tf_op jit(solution)/shard_map/ppermute | solution.py:45
  25.5 4.2 %collective-permute-start.1 = (bf16[256,512]{1,0:T(8,128)(2,1)S(1)}, bf16[256,512]{1,0:T(8,128)(2,1)S(1)}, u32[]{:S(2)}, u32[]{:S(2)}) collective-permute-start(bf16[256,512]{1,0:T(8,128)(2,1)S(1)} %collective-permute-done), channel_id=1, source_target_pairs={{0,0},{4,20},{7,39},{3,51},{1,65},{5,85},{6,102},{2,114},{18,2},{1... | collective-permute-start | bytes 786440 | tf_op jit(solution)/shard_map/ppermute | solution.py:46
  29.8 13.6 %collective-permute-done.1 = bf16[256,512]{1,0:T(8,128)(2,1)S(1)} collective-permute-done((bf16[256,512]{1,0:T(8,128)(2,1)S(1)}, bf16[256,512]{1,0:T(8,128)(2,1)S(1)}, u32[]{:S(2)}, u32[]{:S(2)}) %collective-permute-start.1) | collective-permute-done | bytes 262176 | tf_op jit(solution)/shard_map/ppermute | solution.py:46
  43.4 1.7 pad_maximum_fusion.1
  45.2 3.7 %collective-permute-start.10 = (bf16[512,512]{1,0:T(8,128)(2,1)S(1)}, bf16[512,512]{1,0:T(8,128)(2,1)S(1)}, u32[]{:S(2)}, u32[]{:S(2)}) collective-permute-start(bf16[512,512]{1,0:T(8,128)(2,1)S(1)} %get-tuple-element.50.refs_7_), channel_id=1, source_target_pairs={{0,112},{16,0},{32,16},{48,32},{64,48},{80,64},{96,80},{112,96},{1... | collective-permute-start | bytes 1572872 | tf_op jit(solution)/shard_map/ppermute | solution.py:31
  50.3 9.0 %collective-permute-done.10.refs_9_ = bf16[512,512]{1,0:T(8,128)(2,1)S(1)} collective-permute-done((bf16[512,512]{1,0:T(8,128)(2,1)S(1)}, bf16[512,512]{1,0:T(8,128)(2,1)S(1)}, u32[]{:S(2)}, u32[]{:S(2)}) %collective-permute-start.10) | collective-permute-done | bytes 524320 | tf_op jit(solution)/shard_map/ppermute | solution.py:31
  59.3 3.1 %collective-permute-start.13 = (bf16[512,512]{1,0:T(8,128)(2,1)S(1)}, bf16[512,512]{1,0:T(8,128)(2,1)S(1)}, u32[]{:S(2)}, u32[]{:S(2)}) collective-permute-start(bf16[512,512]{1,0:T(8,128)(2,1)S(1)} %collective-permute-done.10.refs_9_), channel_id=1, source_target_pairs={{0,112},{16,0},{32,16},{48,32},{64,48},{80,64},{96,80},{112,96},{1... | collective-permute-start | bytes 1572872 | tf_op jit(solution)/shard_map/ppermute | solution.py:31
  62.4 3.0 %collective-permute-done.4.refs_3_ = bf16[512,512]{1,0:T(8,128)(2,1)} collective-permute-done((bf16[512,512]{1,0:T(8,128)(2,1)S(1)}, bf16[512,512]{1,0:T(8,128)(2,1)}, u32[]{:S(2)}, u32[]{:S(2)}) %collective-permute-start.4) | collective-permute-done | bytes 524320 | tf_op jit(solution)/shard_map/ppermute | solution.py:31
  65.5 11.1 %collective-permute-done.9.refs_8_ = bf16[512,512]{1,0:T(8,128)(2,1)} collective-permute-done((bf16[512,512]{1,0:T(8,128)(2,1)S(1)}, bf16[512,512]{1,0:T(8,128)(2,1)}, u32[]{:S(2)}, u32[]{:S(2)}) %collective-permute-start.9) | collective-permute-done | bytes 524320 | tf_op jit(solution)/shard_map/ppermute | solution.py:31
  76.6 2.7 %collective-permute-start.14 = (bf16[512,512]{1,0:T(8,128)(2,1)S(1)}, bf16[512,512]{1,0:T(8,128)(2,1)}, u32[]{:S(2)}, u32[]{:S(2)}) collective-permute-start(bf16[512,512]{1,0:T(8,128)(2,1)S(1)} %collective-permute-done.13.refs_1_), channel_id=1, source_target_pairs={{0,112},{16,0},{32,16},{48,32},{64,48},{80,64},{96,80},{112,96},{1... | collective-permute-start | bytes 1572872 | tf_op jit(solution)/shard_map/ppermute | solution.py:31
  79.4 2.1 %fusion.15 = (bf16[512,512]{1,0:T(8,128)(2,1)}, bf16[512,512]{1,0:T(8,128)(2,1)S(1)}) fusion(bf16[512,1024]{1,0:T(8,128)(2,1)} %param.9), kind=kLoop, calls=%fused_computation.38 | loop fusion | bytes 2097152 | tf_op jit(solution)/shard_map/slice | solution.py:119
  81.5 3.9 %collective-permute-done.6.refs_4_ = bf16[512,512]{1,0:T(8,128)(2,1)} collective-permute-done((bf16[512,512]{1,0:T(8,128)(2,1)S(1)}, bf16[512,512]{1,0:T(8,128)(2,1)}, u32[]{:S(2)}, u32[]{:S(2)}) %collective-permute-start.6) | collective-permute-done | bytes 524320 | tf_op jit(solution)/shard_map/ppermute | solution.py:31
  85.4 3.5 %collective-permute-start.7 = (bf16[512,512]{1,0:T(8,128)(2,1)}, bf16[512,512]{1,0:T(8,128)(2,1)S(1)}, u32[]{:S(2)}, u32[]{:S(2)}) collective-permute-start(bf16[512,512]{1,0:T(8,128)(2,1)} %collective-permute-done.6.refs_4_), channel_id=1, source_target_pairs={{0,112},{16,0},{32,16},{48,32},{64,48},{80,64},{96,80},{112,96},{1... | collective-permute-start | bytes 1572872 | tf_op jit(solution)/shard_map/ppermute | solution.py:31
  90.0 5.3 %shard_map.86 = (f32[256,512]{1,0:T(8,128)S(1)}, f32[256,512]{1,0:T(8,128)S(1)}, f32[256,512]{1,0:T(8,128)S(1)}, f32[256,512]{1,0:T(8,128)S(1)}) custom-call(s32[2]{0:T(128)S(1)} %pad_add_fusion.1.where, bf16[16,256,640]{2,1,0:T(8,128)(2,1)} %bitcast.62, bf16[512,512]{1,0:T(8,128)(2,1)S(1)} %get-tuple-element.55.refs_0_, ...), custom_call_target="tpu_custom_call" | custom-call | flops 2684354560 | bytes 11534336 | tf_op jit(solution)/shard_map/pallas_call | solution.py:91
  97.0 2.2 %collective-permute-done.12.refs_0_ = bf16[512,512]{1,0:T(8,128)(2,1)} collective-permute-done((bf16[512,512]{1,0:T(8,128)(2,1)}, bf16[512,512]{1,0:T(8,128)(2,1)}, u32[]{:S(2)}, u32[]{:S(2)}) %collective-permute-start.12) | collective-permute-done | bytes 524320 | tf_op jit(solution)/shard_map/ppermute | solution.py:31
  99.2 3.7 %shard_map.88 = (f32[256,512]{1,0:T(8,128)}, f32[256,512]{1,0:T(8,128)S(1)}) custom-call(s32[2]{0:T(128)S(1)} %pad_add_fusion.1.where, bf16[16,256,640]{2,1,0:T(8,128)(2,1)} %bitcast.63, bf16[512,512]{1,0:T(8,128)(2,1)} %collective-permute-done.12.refs_0_, bf16[512,512]{1,0:T(8,128)(2,1)S(1)} %collective-permute-done.13.refs_1_, ...), custom_call_target="tpu_custom_call" | custom-call | flops 805306368 | bytes 7864320 | tf_op jit(solution)/shard_map/pallas_call | solution.py:91
  102.9 3.0 %collective-permute-start.15 = (f32[256,512]{1,0:T(8,128)}, f32[256,512]{1,0:T(8,128)}, u32[]{:S(2)}, u32[]{:S(2)}) collective-permute-start(f32[256,512]{1,0:T(8,128)} %get-tuple-element.30), channel_id=1, source_target_pairs={{0,128},{128,0},{1,129},{129,1},{2,130},{130,2},{3,131},{131,3},{4... | collective-permute-start | bytes 1572872 | tf_op jit(solution)/shard_map/ppermute | solution.py:192
  105.9 2.3 %slice_bitcast_fusion = bf16[256,16,128]{2,0,1:T(8,128)(2,1)} fusion(bf16[16,256,640]{2,1,0:T(8,128)(2,1)} %bitcast.64), kind=kLoop, calls=%fused_computation.5 | loop fusion | bytes 2097152 | tf_op jit(solution)/shard_map/transpose | solution.py:219
  108.2 2.3 %copy.44 = bf16[256,16,128]{0,2,1:T(8,128)(2,1)} copy(bf16[256,16,128]{2,0,1:T(8,128)(2,1)} %slice_bitcast_fusion) | data formatting | bytes 2097152 | tf_op jit(solution)/shard_map/transpose | solution.py:219
  110.5 3.0 %shard_map.87 = (f32[256,512]{1,0:T(8,128)S(1)}, f32[256,512]{1,0:T(8,128)S(1)}) custom-call(s32[2]{0:T(128)S(1)} %pad_add_fusion.1.where, bf16[16,256,640]{2,1,0:T(8,128)(2,1)} %bitcast.65, bf16[512,512]{1,0:T(8,128)(2,1)S(1)} %collective-permute-done.5.refs_0_, bf16[512,512]{1,0:T(8,128)(2,1)S(1)} %collective-permute-done.7.refs_1_, ...), custom_call_target="tpu_custom_call" | custom-call | flops 805306368 | bytes 7864320 | tf_op jit(solution)/shard_map/pallas_call | solution.py:91
  113.6 1.4 collective-permute-start.11
  116.4 1.5 collective-permute-done.15
  119.0 9.3 %collective-permute-done.11 = f32[256,512]{1,0:T(8,128)S(1)} collective-permute-done((f32[256,512]{1,0:T(8,128)S(1)}, f32[256,512]{1,0:T(8,128)S(1)}, u32[]{:S(2)}, u32[]{:S(2)}) %collective-permute-start.11) | collective-permute-done | bytes 524320 | tf_op jit(solution)/shard_map/ppermute | solution.py:192
  130.0 7.2 %all-to-all-start = ((f32[16,8,256]{2,1,0:T(8,128)}), f32[16,8,256]{2,1,0:T(8,128)S(1)}, u32[]{:S(2)}, u32[]{:S(2)}) async-start(f32[16,8,256]{2,1,0:T(8,128)} %broadcast_in_dim.9), calls=%async_computation | async-start | bytes 262144 | tf_op jit(solution)/shard_map/all_to_all | solution.py:249
  137.4 5.9 %all-to-all-done = f32[16,8,256]{2,1,0:T(8,128)S(1)} async-done(((f32[16,8,256]{2,1,0:T(8,128)}), f32[16,8,256]{2,1,0:T(8,128)S(1)}, u32[]{:S(2)}, u32[]{:S(2)}) %all-to-all-start) | async-done | bytes 131104 | tf_op jit(solution)/shard_map/all_to_all | solution.py:249
  144.1 2.2 %copy-done.1 = bf16[2048,1024]{1,0:T(8,128)(2,1)S(1)} copy-done((bf16[2048,1024]{1,0:T(8,128)(2,1)S(1)}, bf16[2048,1024]{1,0:T(8,128)(2,1)}, u32[]{:S(2)}) %copy-start.1) | copy-done | bytes 4194328
  146.3 3.1 %shard_map.89 = (f32[8,256,128]{2,1,0:T(8,128)S(1)}, f32[8,256,128]{2,1,0:T(8,128)S(1)}) custom-call(s32[2]{0:T(128)S(1)} %pad_add_fusion.first, f32[256,8]{1,0:T(8,128)S(1)} %bitcast.61, s32[256,1]{1,0:T(8,128)S(1)} %copy.49.ids, f32[256,1024]{1,0:T(8,128)S(1)} %get-tuple-element.49.teacher, f32[256,1024]{1,0:T(8,128)S(1)} %get-tuple-element.69.student, ...), custom_call_target="tpu_custom_call" | custom-call | flops 1073741824 | bytes 7340032 | tf_op jit(solution)/shard_map/pallas_call | solution.py:168
  149.9 2.3 %collective-permute-done.16 = f32[8,256,128]{2,1,0:T(8,128)S(1)} collective-permute-done((f32[8,256,128]{2,1,0:T(8,128)S(1)}, f32[8,256,128]{2,1,0:T(8,128)S(1)}, u32[]{:S(2)}, u32[]{:S(2)}) %collective-permute-start.16) | collective-permute-done | bytes 1048608 | tf_op jit(solution)/shard_map/ppermute | solution.py:297
  152.3 12.6 %all_to_all.10 = bf16[8,256,128]{2,1,0:T(8,128)(2,1)S(1)} all-to-all(bf16[8,256,128]{2,1,0:T(8,128)(2,1)S(1)} %add_convert_fusion), channel_id=1, replica_groups=mesh['yh'=2,'z'=8,'yl'=2,'x'=4,'c'=2] {'yl','x'}, dimensions={0} | all-to-all | bytes 1048576 | tf_op jit(solution)/shard_map/all_to_all | solution.py:298
  (67 shorter events, 13.2 us)
Async XLA Ops:
  7.2 82.9 %all-gather.3.cloned.1.call-start = ((), (), s32[]{:S(2)}) async-start(), calls=%async_computation.2 | async-start | bytes 5570560 | tf_op jit(solution)/shard_map/all_gather | solution.py:206
  7.2 36.2 %collective-permute-start.2 = (bf16[512,1024]{1,0:T(8,128)(2,1)}, bf16[512,1024]{1,0:T(8,128)(2,1)S(1)}, u32[]{:S(2)}, u32[]{:S(2)}) collective-permute-start(bf16[512,1024]{1,0:T(8,128)(2,1)} %param.9), channel_id=1, source_target_pairs={{0,16},{16,32},{32,48},{48,64},{64,80},{80,96},{96,112},{112,0},{1... | collective-permute-start | bytes 3145736 | tf_op jit(solution)/shard_map/ppermute | solution.py:31
  9.8 33.7 %collective-permute-start.3 = (bf16[512,1024]{1,0:T(8,128)(2,1)}, bf16[512,1024]{1,0:T(8,128)(2,1)S(1)}, u32[]{:S(2)}, u32[]{:S(2)}) collective-permute-start(bf16[512,1024]{1,0:T(8,128)(2,1)} %param.9), channel_id=1, source_target_pairs={{0,112},{16,0},{32,16},{48,32},{64,48},{80,64},{96,80},{112,96},{1... | collective-permute-start | bytes 3145736 | tf_op jit(solution)/shard_map/ppermute | solution.py:31
  16.0 9.5 %collective-permute-start = (bf16[256,512]{1,0:T(8,128)(2,1)S(1)}, bf16[256,512]{1,0:T(8,128)(2,1)S(1)}, u32[]{:S(2)}, u32[]{:S(2)}) collective-permute-start(bf16[256,512]{1,0:T(8,128)(2,1)S(1)} %fusion.1), channel_id=1, source_target_pairs={{0,0},{1,4},{2,7},{3,3},{4,1},{5,5},{6,6},{7,2},{16,18},{17,16},{1... | collective-permute-start | bytes 786440 | tf_op jit(solution)/shard_map/ppermute | solution.py:45
  25.5 17.9 %collective-permute-start.1 = (bf16[256,512]{1,0:T(8,128)(2,1)S(1)}, bf16[256,512]{1,0:T(8,128)(2,1)S(1)}, u32[]{:S(2)}, u32[]{:S(2)}) collective-permute-start(bf16[256,512]{1,0:T(8,128)(2,1)S(1)} %collective-permute-done), channel_id=1, source_target_pairs={{0,0},{4,20},{7,39},{3,51},{1,65},{5,85},{6,102},{2,114},{18,2},{1... | collective-permute-start | bytes 786440 | tf_op jit(solution)/shard_map/ppermute | solution.py:46
  43.4 1.7 copy-start.8
  45.2 20.3 %copy-start.6 = (bf16[512,512]{1,0:T(8,128)(2,1)}, bf16[512,512]{1,0:T(8,128)(2,1)S(1)}, u32[]{:S(2)}) copy-start(bf16[512,512]{1,0:T(8,128)(2,1)S(1)} %get-tuple-element.50.refs_7_) | copy-start | bytes 1572868
  45.2 14.1 %collective-permute-start.10 = (bf16[512,512]{1,0:T(8,128)(2,1)S(1)}, bf16[512,512]{1,0:T(8,128)(2,1)S(1)}, u32[]{:S(2)}, u32[]{:S(2)}) collective-permute-start(bf16[512,512]{1,0:T(8,128)(2,1)S(1)} %get-tuple-element.50.refs_7_), channel_id=1, source_target_pairs={{0,112},{16,0},{32,16},{48,32},{64,48},{80,64},{96,80},{112,96},{1... | collective-permute-start | bytes 1572872 | tf_op jit(solution)/shard_map/ppermute | solution.py:31
  50.1 29.2 %copy-start.7 = (bf16[512,512]{1,0:T(8,128)(2,1)}, bf16[512,512]{1,0:T(8,128)(2,1)S(1)}, u32[]{:S(2)}) copy-start(bf16[512,512]{1,0:T(8,128)(2,1)S(1)} %get-tuple-element.52.refs_6_) | copy-start | bytes 1572868
  50.1 15.3 %collective-permute-start.4 = (bf16[512,512]{1,0:T(8,128)(2,1)S(1)}, bf16[512,512]{1,0:T(8,128)(2,1)}, u32[]{:S(2)}, u32[]{:S(2)}) collective-permute-start(bf16[512,512]{1,0:T(8,128)(2,1)S(1)} %get-tuple-element.53.refs_1_), channel_id=1, source_target_pairs={{0,16},{16,32},{32,48},{48,64},{64,80},{80,96},{96,112},{112,0},{1... | collective-permute-start | bytes 1572872 | tf_op jit(solution)/shard_map/ppermute | solution.py:31
  50.2 26.4 %collective-permute-start.9 = (bf16[512,512]{1,0:T(8,128)(2,1)S(1)}, bf16[512,512]{1,0:T(8,128)(2,1)}, u32[]{:S(2)}, u32[]{:S(2)}) collective-permute-start(bf16[512,512]{1,0:T(8,128)(2,1)S(1)} %get-tuple-element.52.refs_6_), channel_id=1, source_target_pairs={{0,16},{16,32},{32,48},{48,64},{64,80},{80,96},{96,112},{112,0},{1... | collective-permute-start | bytes 1572872 | tf_op jit(solution)/shard_map/ppermute | solution.py:31
  59.3 20.0 %copy-start.10 = (bf16[512,512]{1,0:T(8,128)(2,1)}, bf16[512,512]{1,0:T(8,128)(2,1)S(1)}, u32[]{:S(2)}) copy-start(bf16[512,512]{1,0:T(8,128)(2,1)S(1)} %collective-permute-done.10.refs_9_) | copy-start | bytes 1572868
  59.3 17.3 %collective-permute-start.13 = (bf16[512,512]{1,0:T(8,128)(2,1)S(1)}, bf16[512,512]{1,0:T(8,128)(2,1)S(1)}, u32[]{:S(2)}, u32[]{:S(2)}) collective-permute-start(bf16[512,512]{1,0:T(8,128)(2,1)S(1)} %collective-permute-done.10.refs_9_), channel_id=1, source_target_pairs={{0,112},{16,0},{32,16},{48,32},{64,48},{80,64},{96,80},{112,96},{1... | collective-permute-start | bytes 1572872 | tf_op jit(solution)/shard_map/ppermute | solution.py:31
  62.4 23.0 %collective-permute-start.6 = (bf16[512,512]{1,0:T(8,128)(2,1)S(1)}, bf16[512,512]{1,0:T(8,128)(2,1)}, u32[]{:S(2)}, u32[]{:S(2)}) collective-permute-start(bf16[512,512]{1,0:T(8,128)(2,1)S(1)} %get-tuple-element.51.refs_2_), channel_id=1, source_target_pairs={{0,112},{16,0},{32,16},{48,32},{64,48},{80,64},{96,80},{112,96},{1... | collective-permute-start | bytes 1572872 | tf_op jit(solution)/shard_map/ppermute | solution.py:31
  65.5 23.4 %collective-permute-start.5 = (bf16[512,512]{1,0:T(8,128)(2,1)}, bf16[512,512]{1,0:T(8,128)(2,1)S(1)}, u32[]{:S(2)}, u32[]{:S(2)}) collective-permute-start(bf16[512,512]{1,0:T(8,128)(2,1)} %collective-permute-done.4.refs_3_), channel_id=1, source_target_pairs={{0,16},{16,32},{32,48},{48,64},{64,80},{80,96},{96,112},{112,0},{1... | collective-permute-start | bytes 1572872 | tf_op jit(solution)/shard_map/ppermute | solution.py:31
  76.6 22.6 %collective-permute-start.12 = (bf16[512,512]{1,0:T(8,128)(2,1)}, bf16[512,512]{1,0:T(8,128)(2,1)}, u32[]{:S(2)}, u32[]{:S(2)}) collective-permute-start(bf16[512,512]{1,0:T(8,128)(2,1)} %collective-permute-done.9.refs_8_), channel_id=1, source_target_pairs={{0,16},{16,32},{32,48},{48,64},{64,80},{80,96},{96,112},{112,0},{1... | collective-permute-start | bytes 1572872 | tf_op jit(solution)/shard_map/ppermute | solution.py:31
  76.6 22.6 %collective-permute-start.14 = (bf16[512,512]{1,0:T(8,128)(2,1)S(1)}, bf16[512,512]{1,0:T(8,128)(2,1)}, u32[]{:S(2)}, u32[]{:S(2)}) collective-permute-start(bf16[512,512]{1,0:T(8,128)(2,1)S(1)} %collective-permute-done.13.refs_1_), channel_id=1, source_target_pairs={{0,112},{16,0},{32,16},{48,32},{64,48},{80,64},{96,80},{112,96},{1... | collective-permute-start | bytes 1572872 | tf_op jit(solution)/shard_map/ppermute | solution.py:31
  85.4 25.1 %collective-permute-start.7 = (bf16[512,512]{1,0:T(8,128)(2,1)}, bf16[512,512]{1,0:T(8,128)(2,1)S(1)}, u32[]{:S(2)}, u32[]{:S(2)}) collective-permute-start(bf16[512,512]{1,0:T(8,128)(2,1)} %collective-permute-done.6.refs_4_), channel_id=1, source_target_pairs={{0,112},{16,0},{32,16},{48,32},{64,48},{80,64},{96,80},{112,96},{1... | collective-permute-start | bytes 1572872 | tf_op jit(solution)/shard_map/ppermute | solution.py:31
  88.9 21.6 %collective-permute-start.8 = (bf16[512,512]{1,0:T(8,128)(2,1)S(1)}, bf16[512,512]{1,0:T(8,128)(2,1)}, u32[]{:S(2)}, u32[]{:S(2)}) collective-permute-start(bf16[512,512]{1,0:T(8,128)(2,1)S(1)} %collective-permute-done.5.refs_0_), channel_id=1, source_target_pairs={{0,16},{16,32},{32,48},{48,64},{64,80},{80,96},{96,112},{112,0},{1... | collective-permute-start | bytes 1572872 | tf_op jit(solution)/shard_map/ppermute | solution.py:31
  95.4 0.8 copy-start.2
  96.2 0.8 copy-start.4
  99.2 11.3 %copy-start.3 = (f32[256,512]{1,0:T(8,128)S(1)}, f32[256,512]{1,0:T(8,128)}, u32[]{:S(2)}) copy-start(f32[256,512]{1,0:T(8,128)} %copy-done.2) | copy-start | bytes 1572868
  99.2 11.3 %copy-start.5 = (f32[256,512]{1,0:T(8,128)S(1)}, f32[256,512]{1,0:T(8,128)}, u32[]{:S(2)}) copy-start(f32[256,512]{1,0:T(8,128)} %copy-done.4) | copy-start | bytes 1572868
  102.9 14.9 %collective-permute-start.15 = (f32[256,512]{1,0:T(8,128)}, f32[256,512]{1,0:T(8,128)}, u32[]{:S(2)}, u32[]{:S(2)}) collective-permute-start(f32[256,512]{1,0:T(8,128)} %get-tuple-element.30), channel_id=1, source_target_pairs={{0,128},{128,0},{1,129},{129,1},{2,130},{130,2},{3,131},{131,3},{4... | collective-permute-start | bytes 1572872 | tf_op jit(solution)/shard_map/ppermute | solution.py:192
  110.5 4.5 %copy-start = (bf16[2048,1024]{1,0:T(8,128)(2,1)S(1)}, bf16[2048,1024]{1,0:T(8,128)(2,1)}, u32[]{:S(2)}) copy-start(bf16[2048,1024]{1,0:T(8,128)(2,1)} %head.1) | copy-start | bytes 12582916
  110.5 4.5 %copy-start.9 = (bf16[256,16,128]{0,2,1:T(8,128)(2,1)S(1)}, bf16[256,16,128]{0,2,1:T(8,128)(2,1)}, u32[]{:S(2)}) copy-start(bf16[256,16,128]{0,2,1:T(8,128)(2,1)} %copy.44) | copy-start | bytes 3145732
  113.6 14.8 %collective-permute-start.11 = (f32[256,512]{1,0:T(8,128)S(1)}, f32[256,512]{1,0:T(8,128)S(1)}, u32[]{:S(2)}, u32[]{:S(2)}) collective-permute-start(f32[256,512]{1,0:T(8,128)S(1)} %get-tuple-element.24), channel_id=1, source_target_pairs={{0,128},{128,0},{1,129},{129,1},{2,130},{130,2},{3,131},{131,3},{4... | collective-permute-start | bytes 1572872 | tf_op jit(solution)/shard_map/ppermute | solution.py:192
  115.0 13.5 %copy-start.11 = (s32[256]{0:T(256)S(1)}, s32[256]{0:T(256)}, u32[]{:S(2)}) copy-start(s32[256]{0:T(256)} %param.12) | copy-start | bytes 3076
  116.4 27.0 %copy-start.12 = (s32[256]{0:T(256)S(1)}, s32[256]{0:T(256)}, u32[]{:S(2)}) copy-start(s32[256]{0:T(256)} %param.13) | copy-start | bytes 3076
  130.0 13.3 %all-to-all-start = ((f32[16,8,256]{2,1,0:T(8,128)}), f32[16,8,256]{2,1,0:T(8,128)S(1)}, u32[]{:S(2)}, u32[]{:S(2)}) async-start(f32[16,8,256]{2,1,0:T(8,128)} %broadcast_in_dim.9), calls=%async_computation | async-start | bytes 262144 | tf_op jit(solution)/shard_map/all_to_all | solution.py:249
  144.1 2.2 %copy-start.1 = (bf16[2048,1024]{1,0:T(8,128)(2,1)S(1)}, bf16[2048,1024]{1,0:T(8,128)(2,1)}, u32[]{:S(2)}) copy-start(bf16[2048,1024]{1,0:T(8,128)(2,1)} %head.1) | copy-start | bytes 12582916
  149.4 2.8 %collective-permute-start.16 = (f32[8,256,128]{2,1,0:T(8,128)S(1)}, f32[8,256,128]{2,1,0:T(8,128)S(1)}, u32[]{:S(2)}, u32[]{:S(2)}) collective-permute-start(f32[8,256,128]{2,1,0:T(8,128)S(1)} %get-tuple-element.33), channel_id=1, source_target_pairs={{0,1},{1,0},{2,3},{3,2},{4,5},{5,4},{6,7},{7,6},{8,9},{9,8},{10,11... | collective-permute-start | bytes 3145736 | tf_op jit(solution)/shard_map/ppermute | solution.py:297
Sparse Core Ops, SparseCore 0:
  45.2 44.7 all-gather.2
